TPU v7x, 32 devices: a whole 2x2x4 slice. The times are simulated.
32 devices in a mesh: row: 8 (over z, y), col: 4 (over x, core).
Axes of the slice: x: 2, y: 2, z: 4, core: 2. Of those that a mesh axis runs over, the one named last changes fastest.
Arguments:
- pairs: float32 [6400, 6400], P('row', 'col'), may hold values from -6 to 6
- one_body: float32 [80, 80], replicated, may hold values from -0.625 to 0.625
- aux: float32 [80, 80, 512], P('row', 'col'), may hold values from -1 to 1, as said below
- weights: float32 [512], replicated, may hold values from 0.3 to 3
Outputs:
- propagated: float32 [6400, 6400], P('row', 'col')
Inputs may be any that keep to these rules, and one draw needn't show every extreme that they name: aux[p, q, a] equals aux[q, p, a].
All inputs are finite; a program needn't handle non-finite values.
Results may differ from a plain program's by a relative error of at most 0.0001.
Values sent between devices are 32-bit elements; how exact they have to be, the bound alone decides.
No kernel may reach another device: no remote copies, remote signals or barrier semaphores. Data moves between devices by JAX's collectives and lax.ppermute only.
A program may use at most 192 MiB of HBM per device.

v0:
```python
import functools

import jax
import jax.numpy as jnp
from jax import lax
from jax.experimental import pallas as pl
from jax.experimental.pallas import tpu as pltpu
from jax.sharding import PartitionSpec as P

time_step = 0.15
vmem_limit = 60 * 1024 * 1024
f32, bf16 = jnp.float32, jnp.bfloat16


def halves(x):
    high = x.astype(bf16)
    return high, (x - high.astype(f32)).astype(bf16)


def dot(a, b):
    return lax.dot_general(a, b, (((1,), (0,)), ((), ())), preferred_element_type=f32)


def dot3(a, b):
    return dot(a[0], b[0]) + dot(a[0], b[1]) + dot(a[1], b[0])


def stacked(x):
    high, low = halves(x)
    return jnp.concatenate([high, high, low], axis=0)


def call(body, out_shape, operands, scratch=(), flops=0, moved=0):
    vmem, smem = pl.BlockSpec(memory_space=pltpu.VMEM), pl.BlockSpec(memory_space=pltpu.SMEM)
    return pl.pallas_call(
        body,
        in_specs=[smem if x.dtype == jnp.int32 else vmem for x in operands],
        out_specs=jax.tree.map(lambda _: vmem, out_shape),
        out_shape=out_shape,
        scratch_shapes=list(scratch),
        compiler_params=pltpu.CompilerParams(vmem_limit_bytes=vmem_limit),
        cost_estimate=pl.CostEstimate(flops=flops, bytes_accessed=moved, transcendentals=0),
    )(*operands)


def tiles(total, size=128):
    return [slice(start, min(start + size, total)) for start in range(0, total, size)]


def cross_body(n, x_ref, crossed_ref):
    rows = tiles(x_ref.shape[0], n)
    for k in tiles(x_ref.shape[1], n):
        crossed_ref[k, :] = jnp.concatenate([x_ref[i, k] for i in rows], axis=1)


def turn_body(me_ref, x_ref, *refs):
    *outs, stage = refs
    count, batch, _ = stage.shape
    for strip in tiles(x_ref.shape[0]):
        turned = x_ref[strip, :].T
        for b in range(count):
            stage[b, :, strip] = turned[b * batch : (b + 1) * batch]
    hand_out(me_ref, stage, outs)


def hand_out(me_ref, stage, outs):
    for s, out_ref in enumerate(outs):
        out_ref[...] = stage[lax.rem(me_ref[0] + s, len(outs))]


def take_in(me_ref, ins, stage):
    for s, in_ref in enumerate(ins):
        stage[lax.rem(me_ref[0] + len(ins) - s, len(ins))] = in_ref[...]


def finish_body(n, me_ref, x_ref, crossed_ref, *refs):
    *ins, out_ref, stage, total = refs
    take_in(me_ref, ins, stage)
    for strip in tiles(total.shape[0]):
        turned = jnp.concatenate([stage[b, :, strip] for b in range(len(ins))], axis=0)
        total[strip, :] = crossed_ref[strip, :] + turned.T
    cols = tiles(x_ref.shape[1], n)
    for i in tiles(x_ref.shape[0], n):
        out_ref[i, :] = x_ref[i, :] + jnp.concatenate([total[k, i] for k in cols], axis=1)


def split_body(n, x_ref, high_ref, low_ref):
    wide = x_ref.shape[1] * x_ref.shape[0] // n
    each = n // x_ref.shape[0]
    for p in range(wide):
        parts = [x_ref[c, p * each : (p + 1) * each, :] for c in range(x_ref.shape[0])]
        rows = slice(p * n, (p + 1) * n)
        high_ref[rows, :], low_ref[rows, :] = halves(jnp.concatenate(parts, axis=0))


def take(ref, rows, batch):
    parts = [ref[t, rows, : min(128, batch - 128 * t)] for t in range(ref.shape[0])]
    return jnp.concatenate(parts, axis=1) if len(parts) > 1 else parts[0]


def put(ref, rows, value):
    for t in range(ref.shape[0]):
        part = value[:, 128 * t : 128 * (t + 1)]
        ref[t, rows, : part.shape[1]] = part


def apply_operator(
    n, keep, scale, field, target, high_ref, low_ref, weights_ref, major_ref, minor_ref, xp, zp
):
    blocks, batch, width = field.shape

    def span(r):
        return pl.ds(pl.multiple_of(r * width, 16), width)

    def project(r, total):
        x = field[r]
        put(xp, span(r), x.T)
        return total + dot3(halves(x), (high_ref[span(r), :], low_ref[span(r), :]))

    total = jnp.zeros((batch, high_ref.shape[1]), f32)
    total = lax.fori_loop(0, blocks, project, total)
    proj = halves((total * weights_ref[...]).T)

    group = 8 if n % 8 == 0 else 1

    def major(step, carry):
        for g in range(group):
            at = (pl.ds(step * group + g, n, stride=n), slice(None))
            parts = [xp[(t, *at)] for t in range(xp.shape[0])]
            x = jnp.concatenate(parts, axis=1) if len(parts) > 1 else parts[0]
            term = dot(major_ref[...], stacked(x))
            for t in range(xp.shape[0]):
                zp[(t, *at)] = term[:, 128 * t : 128 * (t + 1)]
        return carry

    lax.fori_loop(0, n // group, major, 0)

    def result(r, carry):
        total = dot3((high_ref[span(r), :], low_ref[span(r), :]), proj)
        minor = []
        for p in range(width // n):
            at = pl.ds(pl.multiple_of(r * width + p * n, 16), n)
            minor.append(dot(minor_ref[...], stacked(take(xp, at, batch))))
        total = total + jnp.concatenate(minor, axis=0) + take(zp, span(r), batch)
        if keep:
            target[r] = scale * total.T + keep * field[r]
        else:
            target[r] = scale * total.T
        return carry

    lax.fori_loop(0, blocks, result, 0)


def direct_body(n, keep, scale, x_ref, *refs):
    *consts, out_ref, xp, zp = refs
    apply_operator(n, keep, scale, x_ref, out_ref, *consts, xp, zp)


def arriving_body(n, keep, scale, count, me_ref, *refs):
    ins, (*consts, out_ref, stage, xp, zp) = refs[:count], refs[count:]
    take_in(me_ref, ins, stage)
    apply_operator(n, keep, scale, stage, out_ref, *consts, xp, zp)


def added_body(n, count, me_ref, base_ref, *refs):
    ins, rest = refs[:count], refs[count:]
    consts, outs, (stage, xp, zp) = rest[:-3 - count], rest[-3 - count : -3], rest[-3:]
    for s in range(count):
        b = lax.rem(me_ref[0] + count - s, count)
        stage[b] = base_ref[b] + (time_step * time_step) * ins[s][...]
    apply_operator(n, 0.0, 1.0, stage, stage, *consts, xp, zp)
    hand_out(me_ref, stage, outs)


def tripled(matrix):
    high = lax.reduce_precision(matrix, 8, 7)
    low = matrix - high
    return jnp.concatenate([high, low, high], axis=1).astype(bf16)


def exchange(x, axis):
    return lax.all_to_all(x, axis, split_axis=0, concat_axis=0, tiled=True)


def shift(parts, axis):
    n = len(parts)
    return [parts[0]] + [
        lax.ppermute(parts[s], axis, [(d, (d + s) % n) for d in range(n)]) for s in range(1, n)
    ]


def shards(rows, cols, pairs, one_body, aux, weights):
    n = one_body.shape[0]
    naux = aux.shape[2]
    local_rows, local_cols = pairs.shape
    size = local_rows * local_cols
    me = lax.axis_index("col").astype(jnp.int32).reshape(1)

    crossed = call(
        functools.partial(cross_body, n),
        jax.ShapeDtypeStruct((local_cols, local_rows), f32), [pairs], moved=8 * size,
    )

    crossed, aux = lax.optimization_barrier((crossed, aux))
    whole = lax.all_gather(aux.reshape(-1, naux), "row", axis=0, tiled=True)
    whole = lax.all_gather(whole, "col", axis=0, tiled=False)
    group = 8 if n % 8 == 0 else n
    shape = jax.ShapeDtypeStruct((n * n, naux), bf16)
    high, low = pl.pallas_call(
        functools.partial(split_body, n),
        grid=(n // group,),
        in_specs=[pl.BlockSpec((cols, group * n // cols, naux), lambda s: (0, s, 0))],
        out_specs=[pl.BlockSpec((group * n, naux), lambda s: (s, 0))] * 2,
        out_shape=[shape, shape],
        compiler_params=pltpu.CompilerParams(vmem_limit_bytes=vmem_limit),
        cost_estimate=pl.CostEstimate(
            flops=2 * n * n * naux, bytes_accessed=8 * n * n * naux, transcendentals=0
        ),
    )(whole)

    left = tripled(one_body)
    right = tripled(-one_body.T)
    gain = weights.reshape(1, naux)
    half_square = time_step * time_step / 2.0

    def operator(body, arrays, consts, outs, block, staged):
        blocks, batch, width = block
        work = pltpu.VMEM((-(-batch // 128), n * n, 128), f32)
        return call(
            functools.partial(body, n),
            outs,
            [*arrays, high, low, *consts],
            [pltpu.VMEM(block, f32)] * staged + [work, work],
            flops=12 * n * n * (naux + n) * batch,
            moved=4 * n * n * naux + 12 * size,
        )

    row_block = (rows, local_cols // rows, local_rows)
    col_block = (cols, local_rows // cols, local_cols)
    row_shape = jax.ShapeDtypeStruct(row_block, f32)
    col_shape = jax.ShapeDtypeStruct(col_block, f32)
    parts = [jax.ShapeDtypeStruct(col_block[1:], f32)] * cols
    row_consts = [gain, left, right]
    col_consts = [-gain, right, left]
    stage = pltpu.VMEM(col_block, f32)

    def turn(x):
        return call(turn_body, parts, [me, x], [stage], moved=8 * size)

    mine = exchange(crossed.reshape(row_block), "row")
    theirs = shift(turn(crossed), "col")
    mine, theirs = lax.optimization_barrier((mine, theirs))
    first = operator(
        lambda n, *refs: direct_body(n, 0.0, 1.0, *refs),
        [mine], row_consts, row_shape, row_block, 0,
    )
    first, theirs = lax.optimization_barrier((first, theirs))
    arriving = exchange(first, "row").reshape(local_cols, local_rows)
    double = operator(
        lambda n, *refs: direct_body(n, time_step, half_square, *refs),
        [first], row_consts, row_shape, row_block, 0,
    )
    base = operator(
        lambda n, *refs: arriving_body(n, time_step, half_square, cols, *refs),
        [me, *theirs], col_consts, col_shape, col_block, 1,
    )
    arriving, base, double = lax.optimization_barrier((arriving, base, double))
    double = exchange(double, "row").reshape(local_cols, local_rows)
    first = shift(turn(arriving), "col")
    last = operator(
        lambda n, *refs: added_body(n, cols, *refs),
        [me, base, *first], col_consts, parts, col_block, 1,
    )
    last = shift(last, "col")

    return call(
        functools.partial(finish_body, n),
        jax.ShapeDtypeStruct(pairs.shape, f32),
        [me, pairs, double, *last],
        [stage, pltpu.VMEM((local_cols, local_rows), f32)],
        moved=16 * size,
    )


def solution(mesh):
    body = functools.partial(shards, mesh.shape["row"], mesh.shape["col"])
    in_specs = (P("row", "col"), P(), P("row", "col", None), P())
    return jax.shard_map(
        body, mesh=mesh, in_specs=in_specs, out_specs=P("row", "col"), check_vma=False
    )
```

profile of v0, /device:TPU:1, one launch (start us, length us, event | category | flops | bytes accessed | tf_op | source)
XLA Modules:
  0.0 578.9 jit_solution(2363856126634467635)
XLA Ops:
  6.5 7.8 %shard_map.46.x_ref = f32[1600,800]{1,0:T(8,128)} custom-call(f32[800,1600]{1,0:T(8,128)} %x_ref.3), custom_call_target="tpu_custom_call" | custom-call | bytes 10240000 | tf_op jit(solution)/shard_map/pallas_call | solution.py:35
  14.3 0.0 copy-done.2
  14.4 0.8 reshape.21
  15.1 0.0 all-gather.4.cloned.1.call-update
  15.2 0.0 all-gather.6.cloned.1.call-start
  15.2 63.3 %all-gather.4.cloned.1.call-done = f32[1600,512]{1,0:T(8,128)} async-done(((f32[200,512]{1,0:T(8,128)}), f32[1600,512]{1,0:T(8,128)}) %all-gather.4.cloned.1.call-update) | async-done | bytes 3276816 | tf_op jit(solution)/shard_map/all_gather | solution.py:205
  78.5 0.0 all-gather.6.cloned.1.call-update
  78.5 4.7 all-to-all-start
  83.3 0.0 copy-start.3
  83.3 7.6 %shard_map.47 = (f32[200,1600]{1,0:T(8,128)}, f32[200,1600]{1,0:T(8,128)}, f32[200,1600]{1,0:T(8,128)}, f32[200,1600]{1,0:T(8,128)}) custom-call(s32[1]{0:T(128)} %bitcast.me_ref.refs_0_, f32[1600,800]{1,0:T(8,128)} %shard_map.46.x_ref), custom_call_target="tpu_custom_call" | custom-call | bytes 10240000 | tf_op jit(solution)/shard_map/pallas_call | solution.py:35
  90.9 2.8 collective-permute-start
  93.7 0.6 collective-permute-start.1
  94.3 0.0 collective-permute-start.2
  94.3 0.1 copy.5
  94.4 0.7 pad_maximum_fusion
  95.2 56.2 %collective-permute-done.refs_2_ = f32[200,1600]{1,0:T(8,128)S(1)} collective-permute-done((f32[200,1600]{1,0:T(8,128)}, f32[200,1600]{1,0:T(8,128)S(1)}, u32[]{:S(2)}, u32[]{:S(2)}) %collective-permute-start) | collective-permute-done | bytes 1280032 | tf_op jit(solution)/shard_map/ppermute | solution.py:188
  151.4 58.4 %collective-permute-done.1.refs_3_ = f32[200,1600]{1,0:T(8,128)S(1)} collective-permute-done((f32[200,1600]{1,0:T(8,128)}, f32[200,1600]{1,0:T(8,128)S(1)}, u32[]{:S(2)}, u32[]{:S(2)}) %collective-permute-start.1) | collective-permute-done | bytes 1280032 | tf_op jit(solution)/shard_map/ppermute | solution.py:188
  209.8 0.6 collective-permute-done.2.refs_4_
  210.3 0.0 all-to-all-done.refs_0_
  210.3 11.8 %all-gather.6.cloned.1.call-done = f32[6400,512]{1,0:T(8,128)} async-done(((f32[1600,512]{1,0:T(8,128)}), f32[6400,512]{1,0:T(8,128)}) %all-gather.6.cloned.1.call-update) | async-done | bytes 13107216 | tf_op jit(solution)/shard_map/all_gather | solution.py:206
  222.1 13.1 %shard_map.48 = (bf16[6400,512]{1,0:T(8,128)(2,1)}, bf16[6400,512]{1,0:T(8,128)(2,1)}) custom-call(f32[4,1600,512]{2,1,0:T(8,128)} %bitcast.11), custom_call_target="tpu_custom_call" | custom-call | flops 6553600 | bytes 26214400 | tf_op jit(solution)/shard_map/pallas_call | solution.py:209
  235.2 29.9 %shard_map.49.refs_0_ = f32[8,200,800]{2,1,0:T(8,128)} custom-call(f32[8,200,800]{2,1,0:T(8,128)} %all-to-all-done.refs_0_, bf16[6400,512]{1,0:T(8,128)(2,1)} %get-tuple-element.41.refs_1_.refs_5_.refs_6_, bf16[6400,512]{1,0:T(8,128)(2,1)} %get-tuple-element.42.refs_2_.refs_6_.refs_7_, f32[1,512]{1,0:T(1,128)} %bitcast.12, ...), custom_call_target="tpu_custom_call" | custom-call | flops 9093120000 | bytes 28467200 | tf_op jit(solution)/shard_map/pallas_call | solution.py:35
  265.1 5.4 all-to-all-start.1
  270.5 0.0 copy-done.4
  270.5 0.6 neg.13
  271.1 30.0 %shard_map.51 = f32[8,200,800]{2,1,0:T(8,128)} custom-call(f32[8,200,800]{2,1,0:T(8,128)} %shard_map.49.refs_0_, bf16[6400,512]{1,0:T(8,128)(2,1)} %get-tuple-element.41.refs_1_.refs_5_.refs_6_, bf16[6400,512]{1,0:T(8,128)(2,1)} %get-tuple-element.42.refs_2_.refs_6_.refs_7_, f32[1,512]{1,0:T(1,128)} %bitcast.13, ...), custom_call_target="tpu_custom_call" | custom-call | flops 9093120000 | bytes 28467200 | tf_op jit(solution)/shard_map/pallas_call | solution.py:35
  301.1 28.0 %shard_map.50.refs_1_ = f32[4,200,1600]{2,1,0:T(8,128)} custom-call(s32[1]{0:T(128)} %bitcast.me_ref.refs_0_, f32[200,1600]{1,0:T(8,128)} %get-tuple-element.48.refs_1_, f32[200,1600]{1,0:T(8,128)} %copy-done.5, f32[200,1600]{1,0:T(8,128)} %copy-done.6, f32[200,1600]{1,0:T(8,128)} %collective-permute-done.2.refs_4_, ...), custom_call_target="tpu_custom_call" | custom-call | flops 9093120000 | bytes 28467200 | tf_op jit(solution)/shard_map/pallas_call | solution.py:35
  329.1 67.3 %all-to-all-done.1 = f32[8,200,800]{2,1,0:T(8,128)} async-done(((f32[8,200,800]{2,1,0:T(8,128)}), f32[8,200,800]{2,1,0:T(8,128)}, u32[]{:S(2)}, u32[]{:S(2)}) %all-to-all-start.1) | async-done | bytes 5120032 | tf_op jit(solution)/shard_map/all_to_all | solution.py:182
  396.4 4.7 all-to-all-start.2
  401.1 7.0 %shard_map.52 = (f32[200,1600]{1,0:T(8,128)}, f32[200,1600]{1,0:T(8,128)}, f32[200,1600]{1,0:T(8,128)}, f32[200,1600]{1,0:T(8,128)}) custom-call(s32[1]{0:T(128)} %bitcast.me_ref.refs_0_, f32[1600,800]{1,0:T(8,128)} %bitcast.5.x_ref), custom_call_target="tpu_custom_call" | custom-call | bytes 10240000 | tf_op jit(solution)/shard_map/pallas_call | solution.py:35
  408.0 1.5 collective-permute-start.3
  409.6 1.2 collective-permute-start.4
  410.7 0.0 collective-permute-start.5
  410.7 27.6 %collective-permute-done.3.refs_3_ = f32[200,1600]{1,0:T(8,128)S(1)} collective-permute-done((f32[200,1600]{1,0:T(8,128)}, f32[200,1600]{1,0:T(8,128)S(1)}, u32[]{:S(2)}, u32[]{:S(2)}) %collective-permute-start.3) | collective-permute-done | bytes 1280032 | tf_op jit(solution)/shard_map/ppermute | solution.py:188
  438.4 30.4 %collective-permute-done.4.refs_4_ = f32[200,1600]{1,0:T(8,128)S(1)} collective-permute-done((f32[200,1600]{1,0:T(8,128)}, f32[200,1600]{1,0:T(8,128)S(1)}, u32[]{:S(2)}, u32[]{:S(2)}) %collective-permute-start.4) | collective-permute-done | bytes 1280032 | tf_op jit(solution)/shard_map/ppermute | solution.py:188
  468.8 0.4 collective-permute-done.5.refs_5_
  469.2 0.0 copy-done.7
  469.2 0.6 copy-done.8
  469.9 0.4 copy-done.9
  470.3 29.8 %shard_map.53 = (f32[200,1600]{1,0:T(8,128)}, f32[200,1600]{1,0:T(8,128)}, f32[200,1600]{1,0:T(8,128)}, f32[200,1600]{1,0:T(8,128)}) custom-call(s32[1]{0:T(128)} %bitcast.me_ref.refs_0_, f32[4,200,1600]{2,1,0:T(8,128)} %shard_map.50.refs_1_, f32[200,1600]{1,0:T(8,128)} %get-tuple-element.55.refs_2_, f32[200,1600]{1,0:T(8,128)} %copy-done.7, ...), custom_call_target="tpu_custom_call" | custom-call | flops 9093120000 | bytes 28467200 | tf_op jit(solution)/shard_map/pallas_call | solution.py:35
  500.1 0.0 collective-permute-start.6
  500.1 0.5 collective-permute-start.7
  500.5 0.8 collective-permute-start.8
  501.3 26.6 %collective-permute-done.6.refs_1_ = f32[200,1600]{1,0:T(8,128)S(1)} collective-permute-done((f32[200,1600]{1,0:T(8,128)}, f32[200,1600]{1,0:T(8,128)S(1)}, u32[]{:S(2)}, u32[]{:S(2)}) %collective-permute-start.6) | collective-permute-done | bytes 1280032 | tf_op jit(solution)/shard_map/ppermute | solution.py:188
  528.0 28.7 %collective-permute-done.7.refs_2_ = f32[200,1600]{1,0:T(8,128)S(1)} collective-permute-done((f32[200,1600]{1,0:T(8,128)}, f32[200,1600]{1,0:T(8,128)S(1)}, u32[]{:S(2)}, u32[]{:S(2)}) %collective-permute-start.7) | collective-permute-done | bytes 1280032 | tf_op jit(solution)/shard_map/ppermute | solution.py:188
  556.7 2.2 collective-permute-done.8.refs_3_
  558.8 0.0 all-to-all-done.2
  558.9 13.2 %shard_map.54 = f32[800,1600]{1,0:T(8,128)} custom-call(s32[1]{0:T(128)} %bitcast.me_ref.refs_0_, f32[800,1600]{1,0:T(8,128)} %x_ref.3, f32[1600,800]{1,0:T(8,128)} %bitcast.7.crossed_ref, f32[200,1600]{1,0:T(8,128)} %get-tuple-element.59.refs_0_, f32[200,1600]{1,0:T(8,128)} %copy-done, f32[200,1600]{1,0:T(8,128)} %copy-done.1, ...), custom_call_target="tpu_custom_call" | custom-call | bytes 20480000 | tf_op jit(solution)/shard_map/pallas_call | solution.py:35
  (17 shorter events, 0.1 us)
Async XLA Ops:
  6.5 7.8 %copy-start.2 = (f32[10,20,512]{2,1,0:T(8,128)S(1)}, f32[10,20,512]{2,1,0:T(8,128)}, u32[]{:S(2)}) copy-start(f32[10,20,512]{2,1,0:T(8,128)} %param.6) | copy-start | bytes 1228804
  6.5 72.0 %all-gather.4.cloned.1.call-start = ((), (), s32[]{:S(2)}) async-start(), calls=%async_computation.3 | async-start | bytes 3686400 | tf_op jit(solution)/shard_map/all_gather | solution.py:205
  15.2 206.9 %all-gather.6.cloned.1.call-start = ((), (), s32[]{:S(2)}) async-start(), calls=%async_computation.4 | async-start | bytes 16384000 | tf_op jit(solution)/shard_map/all_gather | solution.py:206
  78.5 131.8 %all-to-all-start = ((f32[8,200,800]{2,1,0:T(8,128)}), f32[8,200,800]{2,1,0:T(8,128)}, u32[]{:S(2)}, u32[]{:S(2)}) async-start(f32[8,200,800]{2,1,0:T(8,128)} %bitcast.10), calls=%async_computation | async-start | bytes 11468800 | tf_op jit(solution)/shard_map/all_to_all | solution.py:182
  83.3 11.1 %copy-start.3 = (f32[80,80]{1,0:T(8,128)S(1)}, f32[80,80]{1,0:T(8,128)}, u32[]{:S(2)}) copy-start(f32[80,80]{1,0:T(8,128)} %param.5) | copy-start | bytes 76804
  90.9 60.5 %collective-permute-start = (f32[200,1600]{1,0:T(8,128)}, f32[200,1600]{1,0:T(8,128)S(1)}, u32[]{:S(2)}, u32[]{:S(2)}) collective-permute-start(f32[200,1600]{1,0:T(8,128)} %get-tuple-element.36), channel_id=1, source_target_pairs={{0,1},{1,2},{2,3},{3,0},{4,5},{5,6},{6,7},{7,4},{8,9},{9,10},{10,1... | collective-permute-start | bytes 3840008 | tf_op jit(solution)/shard_map/ppermute | solution.py:188
  93.7 116.0 %collective-permute-start.1 = (f32[200,1600]{1,0:T(8,128)}, f32[200,1600]{1,0:T(8,128)S(1)}, u32[]{:S(2)}, u32[]{:S(2)}) collective-permute-start(f32[200,1600]{1,0:T(8,128)} %get-tuple-element.37), channel_id=1, source_target_pairs={{0,2},{1,3},{2,0},{3,1},{4,6},{5,7},{6,4},{7,5},{8,10},{9,11},{10,... | collective-permute-start | bytes 3840008 | tf_op jit(solution)/shard_map/ppermute | solution.py:188
  94.3 116.0 %collective-permute-start.2 = (f32[200,1600]{1,0:T(8,128)}, f32[200,1600]{1,0:T(8,128)}, u32[]{:S(2)}, u32[]{:S(2)}) collective-permute-start(f32[200,1600]{1,0:T(8,128)} %get-tuple-element.38), channel_id=1, source_target_pairs={{0,3},{1,0},{2,1},{3,2},{4,7},{5,4},{6,5},{7,6},{8,11},{9,8},{10,9... | collective-permute-start | bytes 3840008 | tf_op jit(solution)/shard_map/ppermute | solution.py:188
  151.4 83.8 %copy-start.5 = (f32[200,1600]{1,0:T(8,128)}, f32[200,1600]{1,0:T(8,128)S(1)}, u32[]{:S(2)}) copy-start(f32[200,1600]{1,0:T(8,128)S(1)} %collective-permute-done.refs_2_) | copy-start | bytes 3840004
  209.7 25.5 %copy-start.6 = (f32[200,1600]{1,0:T(8,128)}, f32[200,1600]{1,0:T(8,128)S(1)}, u32[]{:S(2)}) copy-start(f32[200,1600]{1,0:T(8,128)S(1)} %collective-permute-done.1.refs_3_) | copy-start | bytes 3840004
  265.1 5.4 copy-start.4
  265.1 131.3 %all-to-all-start.1 = ((f32[8,200,800]{2,1,0:T(8,128)}), f32[8,200,800]{2,1,0:T(8,128)}, u32[]{:S(2)}, u32[]{:S(2)}) async-start(f32[8,200,800]{2,1,0:T(8,128)} %shard_map.49.refs_0_), calls=%async_computation.1 | async-start | bytes 11468800 | tf_op jit(solution)/shard_map/all_to_all | solution.py:182
  396.4 162.5 %all-to-all-start.2 = ((f32[8,200,800]{2,1,0:T(8,128)}), f32[8,200,800]{2,1,0:T(8,128)}, u32[]{:S(2)}, u32[]{:S(2)}) async-start(f32[8,200,800]{2,1,0:T(8,128)} %shard_map.51), calls=%async_computation.2 | async-start | bytes 11468800 | tf_op jit(solution)/shard_map/all_to_all | solution.py:182
  408.0 30.3 %collective-permute-start.3 = (f32[200,1600]{1,0:T(8,128)}, f32[200,1600]{1,0:T(8,128)S(1)}, u32[]{:S(2)}, u32[]{:S(2)}) collective-permute-start(f32[200,1600]{1,0:T(8,128)} %get-tuple-element.56), channel_id=1, source_target_pairs={{0,1},{1,2},{2,3},{3,0},{4,5},{5,6},{6,7},{7,4},{8,9},{9,10},{10,1... | collective-permute-start | bytes 3840008 | tf_op jit(solution)/shard_map/ppermute | solution.py:188
  409.6 59.2 %collective-permute-start.4 = (f32[200,1600]{1,0:T(8,128)}, f32[200,1600]{1,0:T(8,128)S(1)}, u32[]{:S(2)}, u32[]{:S(2)}) collective-permute-start(f32[200,1600]{1,0:T(8,128)} %get-tuple-element.57), channel_id=1, source_target_pairs={{0,2},{1,3},{2,0},{3,1},{4,6},{5,7},{6,4},{7,5},{8,10},{9,11},{10,... | collective-permute-start | bytes 3840008 | tf_op jit(solution)/shard_map/ppermute | solution.py:188
  410.7 58.5 %collective-permute-start.5 = (f32[200,1600]{1,0:T(8,128)}, f32[200,1600]{1,0:T(8,128)S(1)}, u32[]{:S(2)}, u32[]{:S(2)}) collective-permute-start(f32[200,1600]{1,0:T(8,128)} %get-tuple-element.58), channel_id=1, source_target_pairs={{0,3},{1,0},{2,1},{3,2},{4,7},{5,4},{6,5},{7,6},{8,11},{9,8},{10,9... | collective-permute-start | bytes 3840008 | tf_op jit(solution)/shard_map/ppermute | solution.py:188
  438.3 30.9 %copy-start.7 = (f32[200,1600]{1,0:T(8,128)}, f32[200,1600]{1,0:T(8,128)S(1)}, u32[]{:S(2)}) copy-start(f32[200,1600]{1,0:T(8,128)S(1)} %collective-permute-done.3.refs_3_) | copy-start | bytes 3840004
  468.8 1.1 copy-start.8
  469.2 1.1 copy-start.9
  500.1 27.9 %collective-permute-start.6 = (f32[200,1600]{1,0:T(8,128)}, f32[200,1600]{1,0:T(8,128)S(1)}, u32[]{:S(2)}, u32[]{:S(2)}) collective-permute-start(f32[200,1600]{1,0:T(8,128)} %get-tuple-element.60), channel_id=1, source_target_pairs={{0,1},{1,2},{2,3},{3,0},{4,5},{5,6},{6,7},{7,4},{8,9},{9,10},{10,1... | collective-permute-start | bytes 3840008 | tf_op jit(solution)/shard_map/ppermute | solution.py:188
  500.1 56.6 %collective-permute-start.7 = (f32[200,1600]{1,0:T(8,128)}, f32[200,1600]{1,0:T(8,128)S(1)}, u32[]{:S(2)}, u32[]{:S(2)}) collective-permute-start(f32[200,1600]{1,0:T(8,128)} %get-tuple-element.61), channel_id=1, source_target_pairs={{0,2},{1,3},{2,0},{3,1},{4,6},{5,7},{6,4},{7,5},{8,10},{9,11},{10,... | collective-permute-start | bytes 3840008 | tf_op jit(solution)/shard_map/ppermute | solution.py:188
  500.5 58.3 %collective-permute-start.8 = (f32[200,1600]{1,0:T(8,128)}, f32[200,1600]{1,0:T(8,128)}, u32[]{:S(2)}, u32[]{:S(2)}) collective-permute-start(f32[200,1600]{1,0:T(8,128)} %get-tuple-element.62), channel_id=1, source_target_pairs={{0,3},{1,0},{2,1},{3,2},{4,7},{5,4},{6,5},{7,6},{8,11},{9,8},{10,9... | collective-permute-start | bytes 3840008 | tf_op jit(solution)/shard_map/ppermute | solution.py:188
  528.0 30.9 %copy-start = (f32[200,1600]{1,0:T(8,128)}, f32[200,1600]{1,0:T(8,128)S(1)}, u32[]{:S(2)}) copy-start(f32[200,1600]{1,0:T(8,128)S(1)} %collective-permute-done.6.refs_1_) | copy-start | bytes 3840004
  556.7 2.2 copy-start.1
Sparse Core Ops, SparseCore 0:
  15.3 63.1 all-gather.3
  80.1 142.0 all-gather.5
where the time goes:
time: 580 us; the launch traced here: 579 us
  waiting for transfers between devices  374 us (64%)
  Pallas kernels  166 us (29%)
  starting transfers between devices  22.2 us (4%)
  between operations  13.5 us (2%)
    ppermute x9, waiting for transfers between devices, shift(): lax.ppermute(parts[s], axis, [(d, (d + s) % n) for d in range(n)])  231 us
    pallas_call x8, Pallas kernels, call(): pl.pallas_call(body, in_specs=[smem if x.dtype == jnp.int32 else vmem for...  153 us
    all_to_all x3, waiting for transfers between devices, exchange(): return lax.all_to_all(x, axis, split_axis=0, concat_axis=0, tiled=True)  67.3 us
    all_gather x1, waiting for transfers between devices, shards(): whole = lax.all_gather(aux.reshape(-1, naux), 'row', axis=0, tiled=True)  63.3 us
    all_to_all x3, starting transfers between devices, exchange(): return lax.all_to_all(x, axis, split_axis=0, concat_axis=0, tiled=True)  14.8 us
    pallas_call x1, Pallas kernels, shards(): pl.pallas_call(functools.partial(split_body, n), grid=(n // group,), in_s...  13.1 us
    all_gather x1, waiting for transfers between devices, shards(): whole = lax.all_gather(whole, 'col', axis=0, tiled=False)  11.8 us
  transfers between devices with their start and end apart: 14, of which 12 were waited for; matrix products, arithmetic and copies ran while one was open for 0% of the time, Pallas kernels for 18%

commit v1 on v0

--- a/solution.py
+++ b/solution.py
@@ -47,38 +47,85 @@
     return [slice(start, min(start + size, total)) for start in range(0, total, size)]
 
 
-def cross_body(n, x_ref, crossed_ref):
+def folded(batch, width):
+    def cost(g):
+        return -(-batch // g // 8) * -(-g * width // 128)
+
+    return min([g for g in range(1, batch + 1) if g == 1 or batch % (8 * g) == 0], key=cost)
+
+
+def wire(block):
+    _, batch, width = block
+    g = folded(batch, width)
+    return jax.ShapeDtypeStruct((batch // g, g * width), f32)
+
+
+def hand_out(me_ref, stage, outs):
+    width = stage.shape[2]
+    for s, out_ref in enumerate(outs):
+        b, rows = lax.rem(me_ref[0] + s, len(outs)), out_ref.shape[0]
+        parts = [
+            stage[b, g * rows : (g + 1) * rows, :] for g in range(out_ref.shape[1] // width)
+        ]
+        out_ref[...] = jnp.concatenate(parts, axis=1) if len(parts) > 1 else parts[0]
+
+
+def take_in(me_ref, ins, stage):
+    width = stage.shape[2]
+    for s, in_ref in enumerate(ins):
+        b, rows = lax.rem(me_ref[0] + len(ins) - s, len(ins)), in_ref.shape[0]
+        for g in range(in_ref.shape[1] // width):
+            stage[b, g * rows : (g + 1) * rows, :] = in_ref[:, g * width : (g + 1) * width]
+
+
+def rows_of(stage, span):
+    batch = stage.shape[1]
+    parts = []
+    for b in range(span.start // batch, -(-span.stop // batch)):
+        low, high = max(span.start - b * batch, 0), min(span.stop - b * batch, batch)
+        parts.append(stage[b, low:high, :])
+    return jnp.concatenate(parts, axis=0) if len(parts) > 1 else parts[0]
+
+
+def cross_body(n, me_ref, x_ref, crossed_ref, *refs):
+    *outs, stage = refs
     rows = tiles(x_ref.shape[0], n)
     for k in tiles(x_ref.shape[1], n):
         crossed_ref[k, :] = jnp.concatenate([x_ref[i, k] for i in rows], axis=1)
+    batch = stage.shape[1]
+    for b in range(stage.shape[0]):
+        stage[b] = crossed_ref[b * batch : (b + 1) * batch, :]
+    hand_out(me_ref, stage, outs)
 
 
 def turn_body(me_ref, x_ref, *refs):
     *outs, stage = refs
+    turn_rows(lambda strip: x_ref[strip, :], x_ref.shape[0], stage)
+    hand_out(me_ref, stage, outs)
+
+
+def turn_rows(rows, total, stage):
     count, batch, _ = stage.shape
-    for strip in tiles(x_ref.shape[0]):
-        turned = x_ref[strip, :].T
+    for strip in tiles(total):
+        turned = rows(strip).T
         for b in range(count):
             stage[b, :, strip] = turned[b * batch : (b + 1) * batch]
-    hand_out(me_ref, stage, outs)
-
-
-def hand_out(me_ref, stage, outs):
-    for s, out_ref in enumerate(outs):
-        out_ref[...] = stage[lax.rem(me_ref[0] + s, len(outs))]
-
-
-def take_in(me_ref, ins, stage):
-    for s, in_ref in enumerate(ins):
-        stage[lax.rem(me_ref[0] + len(ins) - s, len(ins))] = in_ref[...]
-
-
-def finish_body(n, me_ref, x_ref, crossed_ref, *refs):
-    *ins, out_ref, stage, total = refs
+
+
+def turn_arriving_body(count, row_ref, me_ref, *refs):
+    ins, (*outs, arrived, stage) = refs[:count], refs[count:]
+    take_in(row_ref, ins, arrived)
+    turn_rows(lambda strip: rows_of(arrived, strip), arrived.shape[0] * arrived.shape[1], stage)
+    hand_out(me_ref, stage, outs)
+
+
+def finish_body(n, count, row_ref, me_ref, x_ref, *refs):
+    crossed, (*ins, out_ref, arrived, stage, total) = refs[:count], refs[count:]
+    take_in(row_ref, crossed, arrived)
     take_in(me_ref, ins, stage)
     for strip in tiles(total.shape[0]):
         turned = jnp.concatenate([stage[b, :, strip] for b in range(len(ins))], axis=0)
-        total[strip, :] = crossed_ref[strip, :] + turned.T
+        total[strip, :] = rows_of(arrived, strip) + turned.T
     cols = tiles(x_ref.shape[1], n)
     for i in tiles(x_ref.shape[0], n):
         out_ref[i, :] = x_ref[i, :] + jnp.concatenate([total[k, i] for k in cols], axis=1)
@@ -151,23 +198,27 @@
     lax.fori_loop(0, blocks, result, 0)
 
 
-def direct_body(n, keep, scale, x_ref, *refs):
-    *consts, out_ref, xp, zp = refs
-    apply_operator(n, keep, scale, x_ref, out_ref, *consts, xp, zp)
+def leaving_body(n, keep, scale, count, me_ref, x_ref, *refs):
+    *consts, stage, xp, zp = refs
+    consts, outs = consts[:-count], consts[-count:]
+    apply_operator(n, keep, scale, x_ref, stage, *consts, xp, zp)
+    hand_out(me_ref, stage, outs)
 
 
 def arriving_body(n, keep, scale, count, me_ref, *refs):
-    ins, (*consts, out_ref, stage, xp, zp) = refs[:count], refs[count:]
+    ins, (*consts, stage, xp, zp) = refs[:count], refs[count:]
+    consts, (out_ref, *outs) = consts[:5], consts[5:]
     take_in(me_ref, ins, stage)
     apply_operator(n, keep, scale, stage, out_ref, *consts, xp, zp)
+    hand_out(me_ref, out_ref, outs)
 
 
 def added_body(n, count, me_ref, base_ref, *refs):
     ins, rest = refs[:count], refs[count:]
     consts, outs, (stage, xp, zp) = rest[:-3 - count], rest[-3 - count : -3], rest[-3:]
-    for s in range(count):
-        b = lax.rem(me_ref[0] + count - s, count)
-        stage[b] = base_ref[b] + (time_step * time_step) * ins[s][...]
+    take_in(me_ref, ins, stage)
+    for b in range(count):
+        stage[b] = base_ref[b] + (time_step * time_step) * stage[b]
     apply_operator(n, 0.0, 1.0, stage, stage, *consts, xp, zp)
     hand_out(me_ref, stage, outs)
 
@@ -176,10 +227,6 @@
     high = lax.reduce_precision(matrix, 8, 7)
     low = matrix - high
     return jnp.concatenate([high, low, high], axis=1).astype(bf16)
-
-
-def exchange(x, axis):
-    return lax.all_to_all(x, axis, split_axis=0, concat_axis=0, tiled=True)
 
 
 def shift(parts, axis):
@@ -194,15 +241,27 @@
     naux = aux.shape[2]
     local_rows, local_cols = pairs.shape
     size = local_rows * local_cols
-    me = lax.axis_index("col").astype(jnp.int32).reshape(1)
-
-    crossed = call(
+    row_me, col_me = (lax.axis_index(a).astype(jnp.int32).reshape(1) for a in ("row", "col"))
+
+    row_block = (rows, local_cols // rows, local_rows)
+    col_block = (cols, local_rows // cols, local_cols)
+    row_wires, col_wires = [wire(row_block)] * rows, [wire(col_block)] * cols
+    row_shape = jax.ShapeDtypeStruct(row_block, f32)
+    col_shape = jax.ShapeDtypeStruct(col_block, f32)
+    row_stage, col_stage = pltpu.VMEM(row_block, f32), pltpu.VMEM(col_block, f32)
+
+    crossed, *mine = call(
         functools.partial(cross_body, n),
-        jax.ShapeDtypeStruct((local_cols, local_rows), f32), [pairs], moved=8 * size,
-    )
-
-    crossed, aux = lax.optimization_barrier((crossed, aux))
+        [jax.ShapeDtypeStruct((local_cols, local_rows), f32), *row_wires],
+        [row_me, pairs], [row_stage], moved=12 * size,
+    )
+    theirs = call(turn_body, col_wires, [col_me, crossed], [col_stage], moved=8 * size)
+
+    mine[0], aux = lax.optimization_barrier((mine[0], aux))
     whole = lax.all_gather(aux.reshape(-1, naux), "row", axis=0, tiled=True)
+    mine, theirs = shift(mine, "row"), shift(theirs, "col")
+    early = rows // 2 + 1
+    whole, mine[:early], theirs = lax.optimization_barrier((whole, mine[:early], theirs))
     whole = lax.all_gather(whole, "col", axis=0, tiled=False)
     group = 8 if n % 8 == 0 else n
     shape = jax.ShapeDtypeStruct((n * n, naux), bf16)
@@ -223,61 +282,53 @@
     gain = weights.reshape(1, naux)
     half_square = time_step * time_step / 2.0
 
-    def operator(body, arrays, consts, outs, block, staged):
+    def operator(body, arrays, consts, outs, block):
         blocks, batch, width = block
         work = pltpu.VMEM((-(-batch // 128), n * n, 128), f32)
         return call(
             functools.partial(body, n),
             outs,
             [*arrays, high, low, *consts],
-            [pltpu.VMEM(block, f32)] * staged + [work, work],
+            [pltpu.VMEM(block, f32), work, work],
             flops=12 * n * n * (naux + n) * batch,
             moved=4 * n * n * naux + 12 * size,
         )
 
-    row_block = (rows, local_cols // rows, local_rows)
-    col_block = (cols, local_rows // cols, local_cols)
-    row_shape = jax.ShapeDtypeStruct(row_block, f32)
-    col_shape = jax.ShapeDtypeStruct(col_block, f32)
-    parts = [jax.ShapeDtypeStruct(col_block[1:], f32)] * cols
     row_consts = [gain, left, right]
     col_consts = [-gain, right, left]
-    stage = pltpu.VMEM(col_block, f32)
-
-    def turn(x):
-        return call(turn_body, parts, [me, x], [stage], moved=8 * size)
-
-    mine = exchange(crossed.reshape(row_block), "row")
-    theirs = shift(turn(crossed), "col")
-    mine, theirs = lax.optimization_barrier((mine, theirs))
-    first = operator(
-        lambda n, *refs: direct_body(n, 0.0, 1.0, *refs),
-        [mine], row_consts, row_shape, row_block, 0,
+
+    first, *arriving = operator(
+        lambda n, *refs: arriving_body(n, 0.0, 1.0, rows, *refs),
+        [row_me, *mine], row_consts, [row_shape, *row_wires], row_block,
     )
     first, theirs = lax.optimization_barrier((first, theirs))
-    arriving = exchange(first, "row").reshape(local_cols, local_rows)
+    arriving = shift(arriving, "row")
     double = operator(
-        lambda n, *refs: direct_body(n, time_step, half_square, *refs),
-        [first], row_consts, row_shape, row_block, 0,
-    )
-    base = operator(
+        lambda n, *refs: leaving_body(n, time_step, half_square, rows, *refs),
+        [row_me, first], row_consts, row_wires, row_block,
+    )
+    (base,) = operator(
         lambda n, *refs: arriving_body(n, time_step, half_square, cols, *refs),
-        [me, *theirs], col_consts, col_shape, col_block, 1,
+        [col_me, *theirs], col_consts, [col_shape], col_block,
     )
     arriving, base, double = lax.optimization_barrier((arriving, base, double))
-    double = exchange(double, "row").reshape(local_cols, local_rows)
-    first = shift(turn(arriving), "col")
+    double = shift(double, "row")
+    first = call(
+        functools.partial(turn_arriving_body, rows),
+        col_wires, [row_me, col_me, *arriving], [row_stage, col_stage], moved=8 * size,
+    )
+    first = shift(first, "col")
     last = operator(
         lambda n, *refs: added_body(n, cols, *refs),
-        [me, base, *first], col_consts, parts, col_block, 1,
+        [col_me, base, *first], col_consts, col_wires, col_block,
     )
     last = shift(last, "col")
 
     return call(
-        functools.partial(finish_body, n),
+        functools.partial(finish_body, n, rows),
         jax.ShapeDtypeStruct(pairs.shape, f32),
-        [me, pairs, double, *last],
-        [stage, pltpu.VMEM((local_cols, local_rows), f32)],
+        [row_me, col_me, pairs, *double, *last],
+        [row_stage, col_stage, pltpu.VMEM((local_cols, local_rows), f32)],
         moved=16 * size,
     )
 

time: 580 us -> 585 us (level); the launches traced: 579 us -> 575 us
  waiting for transfers between devices: 374 us -> 208 us
  starting transfers between devices: 22.2 us -> 167 us
  Pallas kernels: 166 us -> 177 us
    ppermute x9 -> x30, starting transfers between devices: 7.37 us -> 167 us  [shift(): lax.ppermute(parts[s], axis, [(d, (d + s) % n) for d in range(n)])]
    ppermute x9 -> x30, waiting for transfers between devices: 231 us -> 128 us  [shift(): lax.ppermute(parts[s], axis, [(d, (d + s) % n) for d in range(n)])]
    all_gather x1, waiting for transfers between devices: 11.8 us -> 80.7 us  [shards(): whole = lax.all_gather(whole, 'col', axis=0, tiled=False)]
    all_to_all x3 -> x0, waiting for transfers between devices: 67.3 us -> none  [exchange(): return lax.all_to_all(x, axis, split_axis=0, concat_axis=0, tiled=True)]
    all_gather x1, waiting for transfers between devices: 63.3 us -> 0.17 us  [shards(): whole = lax.all_gather(aux.reshape(-1, naux), 'row', axis=0, tiled=True)]
    all_to_all x3 -> x0, starting transfers between devices: 14.8 us -> none  [exchange(): return lax.all_to_all(x, axis, split_axis=0, concat_axis=0, tiled=True)]
    pallas_call x8, Pallas kernels: 153 us -> 164 us  [call(): pl.pallas_call(body, in_specs=[smem if x.dtype == jnp.int32 else vmem for...]
  transfers between devices with their start and end apart: 14 -> 32, of which waited for: 12 -> 10; matrix products, arithmetic and copies ran while one was open for 0% -> 0% of each run, Pallas kernels for 18% -> 19%
where the time goes in v1:
time: 585 us; the launch traced here: 575 us
  waiting for transfers between devices  208 us (36%)
  Pallas kernels  177 us (30%)
  starting transfers between devices  167 us (29%)
  between operations  14 us (2%)
  local copies, waits for them, and re-layouts  7.69 us (1%)
    ppermute x30, starting transfers between devices, shift(): lax.ppermute(parts[s], axis, [(d, (d + s) % n) for d in range(n)])  167 us
    pallas_call x8, Pallas kernels, call(): pl.pallas_call(body, in_specs=[smem if x.dtype == jnp.int32 else vmem for...  164 us
    ppermute x30, waiting for transfers between devices, shift(): lax.ppermute(parts[s], axis, [(d, (d + s) % n) for d in range(n)])  128 us
    all_gather x1, waiting for transfers between devices, shards(): whole = lax.all_gather(whole, 'col', axis=0, tiled=False)  80.7 us
    pallas_call x1, Pallas kernels, shards(): pl.pallas_call(functools.partial(split_body, n), grid=(n // group,), in_s...  13.1 us
  transfers between devices with their start and end apart: 32, of which 10 were waited for; matrix products, arithmetic and copies ran while one was open for 0% of the time, Pallas kernels for 19%

profile of v1, /device:TPU:1, one launch (start us, length us, event | category | flops | bytes accessed | tf_op | source)
XLA Modules:
  0.0 575.5 jit_solution(10254249277797411569)
XLA Ops:
  6.5 10.5 %shard_map.46 = (f32[1600,800]{1,0:T(8,128)}, f32[8,20000]{1,0:T(8,128)}, f32[8,20000]{1,0:T(8,128)}, f32[8,20000]{1,0:T(8,128)}, f32[8,20000]{1,0:T(8,128)}, /*...) custom-call(s32[1]{0:T(128)} %bitcast.me_ref.refs_0_.row_ref, f32[800,1600]{1,0:T(8,128)} %x_ref.3), custom_call_target="tpu_custom_call" | custom-call | bytes 15360000 | tf_op jit(solution)/shard_map/pallas_call | solution.py:35
  17.0 0.8 reshape.15
  18.3 2.1 collective-permute-start
  20.3 1.3 collective-permute-start.1
  21.6 7.1 %shard_map.47 = (f32[8,40000]{1,0:T(8,128)}, f32[8,40000]{1,0:T(8,128)}, f32[8,40000]{1,0:T(8,128)}, f32[8,40000]{1,0:T(8,128)}) custom-call(s32[1]{0:T(128)} %bitcast.1.me_ref.refs_0_, f32[1600,800]{1,0:T(8,128)} %get-tuple-element.86.x_ref), custom_call_target="tpu_custom_call" | custom-call | bytes 10240000 | tf_op jit(solution)/shard_map/pallas_call | solution.py:35
  28.7 2.3 collective-permute-start.4
  31.5 9.5 %collective-permute-done.refs_2_ = f32[8,20000]{1,0:T(8,128)S(1)} collective-permute-done((f32[8,20000]{1,0:T(8,128)S(1)}, f32[8,20000]{1,0:T(8,128)S(1)}, u32[]{:S(2)}, u32[]{:S(2)}) %collective-permute-start) | collective-permute-done | bytes 640032 | tf_op jit(solution)/shard_map/ppermute | solution.py:235
  41.5 4.7 collective-permute-start.3
  46.3 80.3 %collective-permute-done.2.refs_4_ = f32[8,20000]{1,0:T(8,128)S(1)} collective-permute-done((f32[8,20000]{1,0:T(8,128)S(1)}, f32[8,20000]{1,0:T(8,128)S(1)}, u32[]{:S(2)}, u32[]{:S(2)}) %collective-permute-start.2) | collective-permute-done | bytes 640032 | tf_op jit(solution)/shard_map/ppermute | solution.py:235
  127.5 1.0 copy-done.22
  128.5 18.4 %collective-permute-start.7 = (f32[8,20000]{1,0:T(8,128)S(1)}, f32[8,20000]{1,0:T(8,128)S(1)}, u32[]{:S(2)}, u32[]{:S(2)}) collective-permute-start(f32[8,20000]{1,0:T(8,128)S(1)} %copy-done.22), channel_id=1, source_target_pairs={{0,20},{4,24},{8,28},{12,0},{16,4},{20,8},{24,12},{28,16},{1,21},{... | collective-permute-start | bytes 1920008 | tf_op jit(solution)/shard_map/ppermute | solution.py:235
  147.5 1.2 collective-permute-start.9
  149.5 0.7 pad_maximum_fusion
  150.2 80.7 %all-gather.6.cloned.1.call-done = f32[6400,512]{1,0:T(8,128)} async-done(((f32[1600,512]{1,0:T(8,128)}), f32[6400,512]{1,0:T(8,128)}) %all-gather.6.cloned.1.call-update) | async-done | bytes 13107216 | tf_op jit(solution)/shard_map/all_gather | solution.py:265
  230.9 13.1 %shard_map.48 = (bf16[6400,512]{1,0:T(8,128)(2,1)}, bf16[6400,512]{1,0:T(8,128)(2,1)}) custom-call(f32[4,1600,512]{2,1,0:T(8,128)} %bitcast.8), custom_call_target="tpu_custom_call" | custom-call | flops 6553600 | bytes 26214400 | tf_op jit(solution)/shard_map/pallas_call | solution.py:268
  244.0 0.8 copy-done.26
  245.0 33.7 %shard_map.49 = (f32[8,200,800]{2,1,0:T(8,128)}, f32[8,20000]{1,0:T(8,128)}, f32[8,20000]{1,0:T(8,128)}, f32[8,20000]{1,0:T(8,128)}, f32[8,20000]{1,0:T(8,128)},...) custom-call(s32[1]{0:T(128)} %bitcast.me_ref.refs_0_.row_ref, ...), custom_call_target="tpu_custom_call" | custom-call | flops 9093120000 | bytes 28467200 | tf_op jit(solution)/shard_map/pallas_call | solution.py:35
  278.7 1.2 collective-permute-start.10
  279.9 1.4 collective-permute-start.11
  281.2 2.1 collective-permute-start.12
  283.4 1.1 collective-permute-start.13
  284.5 2.2 collective-permute-start.14
  286.6 30.9 %shard_map.51 = (f32[8,20000]{1,0:T(8,128)}, f32[8,20000]{1,0:T(8,128)}, f32[8,20000]{1,0:T(8,128)}, f32[8,20000]{1,0:T(8,128)}, f32[8,20000]{1,0:T(8,128)}, /*i...) custom-call(s32[1]{0:T(128)} %bitcast.me_ref.refs_0_.row_ref, f32[8,200,800]{2,1,0:T(8,128)} %get-tuple-element.119.refs_1_, ...), custom_call_target="tpu_custom_call" | custom-call | flops 9093120000 | bytes 28467200 | tf_op jit(solution)/shard_map/pallas_call | solution.py:35
  317.6 1.2 collective-permute-start.15
  318.8 1.1 collective-permute-start.16
  319.9 28.3 %shard_map.50.refs_1_ = f32[4,200,1600]{2,1,0:T(8,128)} custom-call(s32[1]{0:T(128)} %bitcast.1.me_ref.refs_0_, f32[8,40000]{1,0:T(8,128)} %get-tuple-element.115.refs_1_, f32[8,40000]{1,0:T(8,128)} %collective-permute-done.4.refs_2_, f32[8,40000]{1,0:T(8,128)} %collective-permute-done.5.refs_3_, f32[8,40000]{1,0:T(8,128)} %collective-permute-done.6.refs_4_, ...), custom_call_target="tpu_custom_call" | custom-call | flops 9093120000 | bytes 28467200 | tf_op jit(solution)/shard_map/pallas_call | solution.py:35
  348.2 4.9 collective-permute-done.12.refs_3_
  353.6 10.2 %collective-permute-done.16.refs_7_ = f32[8,20000]{1,0:T(8,128)} collective-permute-done((f32[8,20000]{1,0:T(8,128)}, f32[8,20000]{1,0:T(8,128)}, u32[]{:S(2)}, u32[]{:S(2)}) %collective-permute-start.16) | collective-permute-done | bytes 640032 | tf_op jit(solution)/shard_map/ppermute | solution.py:235
  363.8 7.9 %shard_map.52 = (f32[8,40000]{1,0:T(8,128)}, f32[8,40000]{1,0:T(8,128)}, f32[8,40000]{1,0:T(8,128)}, f32[8,40000]{1,0:T(8,128)}) custom-call(s32[1]{0:T(128)} %bitcast.me_ref.refs_0_.row_ref, s32[1]{0:T(128)} %bitcast.1.me_ref.refs_0_, f32[8,20000]{1,0:T(8,128)} %get-tuple-element.137.refs_0_, f32[8,20000]{1,0:T(8,128)} %copy-done.8, f32[8,20000]{1,0:T(8,128)} %copy-done.9, ...), custom_call_target="tpu_custom_call" | custom-call | bytes 10240000 | tf_op jit(solution)/shard_map/pallas_call | solution.py:35
  371.8 1.6 collective-permute-start.24
  373.3 1.2 collective-permute-start.25
  374.5 12.1 %collective-permute-start.17 = (f32[8,20000]{1,0:T(8,128)}, f32[8,20000]{1,0:T(8,128)S(1)}, u32[]{:S(2)}, u32[]{:S(2)}) collective-permute-start(f32[8,20000]{1,0:T(8,128)} %get-tuple-element.129), channel_id=1, source_target_pairs={{0,4},{4,8},{8,12},{12,16},{16,20},{20,24},{24,28},{28,0},{1,5},{5... | collective-permute-start | bytes 1920008 | tf_op jit(solution)/shard_map/ppermute | solution.py:235
  386.6 19.7 %collective-permute-start.18 = (f32[8,20000]{1,0:T(8,128)}, f32[8,20000]{1,0:T(8,128)S(1)}, u32[]{:S(2)}, u32[]{:S(2)}) collective-permute-start(f32[8,20000]{1,0:T(8,128)} %get-tuple-element.130), channel_id=1, source_target_pairs={{0,8},{4,12},{8,16},{12,20},{16,24},{20,28},{24,0},{28,4},{1,9},{5... | collective-permute-start | bytes 1920008 | tf_op jit(solution)/shard_map/ppermute | solution.py:235
  406.3 26.2 %collective-permute-start.19 = (f32[8,20000]{1,0:T(8,128)S(1)}, f32[8,20000]{1,0:T(8,128)S(1)}, u32[]{:S(2)}, u32[]{:S(2)}) collective-permute-start(f32[8,20000]{1,0:T(8,128)S(1)} %copy-done.19), channel_id=1, source_target_pairs={{0,12},{4,16},{8,20},{12,24},{16,28},{20,0},{24,4},{28,8},{1,13},{... | collective-permute-start | bytes 1920008 | tf_op jit(solution)/shard_map/ppermute | solution.py:235
  432.5 30.1 %collective-permute-start.20 = (f32[8,20000]{1,0:T(8,128)}, f32[8,20000]{1,0:T(8,128)}, u32[]{:S(2)}, u32[]{:S(2)}) collective-permute-start(f32[8,20000]{1,0:T(8,128)} %get-tuple-element.132), channel_id=1, source_target_pairs={{0,16},{4,20},{8,24},{12,28},{16,0},{20,4},{24,8},{28,12},{1,17},{... | collective-permute-start | bytes 1920008 | tf_op jit(solution)/shard_map/ppermute | solution.py:235
  462.6 1.4 collective-permute-start.21
  464.1 30.9 %shard_map.53 = (f32[8,40000]{1,0:T(8,128)}, f32[8,40000]{1,0:T(8,128)}, f32[8,40000]{1,0:T(8,128)}, f32[8,40000]{1,0:T(8,128)}) custom-call(s32[1]{0:T(128)} %bitcast.1.me_ref.refs_0_, f32[4,200,1600]{2,1,0:T(8,128)} %shard_map.50.refs_1_, f32[8,40000]{1,0:T(8,128)} %get-tuple-element.145.refs_2_, f32[8,40000]{1,0:T(8,128)} %collective-permute-done.24.refs_3_, ...), custom_call_target="tpu_custom_call" | custom-call | flops 9093120000 | bytes 28467200 | tf_op jit(solution)/shard_map/pallas_call | solution.py:35
  495.0 0.8 copy-done.3
  496.0 0.9 copy-done.4
  497.2 0.9 copy-done.5
  498.1 0.7 collective-permute-start.29
  498.8 2.8 collective-permute-start.22
  501.6 28.7 %collective-permute-start.23 = (f32[8,20000]{1,0:T(8,128)}, f32[8,20000]{1,0:T(8,128)S(1)}, u32[]{:S(2)}, u32[]{:S(2)}) collective-permute-start(f32[8,20000]{1,0:T(8,128)} %get-tuple-element.135), channel_id=1, source_target_pairs={{0,28},{4,0},{8,4},{12,8},{16,12},{20,16},{24,20},{28,24},{1,29},{... | collective-permute-start | bytes 1920008 | tf_op jit(solution)/shard_map/ppermute | solution.py:235
  530.3 7.7 %collective-permute-done.23.refs_7_ = f32[8,20000]{1,0:T(8,128)S(1)} collective-permute-done((f32[8,20000]{1,0:T(8,128)}, f32[8,20000]{1,0:T(8,128)S(1)}, u32[]{:S(2)}, u32[]{:S(2)}) %collective-permute-start.23) | collective-permute-done | bytes 640032 | tf_op jit(solution)/shard_map/ppermute | solution.py:235
  538.0 11.6 %collective-permute-done.28.refs_10_ = f32[8,40000]{1,0:T(8,128)S(1)} collective-permute-done((f32[8,40000]{1,0:T(8,128)}, f32[8,40000]{1,0:T(8,128)S(1)}, u32[]{:S(2)}, u32[]{:S(2)}) %collective-permute-start.28) | collective-permute-done | bytes 1280032 | tf_op jit(solution)/shard_map/ppermute | solution.py:235
  549.6 2.8 collective-permute-done.29.refs_11_
  552.4 1.1 copy-done.2
  553.5 14.7 %shard_map.54 = f32[800,1600]{1,0:T(8,128)} custom-call(s32[1]{0:T(128)} %bitcast.me_ref.refs_0_.row_ref, s32[1]{0:T(128)} %bitcast.1.me_ref.refs_0_, f32[800,1600]{1,0:T(8,128)} %x_ref.3, f32[8,20000]{1,0:T(8,128)} %get-tuple-element.128.refs_0_, f32[8,20000]{1,0:T(8,128)} %copy-done.3, f32[8,20000]{1,0:T(8,128)} %copy-done.4, f32[8,20000]{1,0:T(8,128)} %copy-done.5, ...), custom_call_target="tpu_custom_call" | custom-call | bytes 20480000 | tf_op jit(solution)/shard_map/pallas_call | solution.py:35
  (93 shorter events, 4.8 us)
Async XLA Ops:
  6.5 120.2 %all-gather.4.cloned.1.call-start = ((), (), s32[]{:S(2)}) async-start(), calls=%async_computation | async-start | bytes 3686400 | tf_op jit(solution)/shard_map/all_gather | solution.py:261
  6.5 10.5 %copy-start.14 = (f32[10,20,512]{2,1,0:T(8,128)S(1)}, f32[10,20,512]{2,1,0:T(8,128)}, u32[]{:S(2)}) copy-start(f32[10,20,512]{2,1,0:T(8,128)} %param.6) | copy-start | bytes 1228804
  17.9 213.0 %all-gather.6.cloned.1.call-start = ((), (), s32[]{:S(2)}) async-start(), calls=%async_computation.1 | async-start | bytes 16384000 | tf_op jit(solution)/shard_map/all_gather | solution.py:265
  18.3 22.7 %collective-permute-start = (f32[8,20000]{1,0:T(8,128)S(1)}, f32[8,20000]{1,0:T(8,128)S(1)}, u32[]{:S(2)}, u32[]{:S(2)}) collective-permute-start(f32[8,20000]{1,0:T(8,128)S(1)} %copy-done.29), channel_id=1, source_target_pairs={{0,4},{4,8},{8,12},{12,16},{16,20},{20,24},{24,28},{28,0},{1,5},{5... | collective-permute-start | bytes 1920008 | tf_op jit(solution)/shard_map/ppermute | solution.py:235
  20.3 21.2 %collective-permute-start.1 = (f32[8,20000]{1,0:T(8,128)S(1)}, f32[8,20000]{1,0:T(8,128)S(1)}, u32[]{:S(2)}, u32[]{:S(2)}) collective-permute-start(f32[8,20000]{1,0:T(8,128)S(1)} %copy-done.28), channel_id=1, source_target_pairs={{0,8},{4,12},{8,16},{12,20},{16,24},{20,28},{24,0},{28,4},{1,9},{5... | collective-permute-start | bytes 1920008 | tf_op jit(solution)/shard_map/ppermute | solution.py:235
  21.6 19.4 %copy-start.25 = (f32[8,20000]{1,0:T(8,128)S(1)}, f32[8,20000]{1,0:T(8,128)}, u32[]{:S(2)}) copy-start(f32[8,20000]{1,0:T(8,128)} %get-tuple-element.84) | copy-start | bytes 1920004
  21.6 19.9 %copy-start.24 = (f32[8,20000]{1,0:T(8,128)S(1)}, f32[8,20000]{1,0:T(8,128)}, u32[]{:S(2)}) copy-start(f32[8,20000]{1,0:T(8,128)} %get-tuple-element.85) | copy-start | bytes 1920004
  28.7 97.9 %collective-permute-start.4 = (f32[8,40000]{1,0:T(8,128)}, f32[8,40000]{1,0:T(8,128)}, u32[]{:S(2)}, u32[]{:S(2)}) collective-permute-start(f32[8,40000]{1,0:T(8,128)} %get-tuple-element.88), channel_id=1, source_target_pairs={{0,1},{1,2},{2,3},{3,0},{4,5},{5,6},{6,7},{7,4},{8,9},{9,10},{10,1... | collective-permute-start | bytes 3840008 | tf_op jit(solution)/shard_map/ppermute | solution.py:235
  31.0 95.6 %collective-permute-start.5 = (f32[8,40000]{1,0:T(8,128)}, f32[8,40000]{1,0:T(8,128)}, u32[]{:S(2)}, u32[]{:S(2)}) collective-permute-start(f32[8,40000]{1,0:T(8,128)} %get-tuple-element.89), channel_id=1, source_target_pairs={{0,2},{1,3},{2,0},{3,1},{4,6},{5,7},{6,4},{7,5},{8,10},{9,11},{10,... | collective-permute-start | bytes 3840008 | tf_op jit(solution)/shard_map/ppermute | solution.py:235
  31.3 95.3 %collective-permute-start.6 = (f32[8,40000]{1,0:T(8,128)}, f32[8,40000]{1,0:T(8,128)}, u32[]{:S(2)}, u32[]{:S(2)}) collective-permute-start(f32[8,40000]{1,0:T(8,128)} %get-tuple-element.90), channel_id=1, source_target_pairs={{0,3},{1,0},{2,1},{3,2},{4,7},{5,4},{6,5},{7,6},{8,11},{9,8},{10,9... | collective-permute-start | bytes 3840008 | tf_op jit(solution)/shard_map/ppermute | solution.py:235
  41.0 86.5 %copy-start.17 = (f32[8,20000]{1,0:T(8,128)}, f32[8,20000]{1,0:T(8,128)S(1)}, u32[]{:S(2)}) copy-start(f32[8,20000]{1,0:T(8,128)S(1)} %collective-permute-done.refs_2_) | copy-start | bytes 1920004
  41.0 85.6 %collective-permute-start.2 = (f32[8,20000]{1,0:T(8,128)S(1)}, f32[8,20000]{1,0:T(8,128)S(1)}, u32[]{:S(2)}, u32[]{:S(2)}) collective-permute-start(f32[8,20000]{1,0:T(8,128)S(1)} %copy-done.25), channel_id=1, source_target_pairs={{0,12},{4,16},{8,20},{12,24},{16,28},{20,0},{24,4},{28,8},{1,13},{... | collective-permute-start | bytes 1920008 | tf_op jit(solution)/shard_map/ppermute | solution.py:235
  41.5 85.9 %copy-start.20 = (f32[8,20000]{1,0:T(8,128)}, f32[8,20000]{1,0:T(8,128)S(1)}, u32[]{:S(2)}) copy-start(f32[8,20000]{1,0:T(8,128)S(1)} %collective-permute-done.1.refs_3_) | copy-start | bytes 1920004
  41.5 85.0 %collective-permute-start.3 = (f32[8,20000]{1,0:T(8,128)S(1)}, f32[8,20000]{1,0:T(8,128)}, u32[]{:S(2)}, u32[]{:S(2)}) collective-permute-start(f32[8,20000]{1,0:T(8,128)S(1)} %copy-done.24), channel_id=1, source_target_pairs={{0,16},{4,20},{8,24},{12,28},{16,0},{20,4},{24,8},{28,12},{1,17},{... | collective-permute-start | bytes 1920008 | tf_op jit(solution)/shard_map/ppermute | solution.py:235
  127.4 19.4 %copy-start.21 = (f32[8,20000]{1,0:T(8,128)S(1)}, f32[8,20000]{1,0:T(8,128)}, u32[]{:S(2)}) copy-start(f32[8,20000]{1,0:T(8,128)} %get-tuple-element.97) | copy-start | bytes 1920004
  127.4 20.1 %copy-start.18 = (f32[8,20000]{1,0:T(8,128)S(1)}, f32[8,20000]{1,0:T(8,128)}, u32[]{:S(2)}) copy-start(f32[8,20000]{1,0:T(8,128)} %get-tuple-element.98) | copy-start | bytes 1920004
  127.4 21.3 %copy-start.15 = (f32[80,80]{1,0:T(8,128)S(1)}, f32[80,80]{1,0:T(8,128)}, u32[]{:S(2)}) copy-start(f32[80,80]{1,0:T(8,128)} %param.5) | copy-start | bytes 76804
  127.4 21.4 %copy-start.16 = (f32[512]{0:T(512)S(1)}, f32[512]{0:T(512)}, u32[]{:S(2)}) copy-start(f32[512]{0:T(512)} %param.7) | copy-start | bytes 6148
  128.5 115.4 %collective-permute-start.7 = (f32[8,20000]{1,0:T(8,128)S(1)}, f32[8,20000]{1,0:T(8,128)S(1)}, u32[]{:S(2)}, u32[]{:S(2)}) collective-permute-start(f32[8,20000]{1,0:T(8,128)S(1)} %copy-done.22), channel_id=1, source_target_pairs={{0,20},{4,24},{8,28},{12,0},{16,4},{20,8},{24,12},{28,16},{1,21},{... | collective-permute-start | bytes 1920008 | tf_op jit(solution)/shard_map/ppermute | solution.py:235
  146.9 97.1 %collective-permute-start.8 = (f32[8,20000]{1,0:T(8,128)S(1)}, f32[8,20000]{1,0:T(8,128)S(1)}, u32[]{:S(2)}, u32[]{:S(2)}) collective-permute-start(f32[8,20000]{1,0:T(8,128)S(1)} %copy-done.21), channel_id=1, source_target_pairs={{0,24},{4,28},{8,0},{12,4},{16,8},{20,12},{24,16},{28,20},{1,25},{... | collective-permute-start | bytes 1920008 | tf_op jit(solution)/shard_map/ppermute | solution.py:235
  147.5 96.4 %collective-permute-start.9 = (f32[8,20000]{1,0:T(8,128)S(1)}, f32[8,20000]{1,0:T(8,128)}, u32[]{:S(2)}, u32[]{:S(2)}) collective-permute-start(f32[8,20000]{1,0:T(8,128)S(1)} %copy-done.18), channel_id=1, source_target_pairs={{0,28},{4,0},{8,4},{12,8},{16,12},{20,16},{24,20},{28,24},{1,29},{... | collective-permute-start | bytes 1920008 | tf_op jit(solution)/shard_map/ppermute | solution.py:235
  278.7 38.9 %collective-permute-start.10 = (f32[8,20000]{1,0:T(8,128)}, f32[8,20000]{1,0:T(8,128)S(1)}, u32[]{:S(2)}, u32[]{:S(2)}) collective-permute-start(f32[8,20000]{1,0:T(8,128)} %get-tuple-element.103), channel_id=1, source_target_pairs={{0,4},{4,8},{8,12},{12,16},{16,20},{20,24},{24,28},{28,0},{1,5},{5... | collective-permute-start | bytes 1920008 | tf_op jit(solution)/shard_map/ppermute | solution.py:235
  279.9 38.9 %collective-permute-start.11 = (f32[8,20000]{1,0:T(8,128)}, f32[8,20000]{1,0:T(8,128)S(1)}, u32[]{:S(2)}, u32[]{:S(2)}) collective-permute-start(f32[8,20000]{1,0:T(8,128)} %get-tuple-element.104), channel_id=1, source_target_pairs={{0,8},{4,12},{8,16},{12,20},{16,24},{20,28},{24,0},{28,4},{1,9},{5... | collective-permute-start | bytes 1920008 | tf_op jit(solution)/shard_map/ppermute | solution.py:235
  281.2 71.9 %collective-permute-start.12 = (f32[8,20000]{1,0:T(8,128)}, f32[8,20000]{1,0:T(8,128)S(1)}, u32[]{:S(2)}, u32[]{:S(2)}) collective-permute-start(f32[8,20000]{1,0:T(8,128)} %get-tuple-element.105), channel_id=1, source_target_pairs={{0,12},{4,16},{8,20},{12,24},{16,28},{20,0},{24,4},{28,8},{1,13},{... | collective-permute-start | bytes 1920008 | tf_op jit(solution)/shard_map/ppermute | solution.py:235
  283.4 70.2 %collective-permute-start.13 = (f32[8,20000]{1,0:T(8,128)}, f32[8,20000]{1,0:T(8,128)S(1)}, u32[]{:S(2)}, u32[]{:S(2)}) collective-permute-start(f32[8,20000]{1,0:T(8,128)} %get-tuple-element.106), channel_id=1, source_target_pairs={{0,16},{4,20},{8,24},{12,28},{16,0},{20,4},{24,8},{28,12},{1,17},{... | collective-permute-start | bytes 1920008 | tf_op jit(solution)/shard_map/ppermute | solution.py:235
  284.5 69.1 %collective-permute-start.14 = (f32[8,20000]{1,0:T(8,128)}, f32[8,20000]{1,0:T(8,128)S(1)}, u32[]{:S(2)}, u32[]{:S(2)}) collective-permute-start(f32[8,20000]{1,0:T(8,128)} %get-tuple-element.107), channel_id=1, source_target_pairs={{0,20},{4,24},{8,28},{12,0},{16,4},{20,8},{24,12},{28,16},{1,21},{... | collective-permute-start | bytes 1920008 | tf_op jit(solution)/shard_map/ppermute | solution.py:235
  317.6 30.6 %copy-start.8 = (f32[8,20000]{1,0:T(8,128)}, f32[8,20000]{1,0:T(8,128)S(1)}, u32[]{:S(2)}) copy-start(f32[8,20000]{1,0:T(8,128)S(1)} %collective-permute-done.10.refs_1_) | copy-start | bytes 1920004
  317.6 36.0 %collective-permute-start.15 = (f32[8,20000]{1,0:T(8,128)}, f32[8,20000]{1,0:T(8,128)S(1)}, u32[]{:S(2)}, u32[]{:S(2)}) collective-permute-start(f32[8,20000]{1,0:T(8,128)} %get-tuple-element.108), channel_id=1, source_target_pairs={{0,24},{4,28},{8,0},{12,4},{16,8},{20,12},{24,16},{28,20},{1,25},{... | collective-permute-start | bytes 1920008 | tf_op jit(solution)/shard_map/ppermute | solution.py:235
  318.8 29.4 %copy-start.9 = (f32[8,20000]{1,0:T(8,128)}, f32[8,20000]{1,0:T(8,128)S(1)}, u32[]{:S(2)}) copy-start(f32[8,20000]{1,0:T(8,128)S(1)} %collective-permute-done.11.refs_2_) | copy-start | bytes 1920004
  318.8 45.0 %collective-permute-start.16 = (f32[8,20000]{1,0:T(8,128)}, f32[8,20000]{1,0:T(8,128)}, u32[]{:S(2)}, u32[]{:S(2)}) collective-permute-start(f32[8,20000]{1,0:T(8,128)} %get-tuple-element.109), channel_id=1, source_target_pairs={{0,28},{4,0},{8,4},{12,8},{16,12},{20,16},{24,20},{28,24},{1,29},{... | collective-permute-start | bytes 1920008 | tf_op jit(solution)/shard_map/ppermute | solution.py:235
  353.1 10.7 %copy-start.10 = (f32[8,20000]{1,0:T(8,128)}, f32[8,20000]{1,0:T(8,128)S(1)}, u32[]{:S(2)}) copy-start(f32[8,20000]{1,0:T(8,128)S(1)} %collective-permute-done.12.refs_3_) | copy-start | bytes 1920004
  363.8 42.5 %copy-start.19 = (f32[8,20000]{1,0:T(8,128)S(1)}, f32[8,20000]{1,0:T(8,128)}, u32[]{:S(2)}) copy-start(f32[8,20000]{1,0:T(8,128)} %get-tuple-element.131) | copy-start | bytes 1920004
  371.8 34.5 %collective-permute-start.24 = (f32[8,40000]{1,0:T(8,128)}, f32[8,40000]{1,0:T(8,128)}, u32[]{:S(2)}, u32[]{:S(2)}) collective-permute-start(f32[8,40000]{1,0:T(8,128)} %get-tuple-element.146), channel_id=1, source_target_pairs={{0,1},{1,2},{2,3},{3,0},{4,5},{5,6},{6,7},{7,4},{8,9},{9,10},{10,1... | collective-permute-start | bytes 3840008 | tf_op jit(solution)/shard_map/ppermute | solution.py:235
  373.3 59.2 %collective-permute-start.25 = (f32[8,40000]{1,0:T(8,128)}, f32[8,40000]{1,0:T(8,128)}, u32[]{:S(2)}, u32[]{:S(2)}) collective-permute-start(f32[8,40000]{1,0:T(8,128)} %get-tuple-element.147), channel_id=1, source_target_pairs={{0,2},{1,3},{2,0},{3,1},{4,6},{5,7},{6,4},{7,5},{8,10},{9,11},{10,... | collective-permute-start | bytes 3840008 | tf_op jit(solution)/shard_map/ppermute | solution.py:235
  374.5 88.2 %collective-permute-start.26 = (f32[8,40000]{1,0:T(8,128)}, f32[8,40000]{1,0:T(8,128)}, u32[]{:S(2)}, u32[]{:S(2)}) collective-permute-start(f32[8,40000]{1,0:T(8,128)} %get-tuple-element.148), channel_id=1, source_target_pairs={{0,3},{1,0},{2,1},{3,2},{4,7},{5,4},{6,5},{7,6},{8,11},{9,8},{10,9... | collective-permute-start | bytes 3840008 | tf_op jit(solution)/shard_map/ppermute | solution.py:235
  374.5 120.5 %collective-permute-start.17 = (f32[8,20000]{1,0:T(8,128)}, f32[8,20000]{1,0:T(8,128)S(1)}, u32[]{:S(2)}, u32[]{:S(2)}) collective-permute-start(f32[8,20000]{1,0:T(8,128)} %get-tuple-element.129), channel_id=1, source_target_pairs={{0,4},{4,8},{8,12},{12,16},{16,20},{20,24},{24,28},{28,0},{1,5},{5... | collective-permute-start | bytes 1920008 | tf_op jit(solution)/shard_map/ppermute | solution.py:235
  386.6 109.4 %collective-permute-start.18 = (f32[8,20000]{1,0:T(8,128)}, f32[8,20000]{1,0:T(8,128)S(1)}, u32[]{:S(2)}, u32[]{:S(2)}) collective-permute-start(f32[8,20000]{1,0:T(8,128)} %get-tuple-element.130), channel_id=1, source_target_pairs={{0,8},{4,12},{8,16},{12,20},{16,24},{20,28},{24,0},{28,4},{1,9},{5... | collective-permute-start | bytes 1920008 | tf_op jit(solution)/shard_map/ppermute | solution.py:235
  406.3 90.9 %collective-permute-start.19 = (f32[8,20000]{1,0:T(8,128)S(1)}, f32[8,20000]{1,0:T(8,128)S(1)}, u32[]{:S(2)}, u32[]{:S(2)}) collective-permute-start(f32[8,20000]{1,0:T(8,128)S(1)} %copy-done.19), channel_id=1, source_target_pairs={{0,12},{4,16},{8,20},{12,24},{16,28},{20,0},{24,4},{28,8},{1,13},{... | collective-permute-start | bytes 1920008 | tf_op jit(solution)/shard_map/ppermute | solution.py:235
  432.5 66.2 %collective-permute-start.20 = (f32[8,20000]{1,0:T(8,128)}, f32[8,20000]{1,0:T(8,128)}, u32[]{:S(2)}, u32[]{:S(2)}) collective-permute-start(f32[8,20000]{1,0:T(8,128)} %get-tuple-element.132), channel_id=1, source_target_pairs={{0,16},{4,20},{8,24},{12,28},{16,0},{20,4},{24,8},{28,12},{1,17},{... | collective-permute-start | bytes 1920008 | tf_op jit(solution)/shard_map/ppermute | solution.py:235
  462.6 39.0 %collective-permute-start.21 = (f32[8,20000]{1,0:T(8,128)}, f32[8,20000]{1,0:T(8,128)}, u32[]{:S(2)}, u32[]{:S(2)}) collective-permute-start(f32[8,20000]{1,0:T(8,128)} %get-tuple-element.133), channel_id=1, source_target_pairs={{0,20},{4,24},{8,28},{12,0},{16,4},{20,8},{24,12},{28,16},{1,21},{... | collective-permute-start | bytes 1920008 | tf_op jit(solution)/shard_map/ppermute | solution.py:235
  495.9 42.2 %collective-permute-start.27 = (f32[8,40000]{1,0:T(8,128)}, f32[8,40000]{1,0:T(8,128)S(1)}, u32[]{:S(2)}, u32[]{:S(2)}) collective-permute-start(f32[8,40000]{1,0:T(8,128)} %get-tuple-element.150), channel_id=1, source_target_pairs={{0,1},{1,2},{2,3},{3,0},{4,5},{5,6},{6,7},{7,4},{8,9},{9,10},{10,1... | collective-permute-start | bytes 3840008 | tf_op jit(solution)/shard_map/ppermute | solution.py:235
  496.9 52.7 %collective-permute-start.28 = (f32[8,40000]{1,0:T(8,128)}, f32[8,40000]{1,0:T(8,128)S(1)}, u32[]{:S(2)}, u32[]{:S(2)}) collective-permute-start(f32[8,40000]{1,0:T(8,128)} %get-tuple-element.151), channel_id=1, source_target_pairs={{0,2},{1,3},{2,0},{3,1},{4,6},{5,7},{6,4},{7,5},{8,10},{9,11},{10,... | collective-permute-start | bytes 3840008 | tf_op jit(solution)/shard_map/ppermute | solution.py:235
  498.1 54.3 %collective-permute-start.29 = (f32[8,40000]{1,0:T(8,128)}, f32[8,40000]{1,0:T(8,128)S(1)}, u32[]{:S(2)}, u32[]{:S(2)}) collective-permute-start(f32[8,40000]{1,0:T(8,128)} %get-tuple-element.152), channel_id=1, source_target_pairs={{0,3},{1,0},{2,1},{3,2},{4,7},{5,4},{6,5},{7,6},{8,11},{9,8},{10,9... | collective-permute-start | bytes 3840008 | tf_op jit(solution)/shard_map/ppermute | solution.py:235
  498.8 31.5 %collective-permute-start.22 = (f32[8,20000]{1,0:T(8,128)}, f32[8,20000]{1,0:T(8,128)S(1)}, u32[]{:S(2)}, u32[]{:S(2)}) collective-permute-start(f32[8,20000]{1,0:T(8,128)} %get-tuple-element.134), channel_id=1, source_target_pairs={{0,24},{4,28},{8,0},{12,4},{16,8},{20,12},{24,16},{28,20},{1,25},{... | collective-permute-start | bytes 1920008 | tf_op jit(solution)/shard_map/ppermute | solution.py:235
  501.6 36.4 %collective-permute-start.23 = (f32[8,20000]{1,0:T(8,128)}, f32[8,20000]{1,0:T(8,128)S(1)}, u32[]{:S(2)}, u32[]{:S(2)}) collective-permute-start(f32[8,20000]{1,0:T(8,128)} %get-tuple-element.135), channel_id=1, source_target_pairs={{0,28},{4,0},{8,4},{12,8},{16,12},{20,16},{24,20},{28,24},{1,29},{... | collective-permute-start | bytes 1920008 | tf_op jit(solution)/shard_map/ppermute | solution.py:235
  530.3 22.1 %copy-start.6 = (f32[8,20000]{1,0:T(8,128)}, f32[8,20000]{1,0:T(8,128)S(1)}, u32[]{:S(2)}) copy-start(f32[8,20000]{1,0:T(8,128)S(1)} %collective-permute-done.22.refs_6_) | copy-start | bytes 1920004
  538.0 14.4 %copy-start.7 = (f32[8,20000]{1,0:T(8,128)}, f32[8,20000]{1,0:T(8,128)S(1)}, u32[]{:S(2)}) copy-start(f32[8,20000]{1,0:T(8,128)S(1)} %collective-permute-done.23.refs_7_) | copy-start | bytes 1920004
  538.0 14.4 %copy-start = (f32[8,40000]{1,0:T(8,128)}, f32[8,40000]{1,0:T(8,128)S(1)}, u32[]{:S(2)}) copy-start(f32[8,40000]{1,0:T(8,128)S(1)} %collective-permute-done.27.refs_9_) | copy-start | bytes 3840004
  (14 other events, 45.5 us)
Sparse Core Ops, SparseCore 0:
  18.0 108.7 all-gather.3
  128.3 102.4 all-gather.5

commit v2 on v1

--- a/solution.py
+++ b/solution.py
@@ -60,22 +60,26 @@
     return jax.ShapeDtypeStruct((batch // g, g * width), f32)
 
 
+def fold(stage, b, out_ref):
+    width, rows = stage.shape[2], out_ref.shape[0]
+    parts = [stage[b, g * rows : (g + 1) * rows, :] for g in range(out_ref.shape[1] // width)]
+    out_ref[...] = jnp.concatenate(parts, axis=1) if len(parts) > 1 else parts[0]
+
+
+def unfold(in_ref, stage, b):
+    width, rows = stage.shape[2], in_ref.shape[0]
+    for g in range(in_ref.shape[1] // width):
+        stage[b, g * rows : (g + 1) * rows, :] = in_ref[:, g * width : (g + 1) * width]
+
+
 def hand_out(me_ref, stage, outs):
-    width = stage.shape[2]
     for s, out_ref in enumerate(outs):
-        b, rows = lax.rem(me_ref[0] + s, len(outs)), out_ref.shape[0]
-        parts = [
-            stage[b, g * rows : (g + 1) * rows, :] for g in range(out_ref.shape[1] // width)
-        ]
-        out_ref[...] = jnp.concatenate(parts, axis=1) if len(parts) > 1 else parts[0]
+        fold(stage, lax.rem(me_ref[0] + s, len(outs)), out_ref)
 
 
 def take_in(me_ref, ins, stage):
-    width = stage.shape[2]
     for s, in_ref in enumerate(ins):
-        b, rows = lax.rem(me_ref[0] + len(ins) - s, len(ins)), in_ref.shape[0]
-        for g in range(in_ref.shape[1] // width):
-            stage[b, g * rows : (g + 1) * rows, :] = in_ref[:, g * width : (g + 1) * width]
+        unfold(in_ref, stage, lax.rem(me_ref[0] + len(ins) - s, len(ins)))
 
 
 def rows_of(stage, span):
@@ -119,9 +123,10 @@
     hand_out(me_ref, stage, outs)
 
 
-def finish_body(n, count, row_ref, me_ref, x_ref, *refs):
-    crossed, (*ins, out_ref, arrived, stage, total) = refs[:count], refs[count:]
-    take_in(row_ref, crossed, arrived)
+def finish_body(n, me_ref, x_ref, crossed_ref, *refs):
+    *ins, out_ref, arrived, stage, total = refs
+    for b in range(arrived.shape[0]):
+        unfold(crossed_ref.at[b], arrived, b)
     take_in(me_ref, ins, stage)
     for strip in tiles(total.shape[0]):
         turned = jnp.concatenate([stage[b, :, strip] for b in range(len(ins))], axis=0)
@@ -131,13 +136,22 @@
         out_ref[i, :] = x_ref[i, :] + jnp.concatenate([total[k, i] for k in cols], axis=1)
 
 
-def split_body(n, x_ref, high_ref, low_ref):
-    wide = x_ref.shape[1] * x_ref.shape[0] // n
-    each = n // x_ref.shape[0]
-    for p in range(wide):
-        parts = [x_ref[c, p * each : (p + 1) * each, :] for c in range(x_ref.shape[0])]
-        rows = slice(p * n, (p + 1) * n)
-        high_ref[rows, :], low_ref[rows, :] = halves(jnp.concatenate(parts, axis=0))
+def split_body(n, places, row_ref, col_ref, *refs):
+    *ins, high_ref, low_ref, stage = refs
+    cols, rows, each, _ = stage.shape
+    pieces = len(ins) // cols
+    for index, in_ref in enumerate(ins):
+        c = lax.bitwise_xor(col_ref[0], places[index // pieces])
+        for u in range(rows // pieces):
+            s = index % pieces * (rows // pieces) + u
+            r = lax.rem(row_ref[0] + rows - s, rows)
+            stage[c, r] = in_ref[u]
+    wide = n // cols
+    for p in range(n):
+        r, at = p * wide // each, p * wide % each
+        parts = [stage[c, r, at : at + wide, :] for c in range(cols)]
+        span = slice(p * n, (p + 1) * n)
+        high_ref[span, :], low_ref[span, :] = halves(jnp.concatenate(parts, axis=0))
 
 
 def take(ref, rows, batch):
@@ -198,11 +212,11 @@
     lax.fori_loop(0, blocks, result, 0)
 
 
-def leaving_body(n, keep, scale, count, me_ref, x_ref, *refs):
-    *consts, stage, xp, zp = refs
-    consts, outs = consts[:-count], consts[-count:]
+def leaving_body(n, keep, scale, x_ref, *refs):
+    *consts, out_ref, stage, xp, zp = refs
     apply_operator(n, keep, scale, x_ref, stage, *consts, xp, zp)
-    hand_out(me_ref, stage, outs)
+    for b in range(stage.shape[0]):
+        fold(stage, b, out_ref.at[b])
 
 
 def arriving_body(n, keep, scale, count, me_ref, *refs):
@@ -236,6 +250,10 @@
     ]
 
 
+def swap(x, axis, n, bit):
+    return lax.ppermute(x, axis, [(d, d ^ bit) for d in range(n)])
+
+
 def shards(rows, cols, pairs, one_body, aux, weights):
     n = one_body.shape[0]
     naux = aux.shape[2]
@@ -255,27 +273,31 @@
         [jax.ShapeDtypeStruct((local_cols, local_rows), f32), *row_wires],
         [row_me, pairs], [row_stage], moved=12 * size,
     )
+
+    vectors = shift([aux.reshape(-1, naux)] * rows, "row")
+    mine = shift(mine, "row")
+    early = rows // 2
+    near, far = jnp.stack(vectors[:early]), vectors[early:]
+    far, mine[1:early] = lax.optimization_barrier((far, mine[1:early]))
+    held = {0: [near, jnp.stack(far)]}
+    bit = cols // 2
+    while bit:
+        for t in list(held):
+            held[t ^ bit] = [swap(x, "col", cols, bit) for x in held[t]]
+        if bit == cols // 2:
+            crossed, held[bit] = lax.optimization_barrier((crossed, held[bit]))
+        bit //= 2
     theirs = call(turn_body, col_wires, [col_me, crossed], [col_stage], moved=8 * size)
-
-    mine[0], aux = lax.optimization_barrier((mine[0], aux))
-    whole = lax.all_gather(aux.reshape(-1, naux), "row", axis=0, tiled=True)
-    mine, theirs = shift(mine, "row"), shift(theirs, "col")
-    early = rows // 2 + 1
-    whole, mine[:early], theirs = lax.optimization_barrier((whole, mine[:early], theirs))
-    whole = lax.all_gather(whole, "col", axis=0, tiled=False)
-    group = 8 if n % 8 == 0 else n
+    theirs = shift(theirs, "col")
+    places = list(held)
     shape = jax.ShapeDtypeStruct((n * n, naux), bf16)
-    high, low = pl.pallas_call(
-        functools.partial(split_body, n),
-        grid=(n // group,),
-        in_specs=[pl.BlockSpec((cols, group * n // cols, naux), lambda s: (0, s, 0))],
-        out_specs=[pl.BlockSpec((group * n, naux), lambda s: (s, 0))] * 2,
-        out_shape=[shape, shape],
-        compiler_params=pltpu.CompilerParams(vmem_limit_bytes=vmem_limit),
-        cost_estimate=pl.CostEstimate(
-            flops=2 * n * n * naux, bytes_accessed=8 * n * n * naux, transcendentals=0
-        ),
-    )(whole)
+    high, low = call(
+        functools.partial(split_body, n, places),
+        [shape, shape],
+        [row_me, col_me, *[x for t in places for x in held[t]]],
+        [pltpu.VMEM((cols, rows, n * n // cols // rows, naux), f32)],
+        flops=2 * n * n * naux, moved=8 * n * n * naux,
+    )
 
     left = tripled(one_body)
     right = tripled(-one_body.T)
@@ -304,15 +326,15 @@
     first, theirs = lax.optimization_barrier((first, theirs))
     arriving = shift(arriving, "row")
     double = operator(
-        lambda n, *refs: leaving_body(n, time_step, half_square, rows, *refs),
-        [row_me, first], row_consts, row_wires, row_block,
+        lambda n, *refs: leaving_body(n, time_step, half_square, *refs),
+        [first], row_consts, jax.ShapeDtypeStruct((rows, *row_wires[0].shape), f32), row_block,
     )
     (base,) = operator(
         lambda n, *refs: arriving_body(n, time_step, half_square, cols, *refs),
         [col_me, *theirs], col_consts, [col_shape], col_block,
     )
     arriving, base, double = lax.optimization_barrier((arriving, base, double))
-    double = shift(double, "row")
+    double = lax.all_to_all(double, "row", split_axis=0, concat_axis=0, tiled=True)
     first = call(
         functools.partial(turn_arriving_body, rows),
         col_wires, [row_me, col_me, *arriving], [row_stage, col_stage], moved=8 * size,
@@ -325,9 +347,9 @@
     last = shift(last, "col")
 
     return call(
-        functools.partial(finish_body, n, rows),
+        functools.partial(finish_body, n),
         jax.ShapeDtypeStruct(pairs.shape, f32),
-        [row_me, col_me, pairs, *double, *last],
+        [col_me, pairs, double, *last],
         [row_stage, col_stage, pltpu.VMEM((local_cols, local_rows), f32)],
         moved=16 * size,
     )

time: 585 us -> 620 us (1.060)
  waiting for transfers between devices: 208 us -> 275 us
  between operations: 14 us -> 0.5 us
  starting transfers between devices: 167 us -> 154 us
    ppermute x30, waiting for transfers between devices: 128 us -> 239 us  [shift(): lax.ppermute(parts[s], axis, [(d, (d + s) % n) for d in range(n)])]
    all_gather x2 -> x0, waiting for transfers between devices: 80.8 us -> none  [the longest x1 80.7 us: shards(): whole = lax.all_gather(whole, 'col', axis=0, tiled=False)]
    ppermute x30, starting transfers between devices: 167 us -> 115 us  [shift(): lax.ppermute(parts[s], axis, [(d, (d + s) % n) for d in range(n)])]
    ppermute x0 -> x6, waiting for transfers between devices: none -> 35.8 us  [swap(): return lax.ppermute(x, axis, [(d, d ^ bit) for d in range(n)])]
    all_to_all x0 -> x1, starting transfers between devices: none -> 32.8 us  [shards(): lax.all_to_all(double, 'row', split_axis=0, concat_axis=0, tiled=True)]
    pallas_call x1 -> x0, Pallas kernels: 13.1 us -> none  [shards(): pl.pallas_call(functools.partial(split_body, n), grid=(n // group,), in_s...]
    pallas_call x8 -> x9, Pallas kernels: 164 us -> 176 us  [call(): pl.pallas_call(body, in_specs=[smem if x.dtype == jnp.int32 else vmem for...]
  transfers between devices with their start and end apart: 32 -> 37, of which waited for: 10 -> 18; matrix products, arithmetic and copies ran while one was open for 0% -> 1% of each run, Pallas kernels for 19% -> 26%
where the time goes in v2:
time: 620 us; the launch traced here: 613 us
  waiting for transfers between devices  275 us (44%)
  Pallas kernels  176 us (28%)
  starting transfers between devices  154 us (25%)
    ppermute x30, waiting for transfers between devices, shift(): lax.ppermute(parts[s], axis, [(d, (d + s) % n) for d in range(n)])  239 us
    pallas_call x9, Pallas kernels, call(): pl.pallas_call(body, in_specs=[smem if x.dtype == jnp.int32 else vmem for...  176 us
    ppermute x30, starting transfers between devices, shift(): lax.ppermute(parts[s], axis, [(d, (d + s) % n) for d in range(n)])  115 us
    ppermute x6, waiting for transfers between devices, swap(): return lax.ppermute(x, axis, [(d, d ^ bit) for d in range(n)])  35.8 us
    all_to_all x1, starting transfers between devices, shards(): lax.all_to_all(double, 'row', split_axis=0, concat_axis=0, tiled=True)  32.8 us
  transfers between devices with their start and end apart: 37, of which 18 were waited for; matrix products, arithmetic and copies ran while one was open for 1% of the time, Pallas kernels for 26%

profile of v2, /device:TPU:1, one launch (start us, length us, event | category | flops | bytes accessed | tf_op | source)
XLA Modules:
  0.0 613.3 jit_solution(8650763280042293662)
XLA Ops:
  0.0 1.9 reshape.15
  1.9 3.1 collective-permute-start.13
  5.0 1.3 collective-permute-start.12
  6.3 1.2 collective-permute-start.11
  7.5 2.9 collective-permute-start.3
  10.6 10.4 %shard_map.46 = (f32[1600,800]{1,0:T(8,128)}, f32[8,20000]{1,0:T(8,128)}, f32[8,20000]{1,0:T(8,128)}, f32[8,20000]{1,0:T(8,128)}, f32[8,20000]{1,0:T(8,128)}, /*...) custom-call(s32[1]{0:T(128)} %bitcast.1.me_ref.row_ref.refs_0_, f32[800,1600]{1,0:T(8,128)} %x_ref.3), custom_call_target="tpu_custom_call" | custom-call | bytes 15360000 | tf_op jit(solution)/shard_map/pallas_call | solution.py:35
  21.0 20.8 %collective-permute-done.13 = f32[200,512]{1,0:T(8,128)S(1)} collective-permute-done((f32[200,512]{1,0:T(8,128)}, f32[200,512]{1,0:T(8,128)S(1)}, u32[]{:S(2)}, u32[]{:S(2)}) %collective-permute-start.13) | collective-permute-done | bytes 409632 | tf_op jit(solution)/shard_map/ppermute | solution.py:249
  41.8 10.0 %collective-permute-start.6 = (f32[8,20000]{1,0:T(8,128)}, f32[8,20000]{1,0:T(8,128)}, u32[]{:S(2)}, u32[]{:S(2)}) collective-permute-start(f32[8,20000]{1,0:T(8,128)} %get-tuple-element.65), channel_id=1, source_target_pairs={{0,12},{4,16},{8,20},{12,24},{16,28},{20,0},{24,4},{28,8},{1,13},{... | collective-permute-start | bytes 1920008 | tf_op jit(solution)/shard_map/ppermute | solution.py:249
  51.8 5.1 collective-permute-start
  57.1 26.7 %collective-permute-done.1 = f32[200,512]{1,0:T(8,128)} collective-permute-done((f32[200,512]{1,0:T(8,128)}, f32[200,512]{1,0:T(8,128)}, u32[]{:S(2)}, u32[]{:S(2)}) %collective-permute-start.1) | collective-permute-done | bytes 409632 | tf_op jit(solution)/shard_map/ppermute | solution.py:249
  84.7 24.4 %collective-permute-done = f32[200,512]{1,0:T(8,128)} collective-permute-done((f32[200,512]{1,0:T(8,128)}, f32[200,512]{1,0:T(8,128)}, u32[]{:S(2)}, u32[]{:S(2)}) %collective-permute-start) | collective-permute-done | bytes 409632 | tf_op jit(solution)/shard_map/ppermute | solution.py:249
  109.2 5.4 collective-permute-done.6.refs_4_
  114.6 1.6 pad_maximum_fusion.1.refs_1_
  116.2 1.0 collective-permute-start.15
  117.1 2.9 collective-permute-start.16
  120.7 35.2 %collective-permute-done.15.refs_3_ = f32[4,200,512]{2,1,0:T(8,128)} collective-permute-done((f32[4,200,512]{2,1,0:T(8,128)S(1)}, f32[4,200,512]{2,1,0:T(8,128)}, u32[]{:S(2)}, u32[]{:S(2)}) %collective-permute-start.15) | collective-permute-done | bytes 1638432 | tf_op jit(solution)/shard_map/ppermute | solution.py:254
  155.9 1.3 collective-permute-start.18
  157.3 15.8 %collective-permute-start.7 = (f32[8,20000]{1,0:T(8,128)S(1)}, f32[8,20000]{1,0:T(8,128)S(1)}, u32[]{:S(2)}, u32[]{:S(2)}) collective-permute-start(f32[8,20000]{1,0:T(8,128)S(1)} %copy-done.23), channel_id=1, source_target_pairs={{0,16},{4,20},{8,24},{12,28},{16,0},{20,4},{24,8},{28,12},{1,17},{... | collective-permute-start | bytes 1920008 | tf_op jit(solution)/shard_map/ppermute | solution.py:249
  173.1 14.4 %collective-permute-done.7.refs_5_ = f32[8,20000]{1,0:T(8,128)S(1)} collective-permute-done((f32[8,20000]{1,0:T(8,128)S(1)}, f32[8,20000]{1,0:T(8,128)S(1)}, u32[]{:S(2)}, u32[]{:S(2)}) %collective-permute-start.7) | collective-permute-done | bytes 640032 | tf_op jit(solution)/shard_map/ppermute | solution.py:249
  187.5 25.0 %collective-permute-start.8 = (f32[8,20000]{1,0:T(8,128)S(1)}, f32[8,20000]{1,0:T(8,128)S(1)}, u32[]{:S(2)}, u32[]{:S(2)}) collective-permute-start(f32[8,20000]{1,0:T(8,128)S(1)} %copy-done.21), channel_id=1, source_target_pairs={{0,20},{4,24},{8,28},{12,0},{16,4},{20,8},{24,12},{28,16},{1,21},{... | collective-permute-start | bytes 1920008 | tf_op jit(solution)/shard_map/ppermute | solution.py:249
  212.5 12.5 %collective-permute-done.8.refs_6_ = f32[8,20000]{1,0:T(8,128)S(1)} collective-permute-done((f32[8,20000]{1,0:T(8,128)S(1)}, f32[8,20000]{1,0:T(8,128)S(1)}, u32[]{:S(2)}, u32[]{:S(2)}) %collective-permute-start.8) | collective-permute-done | bytes 640032 | tf_op jit(solution)/shard_map/ppermute | solution.py:249
  225.0 6.2 %collective-permute-start.9 = (f32[8,20000]{1,0:T(8,128)}, f32[8,20000]{1,0:T(8,128)}, u32[]{:S(2)}, u32[]{:S(2)}) collective-permute-start(f32[8,20000]{1,0:T(8,128)} %get-tuple-element.71), channel_id=1, source_target_pairs={{0,24},{4,28},{8,0},{12,4},{16,8},{20,12},{24,16},{28,20},{1,25},{... | collective-permute-start | bytes 1920008 | tf_op jit(solution)/shard_map/ppermute | solution.py:249
  231.1 1.2 copy-done.4
  232.3 27.9 %collective-permute-start.10 = (f32[8,20000]{1,0:T(8,128)}, f32[8,20000]{1,0:T(8,128)}, u32[]{:S(2)}, u32[]{:S(2)}) collective-permute-start(f32[8,20000]{1,0:T(8,128)} %get-tuple-element.72), channel_id=1, source_target_pairs={{0,28},{4,0},{8,4},{12,8},{16,12},{20,16},{24,20},{28,24},{1,29},{... | collective-permute-start | bytes 1920008 | tf_op jit(solution)/shard_map/ppermute | solution.py:249
  260.2 6.9 %shard_map.49 = (f32[8,40000]{1,0:T(8,128)}, f32[8,40000]{1,0:T(8,128)}, f32[8,40000]{1,0:T(8,128)}, f32[8,40000]{1,0:T(8,128)}) custom-call(s32[1]{0:T(128)} %bitcast.col_ref.me_ref.refs_0_, f32[1600,800]{1,0:T(8,128)} %get-tuple-element.91.x_ref), custom_call_target="tpu_custom_call" | custom-call | bytes 10240000 | tf_op jit(solution)/shard_map/pallas_call | solution.py:35
  267.1 1.8 collective-permute-start.27
  271.5 12.8 %shard_map.47 = (bf16[6400,512]{1,0:T(8,128)(2,1)}, bf16[6400,512]{1,0:T(8,128)(2,1)}) custom-call(s32[1]{0:T(128)} %bitcast.1.me_ref.row_ref.refs_0_, s32[1]{0:T(128)} %bitcast.col_ref.me_ref.refs_0_, f32[4,200,512]{2,1,0:T(8,128)} %copy-done, f32[4,200,512]{2,1,0:T(8,128)} %copy-done.1, f32[4,200,512]{2,1,0:T(8,128)} %copy-done.3, ...), custom_call_target="tpu_custom_call" | custom-call | flops 6553600 | bytes 26214400 | tf_op jit(solution)/shard_map/pallas_call | solution.py:35
  284.3 33.7 %shard_map.48 = (f32[8,200,800]{2,1,0:T(8,128)}, f32[8,20000]{1,0:T(8,128)}, f32[8,20000]{1,0:T(8,128)}, f32[8,20000]{1,0:T(8,128)}, f32[8,20000]{1,0:T(8,128)},...) custom-call(s32[1]{0:T(128)} %bitcast.1.me_ref.row_ref.refs_0_, ...), custom_call_target="tpu_custom_call" | custom-call | flops 9093120000 | bytes 28467200 | tf_op jit(solution)/shard_map/pallas_call | solution.py:35
  318.0 7.0 %collective-permute-done.28.refs_3_ = f32[8,40000]{1,0:T(8,128)S(1)} collective-permute-done((f32[8,40000]{1,0:T(8,128)}, f32[8,40000]{1,0:T(8,128)S(1)}, u32[]{:S(2)}, u32[]{:S(2)}) %collective-permute-start.28) | collective-permute-done | bytes 1280032 | tf_op jit(solution)/shard_map/ppermute | solution.py:249
  326.2 1.4 collective-permute-start.21
  327.6 4.4 collective-permute-start.23
  332.1 30.9 %shard_map.51 = f32[8,8,20000]{2,1,0:T(8,128)} custom-call(f32[8,200,800]{2,1,0:T(8,128)} %get-tuple-element.100.refs_0_, bf16[6400,512]{1,0:T(8,128)(2,1)} %get-tuple-element.80.refs_9_.refs_5_.refs_1_.refs_6_, bf16[6400,512]{1,0:T(8,128)(2,1)} %get-tuple-element.81.refs_10_.refs_6_.refs_2_.refs_7_, f32[1,512]{1,0:T(1,128)} %bitcast.20, ...), custom_call_target="tpu_custom_call" | custom-call | flops 9093120000 | bytes 28467200 | tf_op jit(solution)/shard_map/pallas_call | solution.py:35
  363.0 2.1 collective-permute-start.25
  365.1 1.3 collective-permute-start.26
  366.4 28.3 %shard_map.50.refs_1_ = f32[4,200,1600]{2,1,0:T(8,128)} custom-call(s32[1]{0:T(128)} %bitcast.col_ref.me_ref.refs_0_, f32[8,40000]{1,0:T(8,128)} %get-tuple-element.96.refs_1_, f32[8,40000]{1,0:T(8,128)} %copy-done.16, f32[8,40000]{1,0:T(8,128)} %copy-done.17, f32[8,40000]{1,0:T(8,128)} %collective-permute-done.29.refs_4_, ...), custom_call_target="tpu_custom_call" | custom-call | flops 9093120000 | bytes 28467200 | tf_op jit(solution)/shard_map/pallas_call | solution.py:35
  394.7 5.4 collective-permute-done.22.refs_3_
  400.2 10.6 %collective-permute-done.26.refs_7_ = f32[8,20000]{1,0:T(8,128)} collective-permute-done((f32[8,20000]{1,0:T(8,128)}, f32[8,20000]{1,0:T(8,128)}, u32[]{:S(2)}, u32[]{:S(2)}) %collective-permute-start.26) | collective-permute-done | bytes 640032 | tf_op jit(solution)/shard_map/ppermute | solution.py:249
  410.7 32.8 %all-to-all-start = ((f32[8,8,20000]{2,1,0:T(8,128)}), f32[8,8,20000]{2,1,0:T(8,128)}, u32[]{:S(2)}, u32[]{:S(2)}) async-start(f32[8,8,20000]{2,1,0:T(8,128)} %shard_map.51), calls=%async_computation | async-start | bytes 10289152 | tf_op jit(solution)/shard_map/all_to_all | solution.py:337
  443.5 7.8 %shard_map.52 = (f32[8,40000]{1,0:T(8,128)}, f32[8,40000]{1,0:T(8,128)}, f32[8,40000]{1,0:T(8,128)}, f32[8,40000]{1,0:T(8,128)}) custom-call(s32[1]{0:T(128)} %bitcast.1.me_ref.row_ref.refs_0_, s32[1]{0:T(128)} %bitcast.col_ref.me_ref.refs_0_, f32[8,20000]{1,0:T(8,128)} %get-tuple-element.103.refs_0_, f32[8,20000]{1,0:T(8,128)} %copy-done.7, ...), custom_call_target="tpu_custom_call" | custom-call | bytes 10240000 | tf_op jit(solution)/shard_map/pallas_call | solution.py:35
  451.4 1.1 collective-permute-start.30
  453.6 26.6 %collective-permute-done.30.refs_3_ = f32[8,40000]{1,0:T(8,128)S(1)} collective-permute-done((f32[8,40000]{1,0:T(8,128)}, f32[8,40000]{1,0:T(8,128)S(1)}, u32[]{:S(2)}, u32[]{:S(2)}) %collective-permute-start.30) | collective-permute-done | bytes 1280032 | tf_op jit(solution)/shard_map/ppermute | solution.py:249
  480.2 29.2 %collective-permute-done.31.refs_4_ = f32[8,40000]{1,0:T(8,128)S(1)} collective-permute-done((f32[8,40000]{1,0:T(8,128)}, f32[8,40000]{1,0:T(8,128)S(1)}, u32[]{:S(2)}, u32[]{:S(2)}) %collective-permute-start.31) | collective-permute-done | bytes 1280032 | tf_op jit(solution)/shard_map/ppermute | solution.py:249
  510.9 30.7 %shard_map.53 = (f32[8,40000]{1,0:T(8,128)}, f32[8,40000]{1,0:T(8,128)}, f32[8,40000]{1,0:T(8,128)}, f32[8,40000]{1,0:T(8,128)}) custom-call(s32[1]{0:T(128)} %bitcast.col_ref.me_ref.refs_0_, f32[4,200,1600]{2,1,0:T(8,128)} %shard_map.50.refs_1_, f32[8,40000]{1,0:T(8,128)} %get-tuple-element.111.refs_2_, f32[8,40000]{1,0:T(8,128)} %copy-done.18, ...), custom_call_target="tpu_custom_call" | custom-call | flops 9093120000 | bytes 28467200 | tf_op jit(solution)/shard_map/pallas_call | solution.py:35
  542.2 1.0 collective-permute-start.35
  543.2 25.2 %collective-permute-done.33.refs_1_ = f32[8,40000]{1,0:T(8,128)S(1)} collective-permute-done((f32[8,40000]{1,0:T(8,128)}, f32[8,40000]{1,0:T(8,128)S(1)}, u32[]{:S(2)}, u32[]{:S(2)}) %collective-permute-start.33) | collective-permute-done | bytes 1280032 | tf_op jit(solution)/shard_map/ppermute | solution.py:249
  568.4 27.9 %collective-permute-done.34.refs_2_ = f32[8,40000]{1,0:T(8,128)S(1)} collective-permute-done((f32[8,40000]{1,0:T(8,128)}, f32[8,40000]{1,0:T(8,128)S(1)}, u32[]{:S(2)}, u32[]{:S(2)}) %collective-permute-start.34) | collective-permute-done | bytes 1280032 | tf_op jit(solution)/shard_map/ppermute | solution.py:249
  596.3 2.1 collective-permute-done.35.refs_3_
  598.4 14.7 %shard_map.54 = f32[800,1600]{1,0:T(8,128)} custom-call(s32[1]{0:T(128)} %bitcast.col_ref.me_ref.refs_0_, f32[800,1600]{1,0:T(8,128)} %x_ref.3, f32[8,8,20000]{2,1,0:T(8,128)} %all-to-all-done.crossed_ref, f32[8,40000]{1,0:T(8,128)} %get-tuple-element.115.refs_0_, f32[8,40000]{1,0:T(8,128)} %copy-done.5, f32[8,40000]{1,0:T(8,128)} %copy-done.6, ...), custom_call_target="tpu_custom_call" | custom-call | bytes 20480000 | tf_op jit(solution)/shard_map/pallas_call | solution.py:35
  (94 shorter events, 9.0 us)
Async XLA Ops:
  1.9 39.9 %collective-permute-start.13 = (f32[200,512]{1,0:T(8,128)}, f32[200,512]{1,0:T(8,128)S(1)}, u32[]{:S(2)}, u32[]{:S(2)}) collective-permute-start(f32[200,512]{1,0:T(8,128)} %reshape.15), channel_id=1, source_target_pairs={{0,12},{4,16},{8,20},{12,24},{16,28},{20,0},{24,4},{28,8},{1,13},{... | collective-permute-start | bytes 1228808 | tf_op jit(solution)/shard_map/ppermute | solution.py:249
  5.0 36.8 %collective-permute-start.12 = (f32[200,512]{1,0:T(8,128)}, f32[200,512]{1,0:T(8,128)S(1)}, u32[]{:S(2)}, u32[]{:S(2)}) collective-permute-start(f32[200,512]{1,0:T(8,128)} %reshape.15), channel_id=1, source_target_pairs={{0,8},{4,12},{8,16},{12,20},{16,24},{20,28},{24,0},{28,4},{1,9},{5... | collective-permute-start | bytes 1228808 | tf_op jit(solution)/shard_map/ppermute | solution.py:249
  6.3 35.5 %collective-permute-start.11 = (f32[200,512]{1,0:T(8,128)}, f32[200,512]{1,0:T(8,128)S(1)}, u32[]{:S(2)}, u32[]{:S(2)}) collective-permute-start(f32[200,512]{1,0:T(8,128)} %reshape.15), channel_id=1, source_target_pairs={{0,4},{4,8},{8,12},{12,16},{16,20},{20,24},{24,28},{28,0},{1,5},{5... | collective-permute-start | bytes 1228808 | tf_op jit(solution)/shard_map/ppermute | solution.py:249
  7.5 44.3 %collective-permute-start.3 = (f32[200,512]{1,0:T(8,128)}, f32[200,512]{1,0:T(8,128)S(1)}, u32[]{:S(2)}, u32[]{:S(2)}) collective-permute-start(f32[200,512]{1,0:T(8,128)} %reshape.15), channel_id=1, source_target_pairs={{0,28},{4,0},{8,4},{12,8},{16,12},{20,16},{24,20},{28,24},{1,29},{... | collective-permute-start | bytes 1228808 | tf_op jit(solution)/shard_map/ppermute | solution.py:249
  10.4 41.4 %collective-permute-start.2 = (f32[200,512]{1,0:T(8,128)}, f32[200,512]{1,0:T(8,128)S(1)}, u32[]{:S(2)}, u32[]{:S(2)}) collective-permute-start(f32[200,512]{1,0:T(8,128)} %reshape.15), channel_id=1, source_target_pairs={{0,24},{4,28},{8,0},{12,4},{16,8},{20,12},{24,16},{28,20},{1,25},{... | collective-permute-start | bytes 1228808 | tf_op jit(solution)/shard_map/ppermute | solution.py:249
  10.6 46.3 %copy-start.2 = (f32[10,20,512]{2,1,0:T(8,128)S(1)}, f32[10,20,512]{2,1,0:T(8,128)}, u32[]{:S(2)}) copy-start(f32[10,20,512]{2,1,0:T(8,128)} %param.6) | copy-start | bytes 1228804
  41.8 67.4 %collective-permute-start.4 = (f32[8,20000]{1,0:T(8,128)}, f32[8,20000]{1,0:T(8,128)}, u32[]{:S(2)}, u32[]{:S(2)}) collective-permute-start(f32[8,20000]{1,0:T(8,128)} %get-tuple-element.63), channel_id=1, source_target_pairs={{0,4},{4,8},{8,12},{12,16},{16,20},{20,24},{24,28},{28,0},{1,5},{5... | collective-permute-start | bytes 1920008 | tf_op jit(solution)/shard_map/ppermute | solution.py:249
  41.8 67.4 %collective-permute-start.5 = (f32[8,20000]{1,0:T(8,128)}, f32[8,20000]{1,0:T(8,128)}, u32[]{:S(2)}, u32[]{:S(2)}) collective-permute-start(f32[8,20000]{1,0:T(8,128)} %get-tuple-element.64), channel_id=1, source_target_pairs={{0,8},{4,12},{8,16},{12,20},{16,24},{20,28},{24,0},{28,4},{1,9},{5... | collective-permute-start | bytes 1920008 | tf_op jit(solution)/shard_map/ppermute | solution.py:249
  41.8 72.8 %collective-permute-start.6 = (f32[8,20000]{1,0:T(8,128)}, f32[8,20000]{1,0:T(8,128)}, u32[]{:S(2)}, u32[]{:S(2)}) collective-permute-start(f32[8,20000]{1,0:T(8,128)} %get-tuple-element.65), channel_id=1, source_target_pairs={{0,12},{4,16},{8,20},{12,24},{16,28},{20,0},{24,4},{28,8},{1,13},{... | collective-permute-start | bytes 1920008 | tf_op jit(solution)/shard_map/ppermute | solution.py:249
  51.8 32.0 %collective-permute-start.1 = (f32[200,512]{1,0:T(8,128)}, f32[200,512]{1,0:T(8,128)}, u32[]{:S(2)}, u32[]{:S(2)}) collective-permute-start(f32[200,512]{1,0:T(8,128)} %reshape.15), channel_id=1, source_target_pairs={{0,20},{4,24},{8,28},{12,0},{16,4},{20,8},{24,12},{28,16},{1,21},{... | collective-permute-start | bytes 1228808 | tf_op jit(solution)/shard_map/ppermute | solution.py:249
  51.8 57.4 %collective-permute-start = (f32[200,512]{1,0:T(8,128)}, f32[200,512]{1,0:T(8,128)}, u32[]{:S(2)}, u32[]{:S(2)}) collective-permute-start(f32[200,512]{1,0:T(8,128)} %reshape.15), channel_id=1, source_target_pairs={{0,16},{4,20},{8,24},{12,28},{16,0},{20,4},{24,8},{28,12},{1,17},{... | collective-permute-start | bytes 1228808 | tf_op jit(solution)/shard_map/ppermute | solution.py:249
  57.1 60.1 %copy-start = (f32[4,200,512]{2,1,0:T(8,128)}, f32[4,200,512]{2,1,0:T(8,128)S(1)}, u32[]{:S(2)}) copy-start(f32[4,200,512]{2,1,0:T(8,128)S(1)} %pad_maximum_fusion.refs_0_) | copy-start | bytes 4915204
  83.8 36.9 %collective-permute-start.14 = (f32[4,200,512]{2,1,0:T(8,128)S(1)}, f32[4,200,512]{2,1,0:T(8,128)S(1)}, u32[]{:S(2)}, u32[]{:S(2)}) collective-permute-start(f32[4,200,512]{2,1,0:T(8,128)S(1)} %pad_maximum_fusion.refs_0_), channel_id=1, source_target_pairs={{0,2},{1,3},{2,0},{3,1},{4,6},{5,7},{6,4},{7,5},{8,10},{9,11},{10,... | collective-permute-start | bytes 4915208 | tf_op jit(solution)/shard_map/ppermute | solution.py:254
  114.5 42.7 %copy-start.23 = (f32[8,20000]{1,0:T(8,128)S(1)}, f32[8,20000]{1,0:T(8,128)}, u32[]{:S(2)}) copy-start(f32[8,20000]{1,0:T(8,128)} %get-tuple-element.69) | copy-start | bytes 1920004
  114.5 72.9 %copy-start.21 = (f32[8,20000]{1,0:T(8,128)S(1)}, f32[8,20000]{1,0:T(8,128)}, u32[]{:S(2)}) copy-start(f32[8,20000]{1,0:T(8,128)} %get-tuple-element.70) | copy-start | bytes 1920004
  116.2 151.0 %copy-start.1 = (f32[4,200,512]{2,1,0:T(8,128)}, f32[4,200,512]{2,1,0:T(8,128)S(1)}, u32[]{:S(2)}) copy-start(f32[4,200,512]{2,1,0:T(8,128)S(1)} %pad_maximum_fusion.1.refs_1_) | copy-start | bytes 4915204
  116.2 39.8 %collective-permute-start.15 = (f32[4,200,512]{2,1,0:T(8,128)S(1)}, f32[4,200,512]{2,1,0:T(8,128)}, u32[]{:S(2)}, u32[]{:S(2)}) collective-permute-start(f32[4,200,512]{2,1,0:T(8,128)S(1)} %pad_maximum_fusion.1.refs_1_), channel_id=1, source_target_pairs={{0,2},{1,3},{2,0},{3,1},{4,6},{5,7},{6,4},{7,5},{8,10},{9,11},{10,... | collective-permute-start | bytes 4915208 | tf_op jit(solution)/shard_map/ppermute | solution.py:254
  117.1 114.0 %collective-permute-start.16 = (f32[4,200,512]{2,1,0:T(8,128)S(1)}, f32[4,200,512]{2,1,0:T(8,128)S(1)}, u32[]{:S(2)}, u32[]{:S(2)}) collective-permute-start(f32[4,200,512]{2,1,0:T(8,128)S(1)} %pad_maximum_fusion.refs_0_), channel_id=1, source_target_pairs={{0,1},{1,0},{2,3},{3,2},{4,5},{5,4},{6,7},{7,6},{8,9},{9,8},{10,11... | collective-permute-start | bytes 4915208 | tf_op jit(solution)/shard_map/ppermute | solution.py:254
  120.1 147.1 %collective-permute-start.17 = (f32[4,200,512]{2,1,0:T(8,128)S(1)}, f32[4,200,512]{2,1,0:T(8,128)}, u32[]{:S(2)}, u32[]{:S(2)}) collective-permute-start(f32[4,200,512]{2,1,0:T(8,128)S(1)} %pad_maximum_fusion.1.refs_1_), channel_id=1, source_target_pairs={{0,1},{1,0},{2,3},{3,2},{4,5},{5,4},{6,7},{7,6},{8,9},{9,8},{10,11... | collective-permute-start | bytes 4915208 | tf_op jit(solution)/shard_map/ppermute | solution.py:254
  120.7 146.4 %copy-start.3 = (f32[4,200,512]{2,1,0:T(8,128)}, f32[4,200,512]{2,1,0:T(8,128)S(1)}, u32[]{:S(2)}) copy-start(f32[4,200,512]{2,1,0:T(8,128)S(1)} %collective-permute-done.14.refs_2_) | copy-start | bytes 4915204
  155.9 113.0 %collective-permute-start.18 = (f32[4,200,512]{2,1,0:T(8,128)S(1)}, f32[4,200,512]{2,1,0:T(8,128)}, u32[]{:S(2)}, u32[]{:S(2)}) collective-permute-start(f32[4,200,512]{2,1,0:T(8,128)S(1)} %collective-permute-done.14.refs_2_), channel_id=1, source_target_pairs={{0,1},{1,0},{2,3},{3,2},{4,5},{5,4},{6,7},{7,6},{8,9},{9,8},{10,11... | collective-permute-start | bytes 4915208 | tf_op jit(solution)/shard_map/ppermute | solution.py:254
  157.3 112.2 %collective-permute-start.19 = (f32[4,200,512]{2,1,0:T(8,128)}, f32[4,200,512]{2,1,0:T(8,128)}, u32[]{:S(2)}, u32[]{:S(2)}) collective-permute-start(f32[4,200,512]{2,1,0:T(8,128)} %collective-permute-done.15.refs_3_), channel_id=1, source_target_pairs={{0,1},{1,0},{2,3},{3,2},{4,5},{5,4},{6,7},{7,6},{8,9},{9,8},{10,11... | collective-permute-start | bytes 4915208 | tf_op jit(solution)/shard_map/ppermute | solution.py:254
  157.3 30.2 %collective-permute-start.7 = (f32[8,20000]{1,0:T(8,128)S(1)}, f32[8,20000]{1,0:T(8,128)S(1)}, u32[]{:S(2)}, u32[]{:S(2)}) collective-permute-start(f32[8,20000]{1,0:T(8,128)S(1)} %copy-done.23), channel_id=1, source_target_pairs={{0,16},{4,20},{8,24},{12,28},{16,0},{20,4},{24,8},{28,12},{1,17},{... | collective-permute-start | bytes 1920008 | tf_op jit(solution)/shard_map/ppermute | solution.py:249
  187.5 44.8 %copy-start.22 = (f32[8,20000]{1,0:T(8,128)}, f32[8,20000]{1,0:T(8,128)S(1)}, u32[]{:S(2)}) copy-start(f32[8,20000]{1,0:T(8,128)S(1)} %collective-permute-done.7.refs_5_) | copy-start | bytes 1920004
  187.5 37.5 %collective-permute-start.8 = (f32[8,20000]{1,0:T(8,128)S(1)}, f32[8,20000]{1,0:T(8,128)S(1)}, u32[]{:S(2)}, u32[]{:S(2)}) collective-permute-start(f32[8,20000]{1,0:T(8,128)S(1)} %copy-done.21), channel_id=1, source_target_pairs={{0,20},{4,24},{8,28},{12,0},{16,4},{20,8},{24,12},{28,16},{1,21},{... | collective-permute-start | bytes 1920008 | tf_op jit(solution)/shard_map/ppermute | solution.py:249
  225.0 59.3 %collective-permute-start.9 = (f32[8,20000]{1,0:T(8,128)}, f32[8,20000]{1,0:T(8,128)}, u32[]{:S(2)}, u32[]{:S(2)}) collective-permute-start(f32[8,20000]{1,0:T(8,128)} %get-tuple-element.71), channel_id=1, source_target_pairs={{0,24},{4,28},{8,0},{12,4},{16,8},{20,12},{24,16},{28,20},{1,25},{... | collective-permute-start | bytes 1920008 | tf_op jit(solution)/shard_map/ppermute | solution.py:249
  232.3 52.0 %collective-permute-start.10 = (f32[8,20000]{1,0:T(8,128)}, f32[8,20000]{1,0:T(8,128)}, u32[]{:S(2)}, u32[]{:S(2)}) collective-permute-start(f32[8,20000]{1,0:T(8,128)} %get-tuple-element.72), channel_id=1, source_target_pairs={{0,28},{4,0},{8,4},{12,8},{16,12},{20,16},{24,20},{28,24},{1,29},{... | collective-permute-start | bytes 1920008 | tf_op jit(solution)/shard_map/ppermute | solution.py:249
  267.1 50.8 %collective-permute-start.27 = (f32[8,40000]{1,0:T(8,128)}, f32[8,40000]{1,0:T(8,128)S(1)}, u32[]{:S(2)}, u32[]{:S(2)}) collective-permute-start(f32[8,40000]{1,0:T(8,128)} %get-tuple-element.93), channel_id=1, source_target_pairs={{0,1},{1,2},{2,3},{3,0},{4,5},{5,6},{6,7},{7,4},{8,9},{9,10},{10,1... | collective-permute-start | bytes 3840008 | tf_op jit(solution)/shard_map/ppermute | solution.py:249
  268.9 56.0 %collective-permute-start.28 = (f32[8,40000]{1,0:T(8,128)}, f32[8,40000]{1,0:T(8,128)S(1)}, u32[]{:S(2)}, u32[]{:S(2)}) collective-permute-start(f32[8,40000]{1,0:T(8,128)} %get-tuple-element.94), channel_id=1, source_target_pairs={{0,2},{1,3},{2,0},{3,1},{4,6},{5,7},{6,4},{7,5},{8,10},{9,11},{10,... | collective-permute-start | bytes 3840008 | tf_op jit(solution)/shard_map/ppermute | solution.py:249
  269.5 56.2 %collective-permute-start.29 = (f32[8,40000]{1,0:T(8,128)}, f32[8,40000]{1,0:T(8,128)}, u32[]{:S(2)}, u32[]{:S(2)}) collective-permute-start(f32[8,40000]{1,0:T(8,128)} %get-tuple-element.95), channel_id=1, source_target_pairs={{0,3},{1,0},{2,1},{3,2},{4,7},{5,4},{6,5},{7,6},{8,11},{9,8},{10,9... | collective-permute-start | bytes 3840008 | tf_op jit(solution)/shard_map/ppermute | solution.py:249
  326.1 36.9 %collective-permute-start.20 = (f32[8,20000]{1,0:T(8,128)}, f32[8,20000]{1,0:T(8,128)S(1)}, u32[]{:S(2)}, u32[]{:S(2)}) collective-permute-start(f32[8,20000]{1,0:T(8,128)} %get-tuple-element.83), channel_id=1, source_target_pairs={{0,4},{4,8},{8,12},{12,16},{16,20},{20,24},{24,28},{28,0},{1,5},{5... | collective-permute-start | bytes 1920008 | tf_op jit(solution)/shard_map/ppermute | solution.py:249
  326.2 38.8 %collective-permute-start.21 = (f32[8,20000]{1,0:T(8,128)}, f32[8,20000]{1,0:T(8,128)S(1)}, u32[]{:S(2)}, u32[]{:S(2)}) collective-permute-start(f32[8,20000]{1,0:T(8,128)} %get-tuple-element.84), channel_id=1, source_target_pairs={{0,8},{4,12},{8,16},{12,20},{16,24},{20,28},{24,0},{28,4},{1,9},{5... | collective-permute-start | bytes 1920008 | tf_op jit(solution)/shard_map/ppermute | solution.py:249
  327.6 72.5 %collective-permute-start.22 = (f32[8,20000]{1,0:T(8,128)}, f32[8,20000]{1,0:T(8,128)S(1)}, u32[]{:S(2)}, u32[]{:S(2)}) collective-permute-start(f32[8,20000]{1,0:T(8,128)} %get-tuple-element.85), channel_id=1, source_target_pairs={{0,12},{4,16},{8,20},{12,24},{16,28},{20,0},{24,4},{28,8},{1,13},{... | collective-permute-start | bytes 1920008 | tf_op jit(solution)/shard_map/ppermute | solution.py:249
  327.6 72.5 %collective-permute-start.23 = (f32[8,20000]{1,0:T(8,128)}, f32[8,20000]{1,0:T(8,128)S(1)}, u32[]{:S(2)}, u32[]{:S(2)}) collective-permute-start(f32[8,20000]{1,0:T(8,128)} %get-tuple-element.86), channel_id=1, source_target_pairs={{0,16},{4,20},{8,24},{12,28},{16,0},{20,4},{24,8},{28,12},{1,17},{... | collective-permute-start | bytes 1920008 | tf_op jit(solution)/shard_map/ppermute | solution.py:249
  332.1 68.0 %collective-permute-start.24 = (f32[8,20000]{1,0:T(8,128)}, f32[8,20000]{1,0:T(8,128)S(1)}, u32[]{:S(2)}, u32[]{:S(2)}) collective-permute-start(f32[8,20000]{1,0:T(8,128)} %get-tuple-element.87), channel_id=1, source_target_pairs={{0,20},{4,24},{8,28},{12,0},{16,4},{20,8},{24,12},{28,16},{1,21},{... | collective-permute-start | bytes 1920008 | tf_op jit(solution)/shard_map/ppermute | solution.py:249
  363.0 31.7 %copy-start.7 = (f32[8,20000]{1,0:T(8,128)}, f32[8,20000]{1,0:T(8,128)S(1)}, u32[]{:S(2)}) copy-start(f32[8,20000]{1,0:T(8,128)S(1)} %collective-permute-done.20.refs_1_) | copy-start | bytes 1920004
  363.0 37.2 %collective-permute-start.25 = (f32[8,20000]{1,0:T(8,128)}, f32[8,20000]{1,0:T(8,128)}, u32[]{:S(2)}, u32[]{:S(2)}) collective-permute-start(f32[8,20000]{1,0:T(8,128)} %get-tuple-element.88), channel_id=1, source_target_pairs={{0,24},{4,28},{8,0},{12,4},{16,8},{20,12},{24,16},{28,20},{1,25},{... | collective-permute-start | bytes 1920008 | tf_op jit(solution)/shard_map/ppermute | solution.py:249
  365.1 29.6 %copy-start.8 = (f32[8,20000]{1,0:T(8,128)}, f32[8,20000]{1,0:T(8,128)S(1)}, u32[]{:S(2)}) copy-start(f32[8,20000]{1,0:T(8,128)S(1)} %collective-permute-done.21.refs_2_) | copy-start | bytes 1920004
  365.1 45.7 %collective-permute-start.26 = (f32[8,20000]{1,0:T(8,128)}, f32[8,20000]{1,0:T(8,128)}, u32[]{:S(2)}, u32[]{:S(2)}) collective-permute-start(f32[8,20000]{1,0:T(8,128)} %get-tuple-element.89), channel_id=1, source_target_pairs={{0,28},{4,0},{8,4},{12,8},{16,12},{20,16},{24,20},{28,24},{1,29},{... | collective-permute-start | bytes 1920008 | tf_op jit(solution)/shard_map/ppermute | solution.py:249
  410.7 187.7 %all-to-all-start = ((f32[8,8,20000]{2,1,0:T(8,128)}), f32[8,8,20000]{2,1,0:T(8,128)}, u32[]{:S(2)}, u32[]{:S(2)}) async-start(f32[8,8,20000]{2,1,0:T(8,128)} %shard_map.51), calls=%async_computation | async-start | bytes 10289152 | tf_op jit(solution)/shard_map/all_to_all | solution.py:337
  451.4 28.8 %collective-permute-start.30 = (f32[8,40000]{1,0:T(8,128)}, f32[8,40000]{1,0:T(8,128)S(1)}, u32[]{:S(2)}, u32[]{:S(2)}) collective-permute-start(f32[8,40000]{1,0:T(8,128)} %get-tuple-element.112), channel_id=1, source_target_pairs={{0,1},{1,2},{2,3},{3,0},{4,5},{5,6},{6,7},{7,4},{8,9},{9,10},{10,1... | collective-permute-start | bytes 3840008 | tf_op jit(solution)/shard_map/ppermute | solution.py:249
  452.4 56.9 %collective-permute-start.31 = (f32[8,40000]{1,0:T(8,128)}, f32[8,40000]{1,0:T(8,128)S(1)}, u32[]{:S(2)}, u32[]{:S(2)}) collective-permute-start(f32[8,40000]{1,0:T(8,128)} %get-tuple-element.113), channel_id=1, source_target_pairs={{0,2},{1,3},{2,0},{3,1},{4,6},{5,7},{6,4},{7,5},{8,10},{9,11},{10,... | collective-permute-start | bytes 3840008 | tf_op jit(solution)/shard_map/ppermute | solution.py:249
  453.4 56.5 %collective-permute-start.32 = (f32[8,40000]{1,0:T(8,128)}, f32[8,40000]{1,0:T(8,128)S(1)}, u32[]{:S(2)}, u32[]{:S(2)}) collective-permute-start(f32[8,40000]{1,0:T(8,128)} %get-tuple-element.114), channel_id=1, source_target_pairs={{0,3},{1,0},{2,1},{3,2},{4,7},{5,4},{6,5},{7,6},{8,11},{9,8},{10,9... | collective-permute-start | bytes 3840008 | tf_op jit(solution)/shard_map/ppermute | solution.py:249
  480.2 29.7 %copy-start.18 = (f32[8,40000]{1,0:T(8,128)}, f32[8,40000]{1,0:T(8,128)S(1)}, u32[]{:S(2)}) copy-start(f32[8,40000]{1,0:T(8,128)S(1)} %collective-permute-done.30.refs_3_) | copy-start | bytes 3840004
  541.6 26.7 %collective-permute-start.33 = (f32[8,40000]{1,0:T(8,128)}, f32[8,40000]{1,0:T(8,128)S(1)}, u32[]{:S(2)}, u32[]{:S(2)}) collective-permute-start(f32[8,40000]{1,0:T(8,128)} %get-tuple-element.116), channel_id=1, source_target_pairs={{0,1},{1,2},{2,3},{3,0},{4,5},{5,6},{6,7},{7,4},{8,9},{9,10},{10,1... | collective-permute-start | bytes 3840008 | tf_op jit(solution)/shard_map/ppermute | solution.py:249
  541.6 54.6 %collective-permute-start.34 = (f32[8,40000]{1,0:T(8,128)}, f32[8,40000]{1,0:T(8,128)S(1)}, u32[]{:S(2)}, u32[]{:S(2)}) collective-permute-start(f32[8,40000]{1,0:T(8,128)} %get-tuple-element.117), channel_id=1, source_target_pairs={{0,2},{1,3},{2,0},{3,1},{4,6},{5,7},{6,4},{7,5},{8,10},{9,11},{10,... | collective-permute-start | bytes 3840008 | tf_op jit(solution)/shard_map/ppermute | solution.py:249
  542.2 56.2 %collective-permute-start.35 = (f32[8,40000]{1,0:T(8,128)}, f32[8,40000]{1,0:T(8,128)}, u32[]{:S(2)}, u32[]{:S(2)}) collective-permute-start(f32[8,40000]{1,0:T(8,128)} %get-tuple-element.118), channel_id=1, source_target_pairs={{0,3},{1,0},{2,1},{3,2},{4,7},{5,4},{6,5},{7,6},{8,11},{9,8},{10,9... | collective-permute-start | bytes 3840008 | tf_op jit(solution)/shard_map/ppermute | solution.py:249
  568.4 30.0 %copy-start.5 = (f32[8,40000]{1,0:T(8,128)}, f32[8,40000]{1,0:T(8,128)S(1)}, u32[]{:S(2)}) copy-start(f32[8,40000]{1,0:T(8,128)S(1)} %collective-permute-done.33.refs_1_) | copy-start | bytes 3840004
  (14 other events, 83.7 us)

commit v3 on v1

--- a/solution.py
+++ b/solution.py
@@ -54,28 +54,35 @@
     return min([g for g in range(1, batch + 1) if g == 1 or batch % (8 * g) == 0], key=cost)
 
 
-def wire(block):
-    _, batch, width = block
+def wire(batch, width):
     g = folded(batch, width)
-    return jax.ShapeDtypeStruct((batch // g, g * width), f32)
+    return (batch // g, g * width)
+
+
+def fold(block, shape):
+    rows, g = shape[0], shape[1] // block.shape[1]
+    parts = [block[h * rows : (h + 1) * rows, :] for h in range(g)]
+    return jnp.concatenate(parts, axis=1) if g > 1 else block
+
+
+def unfold(in_ref, width):
+    parts = [in_ref[:, h * width : (h + 1) * width] for h in range(in_ref.shape[1] // width)]
+    return jnp.concatenate(parts, axis=0) if len(parts) > 1 else parts[0]
+
+
+def halved(batch):
+    cut = -(-batch // 16) * 8
+    return [(0, cut), (cut, batch)] if cut < batch else [(0, batch)]
 
 
 def hand_out(me_ref, stage, outs):
-    width = stage.shape[2]
     for s, out_ref in enumerate(outs):
-        b, rows = lax.rem(me_ref[0] + s, len(outs)), out_ref.shape[0]
-        parts = [
-            stage[b, g * rows : (g + 1) * rows, :] for g in range(out_ref.shape[1] // width)
-        ]
-        out_ref[...] = jnp.concatenate(parts, axis=1) if len(parts) > 1 else parts[0]
+        out_ref[...] = fold(stage[lax.rem(me_ref[0] + s, len(outs))], out_ref.shape)
 
 
 def take_in(me_ref, ins, stage):
-    width = stage.shape[2]
     for s, in_ref in enumerate(ins):
-        b, rows = lax.rem(me_ref[0] + len(ins) - s, len(ins)), in_ref.shape[0]
-        for g in range(in_ref.shape[1] // width):
-            stage[b, g * rows : (g + 1) * rows, :] = in_ref[:, g * width : (g + 1) * width]
+        stage[lax.rem(me_ref[0] + len(ins) - s, len(ins))] = unfold(in_ref, stage.shape[2])
 
 
 def rows_of(stage, span):
@@ -87,15 +94,15 @@
     return jnp.concatenate(parts, axis=0) if len(parts) > 1 else parts[0]
 
 
-def cross_body(n, me_ref, x_ref, crossed_ref, *refs):
-    *outs, stage = refs
+def cross_body(n, x_ref, crossed_ref, out_ref):
     rows = tiles(x_ref.shape[0], n)
     for k in tiles(x_ref.shape[1], n):
         crossed_ref[k, :] = jnp.concatenate([x_ref[i, k] for i in rows], axis=1)
-    batch = stage.shape[1]
-    for b in range(stage.shape[0]):
-        stage[b] = crossed_ref[b * batch : (b + 1) * batch, :]
-    hand_out(me_ref, stage, outs)
+    count = out_ref.shape[0]
+    batch = crossed_ref.shape[0] // count
+    for b in range(count):
+        block = crossed_ref[b * batch : (b + 1) * batch, :]
+        out_ref[b] = fold(block, out_ref.shape[1:])
 
 
 def turn_body(me_ref, x_ref, *refs):
@@ -112,16 +119,18 @@
             stage[b, :, strip] = turned[b * batch : (b + 1) * batch]
 
 
-def turn_arriving_body(count, row_ref, me_ref, *refs):
-    ins, (*outs, arrived, stage) = refs[:count], refs[count:]
-    take_in(row_ref, ins, arrived)
+def turn_arriving_body(me_ref, x_ref, *refs):
+    *outs, arrived, stage = refs
+    for b in range(arrived.shape[0]):
+        arrived[b] = unfold(x_ref.at[b], arrived.shape[2])
     turn_rows(lambda strip: rows_of(arrived, strip), arrived.shape[0] * arrived.shape[1], stage)
     hand_out(me_ref, stage, outs)
 
 
-def finish_body(n, count, row_ref, me_ref, x_ref, *refs):
-    crossed, (*ins, out_ref, arrived, stage, total) = refs[:count], refs[count:]
-    take_in(row_ref, crossed, arrived)
+def finish_body(n, me_ref, x_ref, crossed_ref, *refs):
+    *ins, out_ref, arrived, stage, total = refs
+    for b in range(arrived.shape[0]):
+        arrived[b] = unfold(crossed_ref.at[b], arrived.shape[2])
     take_in(me_ref, ins, stage)
     for strip in tiles(total.shape[0]):
         turned = jnp.concatenate([stage[b, :, strip] for b in range(len(ins))], axis=0)
@@ -198,27 +207,49 @@
     lax.fori_loop(0, blocks, result, 0)
 
 
-def leaving_body(n, keep, scale, count, me_ref, x_ref, *refs):
-    *consts, stage, xp, zp = refs
-    consts, outs = consts[:-count], consts[-count:]
-    apply_operator(n, keep, scale, x_ref, stage, *consts, xp, zp)
-    hand_out(me_ref, stage, outs)
-
-
-def arriving_body(n, keep, scale, count, me_ref, *refs):
-    ins, (*consts, stage, xp, zp) = refs[:count], refs[count:]
-    consts, (out_ref, *outs) = consts[:5], consts[5:]
+def send_left(spans, stage, outs):
+    for b in range(stage.shape[0]):
+        for (start, stop), out_ref in zip(spans, outs):
+            out_ref[b] = fold(stage[b, start:stop, :], out_ref.shape[1:])
+
+
+def left_body(n, spans, x_ref, *refs):
+    *consts, out_ref = refs[:6]
+    outs, (stage, xp, zp) = refs[6 : 6 + len(spans)], refs[6 + len(spans) :]
+    for b in range(stage.shape[0]):
+        stage[b] = unfold(x_ref.at[b], stage.shape[2])
+    apply_operator(n, 0.0, 1.0, stage, out_ref, *consts, xp, zp)
+    send_left(spans, out_ref, outs)
+
+
+def left_again_body(n, x_ref, *refs):
+    *consts, out_ref, stage, xp, zp = refs
+    apply_operator(n, time_step, time_step * time_step / 2.0, x_ref, stage, *consts, xp, zp)
+    send_left([(0, stage.shape[1])], stage, [out_ref])
+
+
+def right_body(n, count, me_ref, *refs):
+    ins, (*consts, out_ref, stage, xp, zp) = refs[:count], refs[count:]
     take_in(me_ref, ins, stage)
-    apply_operator(n, keep, scale, stage, out_ref, *consts, xp, zp)
-    hand_out(me_ref, out_ref, outs)
-
-
-def added_body(n, count, me_ref, base_ref, *refs):
-    ins, rest = refs[:count], refs[count:]
-    consts, outs, (stage, xp, zp) = rest[:-3 - count], rest[-3 - count : -3], rest[-3:]
-    take_in(me_ref, ins, stage)
+    apply_operator(
+        n, time_step, time_step * time_step / 2.0, stage, out_ref, *consts, xp, zp
+    )
+
+
+def right_again_body(n, count, rows, spans, me_ref, base_ref, *refs):
+    split = count * len(spans)
+    ins, consts, outs = refs[:split], refs[split : split + 5], refs[split + 5 : split + 5 + count]
+    stage, xp, zp, *arrived = refs[split + 5 + count :]
+    for h, part in enumerate(arrived):
+        take_in(me_ref, ins[h * count : (h + 1) * count], part)
+    sizes = [stop - start for start, stop in spans]
     for b in range(count):
-        stage[b] = base_ref[b] + (time_step * time_step) * stage[b]
+        parts = [
+            part[b, :, r * size : (r + 1) * size]
+            for r in range(rows)
+            for part, size in zip(arrived, sizes)
+        ]
+        stage[b] = base_ref[b] + (time_step * time_step) * jnp.concatenate(parts, axis=1)
     apply_operator(n, 0.0, 1.0, stage, stage, *consts, xp, zp)
     hand_out(me_ref, stage, outs)
 
@@ -236,33 +267,42 @@
     ]
 
 
+def exchange(x, axis):
+    return lax.all_to_all(x, axis, split_axis=0, concat_axis=0, tiled=True)
+
+
 def shards(rows, cols, pairs, one_body, aux, weights):
     n = one_body.shape[0]
     naux = aux.shape[2]
     local_rows, local_cols = pairs.shape
     size = local_rows * local_cols
-    row_me, col_me = (lax.axis_index(a).astype(jnp.int32).reshape(1) for a in ("row", "col"))
+    me = lax.axis_index("col").astype(jnp.int32).reshape(1)
 
     row_block = (rows, local_cols // rows, local_rows)
     col_block = (cols, local_rows // cols, local_cols)
-    row_wires, col_wires = [wire(row_block)] * rows, [wire(col_block)] * cols
-    row_shape = jax.ShapeDtypeStruct(row_block, f32)
-    col_shape = jax.ShapeDtypeStruct(col_block, f32)
+    spans = halved(row_block[1])
+
+    def row_wire(batch):
+        return jax.ShapeDtypeStruct((rows, *wire(batch, local_rows)), f32)
+
+    def col_wires(width):
+        return [jax.ShapeDtypeStruct(wire(col_block[1], width), f32)] * cols
+
     row_stage, col_stage = pltpu.VMEM(row_block, f32), pltpu.VMEM(col_block, f32)
 
-    crossed, *mine = call(
+    crossed, mine = call(
         functools.partial(cross_body, n),
-        [jax.ShapeDtypeStruct((local_cols, local_rows), f32), *row_wires],
-        [row_me, pairs], [row_stage], moved=12 * size,
-    )
-    theirs = call(turn_body, col_wires, [col_me, crossed], [col_stage], moved=8 * size)
-
-    mine[0], aux = lax.optimization_barrier((mine[0], aux))
+        [jax.ShapeDtypeStruct((local_cols, local_rows), f32), row_wire(row_block[1])],
+        [pairs], moved=12 * size,
+    )
+
     whole = lax.all_gather(aux.reshape(-1, naux), "row", axis=0, tiled=True)
-    mine, theirs = shift(mine, "row"), shift(theirs, "col")
-    early = rows // 2 + 1
-    whole, mine[:early], theirs = lax.optimization_barrier((whole, mine[:early], theirs))
     whole = lax.all_gather(whole, "col", axis=0, tiled=False)
+    mine = exchange(mine, "row")
+    whole, crossed = lax.optimization_barrier((whole, crossed))
+    theirs = call(turn_body, col_wires(local_cols), [me, crossed], [col_stage], moved=8 * size)
+    mine, theirs = lax.optimization_barrier((mine, theirs))
+    theirs = shift(theirs, "col")
     group = 8 if n % 8 == 0 else n
     shape = jax.ShapeDtypeStruct((n * n, naux), bf16)
     high, low = pl.pallas_call(
@@ -280,16 +320,15 @@
     left = tripled(one_body)
     right = tripled(-one_body.T)
     gain = weights.reshape(1, naux)
-    half_square = time_step * time_step / 2.0
-
-    def operator(body, arrays, consts, outs, block):
-        blocks, batch, width = block
+
+    def operator(body, arrays, consts, outs, block, scratch=()):
+        batch = block[1]
         work = pltpu.VMEM((-(-batch // 128), n * n, 128), f32)
         return call(
             functools.partial(body, n),
             outs,
             [*arrays, high, low, *consts],
-            [pltpu.VMEM(block, f32), work, work],
+            [pltpu.VMEM(block, f32), work, work, *scratch],
             flops=12 * n * n * (naux + n) * batch,
             moved=4 * n * n * naux + 12 * size,
         )
@@ -297,37 +336,45 @@
     row_consts = [gain, left, right]
     col_consts = [-gain, right, left]
 
-    first, *arriving = operator(
-        lambda n, *refs: arriving_body(n, 0.0, 1.0, rows, *refs),
-        [row_me, *mine], row_consts, [row_shape, *row_wires], row_block,
-    )
-    first, theirs = lax.optimization_barrier((first, theirs))
-    arriving = shift(arriving, "row")
-    double = operator(
-        lambda n, *refs: leaving_body(n, time_step, half_square, rows, *refs),
-        [row_me, first], row_consts, row_wires, row_block,
-    )
-    (base,) = operator(
-        lambda n, *refs: arriving_body(n, time_step, half_square, cols, *refs),
-        [col_me, *theirs], col_consts, [col_shape], col_block,
-    )
-    arriving, base, double = lax.optimization_barrier((arriving, base, double))
-    double = shift(double, "row")
-    first = call(
-        functools.partial(turn_arriving_body, rows),
-        col_wires, [row_me, col_me, *arriving], [row_stage, col_stage], moved=8 * size,
-    )
-    first = shift(first, "col")
+    first, *parts = operator(
+        lambda n, *refs: left_body(n, spans, *refs),
+        [mine], row_consts,
+        [jax.ShapeDtypeStruct(row_block, f32)] + [row_wire(b - a) for a, b in spans], row_block,
+    )
+    double = operator(left_again_body, [first], row_consts, row_wire(row_block[1]), row_block)
+    double, theirs = lax.optimization_barrier((double, theirs))
+    base = operator(
+        lambda n, *refs: right_body(n, cols, *refs),
+        [me, *theirs], col_consts, jax.ShapeDtypeStruct(col_block, f32), col_block,
+    )
+    arriving = []
+    for h, (start, stop) in enumerate(spans):
+        part = exchange(parts[h], "row")
+        if h + 1 < len(spans):
+            part, parts[h + 1] = lax.optimization_barrier((part, parts[h + 1]))
+        else:
+            part, double, base = lax.optimization_barrier((part, double, base))
+        turned = call(
+            turn_arriving_body, col_wires(rows * (stop - start)), [me, part],
+            [
+                pltpu.VMEM((rows, stop - start, local_rows), f32),
+                pltpu.VMEM((*col_block[:2], rows * (stop - start)), f32),
+            ],
+            moved=8 * size // len(spans),
+        )
+        arriving += shift(turned, "col")
+    double = exchange(double, "row")
     last = operator(
-        lambda n, *refs: added_body(n, cols, *refs),
-        [col_me, base, *first], col_consts, col_wires, col_block,
+        lambda n, *refs: right_again_body(n, cols, rows, spans, *refs),
+        [me, base, *arriving], col_consts, col_wires(local_cols), col_block,
+        [pltpu.VMEM((*col_block[:2], rows * (b - a)), f32) for a, b in spans],
     )
     last = shift(last, "col")
 
     return call(
-        functools.partial(finish_body, n, rows),
+        functools.partial(finish_body, n),
         jax.ShapeDtypeStruct(pairs.shape, f32),
-        [row_me, col_me, pairs, *double, *last],
+        [me, pairs, double, *last],
         [row_stage, col_stage, pltpu.VMEM((local_cols, local_rows), f32)],
         moved=16 * size,
     )

time: 585 us -> 596 us (1.019)
  starting transfers between devices: 167 us -> 25.7 us
  waiting for transfers between devices: 208 us -> 295 us
  blocking collectives: 0 us -> 65.9 us
    ppermute x30 -> x12, starting transfers between devices: 167 us -> 11.3 us  [shift(): lax.ppermute(parts[s], axis, [(d, (d + s) % n) for d in range(n)])]
    all_to_all x0 -> x1, blocking collectives: none -> 65.9 us  [exchange(): return lax.all_to_all(x, axis, split_axis=0, concat_axis=0, tiled=True)]
    all_gather x1, waiting for transfers between devices: 0.17 us -> 64.3 us  [shards(): whole = lax.all_gather(aux.reshape(-1, naux), 'row', axis=0, tiled=True)]
    all_to_all x0 -> x3, waiting for transfers between devices: none -> 35.3 us  [exchange(): return lax.all_to_all(x, axis, split_axis=0, concat_axis=0, tiled=True)]
    all_to_all x0 -> x3, starting transfers between devices: none -> 14.3 us  [exchange(): return lax.all_to_all(x, axis, split_axis=0, concat_axis=0, tiled=True)]
    all_gather x1, waiting for transfers between devices: 80.7 us -> 69 us  [shards(): whole = lax.all_gather(whole, 'col', axis=0, tiled=False)]
    pallas_call x8 -> x9, Pallas kernels: 164 us -> 168 us  [call(): pl.pallas_call(body, in_specs=[smem if x.dtype == jnp.int32 else vmem for...]
    ppermute x30 -> x12, waiting for transfers between devices: 128 us -> 126 us  [shift(): lax.ppermute(parts[s], axis, [(d, (d + s) % n) for d in range(n)])]
  transfers between devices with their start and end apart: 32 -> 17, of which waited for: 10 -> 14; matrix products, arithmetic and copies ran while one was open for 0% -> 0% of each run, Pallas kernels for 19% -> 20%
where the time goes in v3:
time: 596 us; the launch traced here: 587 us
  waiting for transfers between devices  295 us (49%)
  Pallas kernels  181 us (30%)
  blocking collectives  65.9 us (11%)
  starting transfers between devices  25.7 us (4%)
  between operations  13.9 us (2%)
    pallas_call x9, Pallas kernels, call(): pl.pallas_call(body, in_specs=[smem if x.dtype == jnp.int32 else vmem for...  168 us
    ppermute x12, waiting for transfers between devices, shift(): lax.ppermute(parts[s], axis, [(d, (d + s) % n) for d in range(n)])  126 us
    all_gather x1, waiting for transfers between devices, shards(): whole = lax.all_gather(whole, 'col', axis=0, tiled=False)  69 us
    all_to_all x1, blocking collectives, exchange(): return lax.all_to_all(x, axis, split_axis=0, concat_axis=0, tiled=True)  65.9 us
    all_gather x1, waiting for transfers between devices, shards(): whole = lax.all_gather(aux.reshape(-1, naux), 'row', axis=0, tiled=True)  64.3 us
    all_to_all x3, waiting for transfers between devices, exchange(): return lax.all_to_all(x, axis, split_axis=0, concat_axis=0, tiled=True)  35.3 us
    all_to_all x3, starting transfers between devices, exchange(): return lax.all_to_all(x, axis, split_axis=0, concat_axis=0, tiled=True)  14.3 us
    pallas_call x1, Pallas kernels, shards(): pl.pallas_call(functools.partial(split_body, n), grid=(n // group,), in_s...  13.1 us
  transfers between devices with their start and end apart: 17, of which 14 were waited for; matrix products, arithmetic and copies ran while one was open for 0% of the time, Pallas kernels for 20%

profile of v3, /device:TPU:1, one launch (start us, length us, event | category | flops | bytes accessed | tf_op | source)
XLA Modules:
  0.0 587.3 jit_solution(14400008956086521482)
XLA Ops:
  6.5 1.8 reshape.11
  8.4 0.0 all-gather.4.cloned.1.call-update
  8.4 0.0 all-gather.6.cloned.1.call-start
  8.4 64.3 %all-gather.4.cloned.1.call-done = f32[1600,512]{1,0:T(8,128)} async-done(((f32[200,512]{1,0:T(8,128)}), f32[1600,512]{1,0:T(8,128)}) %all-gather.4.cloned.1.call-update) | async-done | bytes 3276816 | tf_op jit(solution)/shard_map/all_gather | solution.py:299
  72.8 0.0 all-gather.6.cloned.1.call-update
  72.8 11.6 %shard_map.46 = (f32[1600,800]{1,0:T(8,128)}, f32[8,8,20000]{2,1,0:T(8,128)}) custom-call(f32[800,1600]{1,0:T(8,128)} %x_ref.3), custom_call_target="tpu_custom_call" | custom-call | bytes 15360000 | tf_op jit(solution)/shard_map/pallas_call | solution.py:35
  84.4 5.0 all-to-all-start
  89.4 0.1 copy.5
  89.5 0.7 pad_maximum_fusion
  90.3 69.0 %all-gather.6.cloned.1.call-done = f32[6400,512]{1,0:T(8,128)} async-done(((f32[1600,512]{1,0:T(8,128)}), f32[6400,512]{1,0:T(8,128)}) %all-gather.6.cloned.1.call-update) | async-done | bytes 13107216 | tf_op jit(solution)/shard_map/all_gather | solution.py:300
  159.3 6.8 %shard_map.47 = (f32[8,40000]{1,0:T(8,128)}, f32[8,40000]{1,0:T(8,128)}, f32[8,40000]{1,0:T(8,128)}, f32[8,40000]{1,0:T(8,128)}) custom-call(s32[1]{0:T(128)} %bitcast.me_ref.refs_0_, f32[1600,800]{1,0:T(8,128)} %get-tuple-element.47.x_ref), custom_call_target="tpu_custom_call" | custom-call | bytes 10240000 | tf_op jit(solution)/shard_map/pallas_call | solution.py:35
  166.1 35.3 %all-to-all-done.refs_0_ = f32[8,8,20000]{2,1,0:T(8,128)} async-done(((f32[8,8,20000]{2,1,0:T(8,128)}), f32[8,8,20000]{2,1,0:T(8,128)}, u32[]{:S(2)}, u32[]{:S(2)}) %all-to-all-start) | async-done | bytes 5120032 | tf_op jit(solution)/shard_map/all_to_all | solution.py:271
  201.5 13.1 %shard_map.48 = (bf16[6400,512]{1,0:T(8,128)(2,1)}, bf16[6400,512]{1,0:T(8,128)(2,1)}) custom-call(f32[4,1600,512]{2,1,0:T(8,128)} %bitcast.7), custom_call_target="tpu_custom_call" | custom-call | flops 6553600 | bytes 26214400 | tf_op jit(solution)/shard_map/pallas_call | solution.py:308
  214.6 33.6 %shard_map.49 = (f32[8,200,800]{2,1,0:T(8,128)}, f32[8,8,10400]{2,1,0:T(8,128)}, f32[8,24,3200]{2,1,0:T(8,128)}) custom-call(f32[8,8,20000]{2,1,0:T(8,128)} %all-to-all-done.refs_0_, bf16[6400,512]{1,0:T(8,128)(2,1)} %get-tuple-element.54.refs_1_.refs_0_.refs_5_.refs_10_, bf16[6400,512]{1,0:T(8,128)(2,1)} %get-tuple-element.55.refs_2_.refs_1_.refs_6_.refs_11_, ...), custom_call_target="tpu_custom_call" | custom-call | flops 9093120000 | bytes 28467200 | tf_op jit(solution)/shard_map/pallas_call | solution.py:35
  248.2 65.9 %all_to_all.20.x_ref = f32[8,8,10400]{2,1,0:T(8,128)} all-to-all(f32[8,8,10400]{2,1,0:T(8,128)} %get-tuple-element.56), channel_id=1, replica_groups=mesh['row'=8,'col'=4] {'row'}, dimensions={0} | all-to-all | bytes 5324800 | tf_op jit(solution)/shard_map/all_to_all | solution.py:271
  314.0 3.8 all-to-all-start.2
  317.8 3.0 collective-permute-start
  320.8 0.4 collective-permute-start.1
  321.2 0.2 collective-permute-start.2
  321.4 0.5 neg.13
  321.9 31.0 %shard_map.50 = f32[8,8,20000]{2,1,0:T(8,128)} custom-call(f32[8,200,800]{2,1,0:T(8,128)} %get-tuple-element.59.x_ref, bf16[6400,512]{1,0:T(8,128)(2,1)} %get-tuple-element.54.refs_1_.refs_0_.refs_5_.refs_10_, bf16[6400,512]{1,0:T(8,128)(2,1)} %get-tuple-element.55.refs_2_.refs_1_.refs_6_.refs_11_, f32[1,512]{1,0:T(1,128)} %bitcast.9, ...), custom_call_target="tpu_custom_call" | custom-call | flops 9093120000 | bytes 28467200 | tf_op jit(solution)/shard_map/pallas_call | solution.py:35
  352.9 23.8 %collective-permute-done.1.refs_3_ = f32[8,40000]{1,0:T(8,128)} collective-permute-done((f32[8,40000]{1,0:T(8,128)}, f32[8,40000]{1,0:T(8,128)}, u32[]{:S(2)}, u32[]{:S(2)}) %collective-permute-start.1) | collective-permute-done | bytes 1280032 | tf_op jit(solution)/shard_map/ppermute | solution.py:266
  376.8 0.6 collective-permute-done.2.refs_4_
  377.4 28.3 %shard_map.51.refs_1_ = f32[4,200,1600]{2,1,0:T(8,128)} custom-call(s32[1]{0:T(128)} %bitcast.me_ref.refs_0_, f32[8,40000]{1,0:T(8,128)} %get-tuple-element.65.refs_1_, f32[8,40000]{1,0:T(8,128)} %collective-permute-done.refs_2_, f32[8,40000]{1,0:T(8,128)} %collective-permute-done.1.refs_3_, f32[8,40000]{1,0:T(8,128)} %collective-permute-done.2.refs_4_, ...), custom_call_target="tpu_custom_call" | custom-call | flops 9093120000 | bytes 28467200 | tf_op jit(solution)/shard_map/pallas_call | solution.py:35
  405.7 1.4 copy-done
  407.1 5.6 all-to-all-start.3
  412.7 5.0 shard_map.52
  417.7 0.1 collective-permute-start.3
  417.8 1.0 collective-permute-start.4
  418.8 0.7 collective-permute-start.5
  419.5 4.8 shard_map.53
  424.3 1.1 collective-permute-start.6
  425.4 0.4 collective-permute-start.7
  425.8 5.2 collective-permute-done.3.refs_3_
  431.0 2.9 collective-permute-start.8
  433.9 13.8 %collective-permute-done.4.refs_4_ = f32[8,20800]{1,0:T(8,128)S(1)} collective-permute-done((f32[8,20800]{1,0:T(8,128)}, f32[8,20800]{1,0:T(8,128)S(1)}, u32[]{:S(2)}, u32[]{:S(2)}) %collective-permute-start.4) | collective-permute-done | bytes 665632 | tf_op jit(solution)/shard_map/ppermute | solution.py:266
  447.7 2.6 collective-permute-done.5.refs_5_
  450.3 8.1 %collective-permute-done.6.refs_7_ = f32[200,768]{1,0:T(8,128)S(1)} collective-permute-done((f32[200,768]{1,0:T(8,128)}, f32[200,768]{1,0:T(8,128)S(1)}, u32[]{:S(2)}, u32[]{:S(2)}) %collective-permute-start.6) | collective-permute-done | bytes 614432 | tf_op jit(solution)/shard_map/ppermute | solution.py:266
  458.4 15.6 %collective-permute-done.7.refs_8_ = f32[200,768]{1,0:T(8,128)S(1)} collective-permute-done((f32[200,768]{1,0:T(8,128)}, f32[200,768]{1,0:T(8,128)S(1)}, u32[]{:S(2)}, u32[]{:S(2)}) %collective-permute-start.7) | collective-permute-done | bytes 614432 | tf_op jit(solution)/shard_map/ppermute | solution.py:266
  474.1 1.3 collective-permute-done.8.refs_9_
  475.4 0.8 copy-done.10
  476.2 32.6 %shard_map.54 = (f32[8,40000]{1,0:T(8,128)}, f32[8,40000]{1,0:T(8,128)}, f32[8,40000]{1,0:T(8,128)}, f32[8,40000]{1,0:T(8,128)}) custom-call(s32[1]{0:T(128)} %bitcast.me_ref.refs_0_, f32[4,200,1600]{2,1,0:T(8,128)} %shard_map.51.refs_1_, f32[8,20800]{1,0:T(8,128)} %get-tuple-element.72.refs_2_, f32[8,20800]{1,0:T(8,128)} %copy-done.5, ...), custom_call_target="tpu_custom_call" | custom-call | flops 9093120000 | bytes 28467200 | tf_op jit(solution)/shard_map/pallas_call | solution.py:35
  508.7 0.5 collective-permute-start.10
  509.2 0.9 collective-permute-start.11
  510.2 25.4 %collective-permute-done.9.refs_1_ = f32[8,40000]{1,0:T(8,128)S(1)} collective-permute-done((f32[8,40000]{1,0:T(8,128)}, f32[8,40000]{1,0:T(8,128)S(1)}, u32[]{:S(2)}, u32[]{:S(2)}) %collective-permute-start.9) | collective-permute-done | bytes 1280032 | tf_op jit(solution)/shard_map/ppermute | solution.py:266
  535.6 27.6 %collective-permute-done.10.refs_2_ = f32[8,40000]{1,0:T(8,128)S(1)} collective-permute-done((f32[8,40000]{1,0:T(8,128)}, f32[8,40000]{1,0:T(8,128)S(1)}, u32[]{:S(2)}, u32[]{:S(2)}) %collective-permute-start.10) | collective-permute-done | bytes 1280032 | tf_op jit(solution)/shard_map/ppermute | solution.py:266
  563.2 2.2 collective-permute-done.11.refs_3_
  565.4 14.6 %shard_map.55 = f32[800,1600]{1,0:T(8,128)} custom-call(s32[1]{0:T(128)} %bitcast.me_ref.refs_0_, f32[800,1600]{1,0:T(8,128)} %x_ref.3, f32[8,8,20000]{2,1,0:T(8,128)} %all-to-all-done.3.crossed_ref, f32[8,40000]{1,0:T(8,128)} %get-tuple-element.81.refs_0_, f32[8,40000]{1,0:T(8,128)} %copy-done.1, f32[8,40000]{1,0:T(8,128)} %copy-done.2, ...), custom_call_target="tpu_custom_call" | custom-call | bytes 20480000 | tf_op jit(solution)/shard_map/pallas_call | solution.py:35
  (27 shorter events, 0.1 us)
Async XLA Ops:
  6.5 66.2 %all-gather.4.cloned.1.call-start = ((), (), s32[]{:S(2)}) async-start(), calls=%async_computation.4 | async-start | bytes 3686400 | tf_op jit(solution)/shard_map/all_gather | solution.py:299
  8.4 150.9 %all-gather.6.cloned.1.call-start = ((), (), s32[]{:S(2)}) async-start(), calls=%async_computation.5 | async-start | bytes 16384000 | tf_op jit(solution)/shard_map/all_gather | solution.py:300
  84.4 5.0 copy-start.3
  84.4 117.1 %all-to-all-start = ((f32[8,8,20000]{2,1,0:T(8,128)}), f32[8,8,20000]{2,1,0:T(8,128)}, u32[]{:S(2)}, u32[]{:S(2)}) async-start(f32[8,8,20000]{2,1,0:T(8,128)} %get-tuple-element.45), calls=%async_computation | async-start | bytes 10289152 | tf_op jit(solution)/shard_map/all_to_all | solution.py:271
  314.0 7.3 %copy-start.4 = (f32[512]{0:T(512)S(1)}, f32[512]{0:T(512)}, u32[]{:S(2)}) copy-start(f32[512]{0:T(512)} %param.7) | copy-start | bytes 6148
  314.0 91.6 %all-to-all-start.2 = ((f32[8,24,3200]{2,1,0:T(8,128)}), f32[8,24,3200]{2,1,0:T(8,128)S(1)}, u32[]{:S(2)}, u32[]{:S(2)}) async-start(f32[8,24,3200]{2,1,0:T(8,128)} %get-tuple-element.58), calls=%async_computation.2 | async-start | bytes 4915200 | tf_op jit(solution)/shard_map/all_to_all | solution.py:271
  317.8 35.1 %collective-permute-start = (f32[8,40000]{1,0:T(8,128)}, f32[8,40000]{1,0:T(8,128)}, u32[]{:S(2)}, u32[]{:S(2)}) collective-permute-start(f32[8,40000]{1,0:T(8,128)} %get-tuple-element.61), channel_id=1, source_target_pairs={{0,1},{1,2},{2,3},{3,0},{4,5},{5,6},{6,7},{7,4},{8,9},{9,10},{10,1... | collective-permute-start | bytes 3840008 | tf_op jit(solution)/shard_map/ppermute | solution.py:266
  320.8 56.0 %collective-permute-start.1 = (f32[8,40000]{1,0:T(8,128)}, f32[8,40000]{1,0:T(8,128)}, u32[]{:S(2)}, u32[]{:S(2)}) collective-permute-start(f32[8,40000]{1,0:T(8,128)} %get-tuple-element.62), channel_id=1, source_target_pairs={{0,2},{1,3},{2,0},{3,1},{4,6},{5,7},{6,4},{7,5},{8,10},{9,11},{10,... | collective-permute-start | bytes 3840008 | tf_op jit(solution)/shard_map/ppermute | solution.py:266
  321.2 56.2 %collective-permute-start.2 = (f32[8,40000]{1,0:T(8,128)}, f32[8,40000]{1,0:T(8,128)}, u32[]{:S(2)}, u32[]{:S(2)}) collective-permute-start(f32[8,40000]{1,0:T(8,128)} %get-tuple-element.63), channel_id=1, source_target_pairs={{0,3},{1,0},{2,1},{3,2},{4,7},{5,4},{6,5},{7,6},{8,11},{9,8},{10,9... | collective-permute-start | bytes 3840008 | tf_op jit(solution)/shard_map/ppermute | solution.py:266
  405.7 1.4 copy-start
  407.1 158.3 %all-to-all-start.3 = ((f32[8,8,20000]{2,1,0:T(8,128)}), f32[8,8,20000]{2,1,0:T(8,128)}, u32[]{:S(2)}, u32[]{:S(2)}) async-start(f32[8,8,20000]{2,1,0:T(8,128)} %shard_map.50), calls=%async_computation.3 | async-start | bytes 10289152 | tf_op jit(solution)/shard_map/all_to_all | solution.py:271
  417.7 13.3 %collective-permute-start.3 = (f32[8,20800]{1,0:T(8,128)}, f32[8,20800]{1,0:T(8,128)S(1)}, u32[]{:S(2)}, u32[]{:S(2)}) collective-permute-start(f32[8,20800]{1,0:T(8,128)} %get-tuple-element.73), channel_id=1, source_target_pairs={{0,1},{1,2},{2,3},{3,0},{4,5},{5,6},{6,7},{7,4},{8,9},{9,10},{10,1... | collective-permute-start | bytes 1996808 | tf_op jit(solution)/shard_map/ppermute | solution.py:266
  417.8 29.9 %collective-permute-start.4 = (f32[8,20800]{1,0:T(8,128)}, f32[8,20800]{1,0:T(8,128)S(1)}, u32[]{:S(2)}, u32[]{:S(2)}) collective-permute-start(f32[8,20800]{1,0:T(8,128)} %get-tuple-element.74), channel_id=1, source_target_pairs={{0,2},{1,3},{2,0},{3,1},{4,6},{5,7},{6,4},{7,5},{8,10},{9,11},{10,... | collective-permute-start | bytes 1996808 | tf_op jit(solution)/shard_map/ppermute | solution.py:266
  418.8 31.5 %collective-permute-start.5 = (f32[8,20800]{1,0:T(8,128)}, f32[8,20800]{1,0:T(8,128)S(1)}, u32[]{:S(2)}, u32[]{:S(2)}) collective-permute-start(f32[8,20800]{1,0:T(8,128)} %get-tuple-element.75), channel_id=1, source_target_pairs={{0,3},{1,0},{2,1},{3,2},{4,7},{5,4},{6,5},{7,6},{8,11},{9,8},{10,9... | collective-permute-start | bytes 1996808 | tf_op jit(solution)/shard_map/ppermute | solution.py:266
  424.3 34.1 %collective-permute-start.6 = (f32[200,768]{1,0:T(8,128)}, f32[200,768]{1,0:T(8,128)S(1)}, u32[]{:S(2)}, u32[]{:S(2)}) collective-permute-start(f32[200,768]{1,0:T(8,128)} %get-tuple-element.78), channel_id=1, source_target_pairs={{0,1},{1,2},{2,3},{3,0},{4,5},{5,6},{6,7},{7,4},{8,9},{9,10},{10,1... | collective-permute-start | bytes 1843208 | tf_op jit(solution)/shard_map/ppermute | solution.py:266
  425.4 48.7 %collective-permute-start.7 = (f32[200,768]{1,0:T(8,128)}, f32[200,768]{1,0:T(8,128)S(1)}, u32[]{:S(2)}, u32[]{:S(2)}) collective-permute-start(f32[200,768]{1,0:T(8,128)} %get-tuple-element.79), channel_id=1, source_target_pairs={{0,2},{1,3},{2,0},{3,1},{4,6},{5,7},{6,4},{7,5},{8,10},{9,11},{10,... | collective-permute-start | bytes 1843208 | tf_op jit(solution)/shard_map/ppermute | solution.py:266
  431.0 44.4 %copy-start.5 = (f32[8,20800]{1,0:T(8,128)}, f32[8,20800]{1,0:T(8,128)S(1)}, u32[]{:S(2)}) copy-start(f32[8,20800]{1,0:T(8,128)S(1)} %collective-permute-done.3.refs_3_) | copy-start | bytes 1996804
  431.0 44.4 %collective-permute-start.8 = (f32[200,768]{1,0:T(8,128)}, f32[200,768]{1,0:T(8,128)S(1)}, u32[]{:S(2)}, u32[]{:S(2)}) collective-permute-start(f32[200,768]{1,0:T(8,128)} %get-tuple-element.80), channel_id=1, source_target_pairs={{0,3},{1,0},{2,1},{3,2},{4,7},{5,4},{6,5},{7,6},{8,11},{9,8},{10,9... | collective-permute-start | bytes 1843208 | tf_op jit(solution)/shard_map/ppermute | solution.py:266
  447.7 27.6 %copy-start.6 = (f32[8,20800]{1,0:T(8,128)}, f32[8,20800]{1,0:T(8,128)S(1)}, u32[]{:S(2)}) copy-start(f32[8,20800]{1,0:T(8,128)S(1)} %collective-permute-done.4.refs_4_) | copy-start | bytes 1996804
  450.3 25.0 %copy-start.7 = (f32[8,20800]{1,0:T(8,128)}, f32[8,20800]{1,0:T(8,128)S(1)}, u32[]{:S(2)}) copy-start(f32[8,20800]{1,0:T(8,128)S(1)} %collective-permute-done.5.refs_5_) | copy-start | bytes 1996804
  458.4 16.9 %copy-start.8 = (f32[200,768]{1,0:T(8,128)}, f32[200,768]{1,0:T(8,128)S(1)}, u32[]{:S(2)}) copy-start(f32[200,768]{1,0:T(8,128)S(1)} %collective-permute-done.6.refs_7_) | copy-start | bytes 1843204
  474.0 1.3 copy-start.9
  475.4 0.8 copy-start.10
  508.7 26.8 %collective-permute-start.9 = (f32[8,40000]{1,0:T(8,128)}, f32[8,40000]{1,0:T(8,128)S(1)}, u32[]{:S(2)}, u32[]{:S(2)}) collective-permute-start(f32[8,40000]{1,0:T(8,128)} %get-tuple-element.82), channel_id=1, source_target_pairs={{0,1},{1,2},{2,3},{3,0},{4,5},{5,6},{6,7},{7,4},{8,9},{9,10},{10,1... | collective-permute-start | bytes 3840008 | tf_op jit(solution)/shard_map/ppermute | solution.py:266
  508.7 54.5 %collective-permute-start.10 = (f32[8,40000]{1,0:T(8,128)}, f32[8,40000]{1,0:T(8,128)S(1)}, u32[]{:S(2)}, u32[]{:S(2)}) collective-permute-start(f32[8,40000]{1,0:T(8,128)} %get-tuple-element.83), channel_id=1, source_target_pairs={{0,2},{1,3},{2,0},{3,1},{4,6},{5,7},{6,4},{7,5},{8,10},{9,11},{10,... | collective-permute-start | bytes 3840008 | tf_op jit(solution)/shard_map/ppermute | solution.py:266
  509.2 56.1 %collective-permute-start.11 = (f32[8,40000]{1,0:T(8,128)}, f32[8,40000]{1,0:T(8,128)}, u32[]{:S(2)}, u32[]{:S(2)}) collective-permute-start(f32[8,40000]{1,0:T(8,128)} %get-tuple-element.84), channel_id=1, source_target_pairs={{0,3},{1,0},{2,1},{3,2},{4,7},{5,4},{6,5},{7,6},{8,11},{9,8},{10,9... | collective-permute-start | bytes 3840008 | tf_op jit(solution)/shard_map/ppermute | solution.py:266
  535.6 29.8 %copy-start.1 = (f32[8,40000]{1,0:T(8,128)}, f32[8,40000]{1,0:T(8,128)S(1)}, u32[]{:S(2)}) copy-start(f32[8,40000]{1,0:T(8,128)S(1)} %collective-permute-done.9.refs_1_) | copy-start | bytes 3840004
  563.2 2.2 copy-start.2
Sparse Core Ops, SparseCore 0:
  9.5 63.1 all-gather.3
  74.3 84.9 all-gather.5

commit v4 on v3

--- a/solution.py
+++ b/solution.py
@@ -267,6 +267,10 @@
     ]
 
 
+def after(x, y):
+    return lax.optimization_barrier((x, y))[0]
+
+
 def exchange(x, axis):
     return lax.all_to_all(x, axis, split_axis=0, concat_axis=0, tiled=True)
 
@@ -296,13 +300,14 @@
         [pairs], moved=12 * size,
     )
 
+    aux = after(aux, mine)
     whole = lax.all_gather(aux.reshape(-1, naux), "row", axis=0, tiled=True)
     whole = lax.all_gather(whole, "col", axis=0, tiled=False)
     mine = exchange(mine, "row")
-    whole, crossed = lax.optimization_barrier((whole, crossed))
-    theirs = call(turn_body, col_wires(local_cols), [me, crossed], [col_stage], moved=8 * size)
-    mine, theirs = lax.optimization_barrier((mine, theirs))
-    theirs = shift(theirs, "col")
+    turned = call(
+        turn_body, col_wires(local_cols), [me, after(crossed, whole)], [col_stage], moved=8 * size
+    )
+    theirs = shift(turned, "col")
     group = 8 if n % 8 == 0 else n
     shape = jax.ShapeDtypeStruct((n * n, naux), bf16)
     high, low = pl.pallas_call(
@@ -338,22 +343,20 @@
 
     first, *parts = operator(
         lambda n, *refs: left_body(n, spans, *refs),
-        [mine], row_consts,
+        [after(mine, turned)], row_consts,
         [jax.ShapeDtypeStruct(row_block, f32)] + [row_wire(b - a) for a, b in spans], row_block,
     )
     double = operator(left_again_body, [first], row_consts, row_wire(row_block[1]), row_block)
-    double, theirs = lax.optimization_barrier((double, theirs))
     base = operator(
         lambda n, *refs: right_body(n, cols, *refs),
-        [me, *theirs], col_consts, jax.ShapeDtypeStruct(col_block, f32), col_block,
-    )
-    arriving = []
+        [me, *after(theirs, double)], col_consts, jax.ShapeDtypeStruct(col_block, f32), col_block,
+    )
+    arriving, part = [], double
     for h, (start, stop) in enumerate(spans):
-        part = exchange(parts[h], "row")
-        if h + 1 < len(spans):
-            part, parts[h + 1] = lax.optimization_barrier((part, parts[h + 1]))
-        else:
-            part, double, base = lax.optimization_barrier((part, double, base))
+        part = exchange(after(parts[h], (part, double)) if h else parts[h], "row")
+        if h + 1 == len(spans):
+            double = after(double, part)
+            part = after(part, base)
         turned = call(
             turn_arriving_body, col_wires(rows * (stop - start)), [me, part],
             [

time: 596 us -> 612 us (1.027)
  waiting for transfers between devices: 295 us -> 322 us
    ppermute x12, waiting for transfers between devices: 126 us -> 138 us  [shift(): lax.ppermute(parts[s], axis, [(d, (d + s) % n) for d in range(n)])]
    all_gather x1, waiting for transfers between devices: 69 us -> 81 us  [shards(): whole = lax.all_gather(whole, 'col', axis=0, tiled=False)]
  transfers between devices with their start and end apart: 17 -> 17, of which waited for: 14 -> 13; matrix products, arithmetic and copies ran while one was open for 0% -> 0% of each run, Pallas kernels for 20% -> 20%
where the time goes in v4:
time: 612 us; the launch traced here: 603 us
  waiting for transfers between devices  322 us (53%)
  Pallas kernels  180 us (29%)
  blocking collectives  59.9 us (10%)
  starting transfers between devices  24.3 us (4%)
  between operations  14 us (2%)
    pallas_call x9, Pallas kernels, call(): pl.pallas_call(body, in_specs=[smem if x.dtype == jnp.int32 else vmem for...  167 us
    ppermute x12, waiting for transfers between devices, shift(): lax.ppermute(parts[s], axis, [(d, (d + s) % n) for d in range(n)])  138 us
    all_gather x1, waiting for transfers between devices, shards(): whole = lax.all_gather(whole, 'col', axis=0, tiled=False)  81 us
    all_gather x1, waiting for transfers between devices, shards(): whole = lax.all_gather(aux.reshape(-1, naux), 'row', axis=0, tiled=True)  63.3 us
    all_to_all x1, blocking collectives, exchange(): return lax.all_to_all(x, axis, split_axis=0, concat_axis=0, tiled=True)  59.9 us
    all_to_all x3, waiting for transfers between devices, exchange(): return lax.all_to_all(x, axis, split_axis=0, concat_axis=0, tiled=True)  39.5 us
    all_to_all x3, starting transfers between devices, exchange(): return lax.all_to_all(x, axis, split_axis=0, concat_axis=0, tiled=True)  14.9 us
    pallas_call x1, Pallas kernels, shards(): pl.pallas_call(functools.partial(split_body, n), grid=(n // group,), in_s...  13.1 us
  transfers between devices with their start and end apart: 17, of which 13 were waited for; matrix products, arithmetic and copies ran while one was open for 0% of the time, Pallas kernels for 20%

profile of v4, /device:TPU:1, one launch (start us, length us, event | category | flops | bytes accessed | tf_op | source)
XLA Modules:
  0.0 603.4 jit_solution(415765542801998958)
XLA Ops:
  6.5 10.6 %shard_map.46 = (f32[1600,800]{1,0:T(8,128)}, f32[8,8,20000]{2,1,0:T(8,128)}) custom-call(f32[800,1600]{1,0:T(8,128)} %x_ref.3), custom_call_target="tpu_custom_call" | custom-call | bytes 15360000 | tf_op jit(solution)/shard_map/pallas_call | solution.py:35
  17.1 0.8 reshape.11
  17.9 0.0 all-gather.4.cloned.1.call-update
  17.9 0.0 all-gather.6.cloned.1.call-start
  18.0 63.3 %all-gather.4.cloned.1.call-done = f32[1600,512]{1,0:T(8,128)} async-done(((f32[200,512]{1,0:T(8,128)}), f32[1600,512]{1,0:T(8,128)}) %all-gather.4.cloned.1.call-update) | async-done | bytes 3276816 | tf_op jit(solution)/shard_map/all_gather | solution.py:304
  81.3 0.0 all-gather.6.cloned.1.call-update
  81.3 0.0 copy-start.4
  81.3 4.7 all-to-all-start
  86.0 0.1 copy.5
  86.1 0.7 pad_maximum_fusion
  86.9 81.0 %all-gather.6.cloned.1.call-done = f32[6400,512]{1,0:T(8,128)} async-done(((f32[1600,512]{1,0:T(8,128)}), f32[6400,512]{1,0:T(8,128)}) %all-gather.6.cloned.1.call-update) | async-done | bytes 13107216 | tf_op jit(solution)/shard_map/all_gather | solution.py:305
  167.8 6.8 %shard_map.47 = (f32[8,40000]{1,0:T(8,128)}, f32[8,40000]{1,0:T(8,128)}, f32[8,40000]{1,0:T(8,128)}, f32[8,40000]{1,0:T(8,128)}) custom-call(s32[1]{0:T(128)} %bitcast.me_ref.refs_0_, f32[1600,800]{1,0:T(8,128)} %get-tuple-element.41.x_ref), custom_call_target="tpu_custom_call" | custom-call | bytes 10240000 | tf_op jit(solution)/shard_map/pallas_call | solution.py:35
  174.6 13.1 %shard_map.48 = (bf16[6400,512]{1,0:T(8,128)(2,1)}, bf16[6400,512]{1,0:T(8,128)(2,1)}) custom-call(f32[4,1600,512]{2,1,0:T(8,128)} %bitcast.7), custom_call_target="tpu_custom_call" | custom-call | flops 6553600 | bytes 26214400 | tf_op jit(solution)/shard_map/pallas_call | solution.py:313
  187.7 10.3 %all-to-all-done.refs_0_ = f32[8,8,20000]{2,1,0:T(8,128)} async-done(((f32[8,8,20000]{2,1,0:T(8,128)}), f32[8,8,20000]{2,1,0:T(8,128)}, u32[]{:S(2)}, u32[]{:S(2)}) %all-to-all-start) | async-done | bytes 5120032 | tf_op jit(solution)/shard_map/all_to_all | solution.py:275
  198.1 33.6 %shard_map.49 = (f32[8,200,800]{2,1,0:T(8,128)}, f32[8,8,10400]{2,1,0:T(8,128)}, f32[8,24,3200]{2,1,0:T(8,128)}) custom-call(f32[8,8,20000]{2,1,0:T(8,128)} %all-to-all-done.refs_0_, bf16[6400,512]{1,0:T(8,128)(2,1)} %get-tuple-element.47.refs_1_.refs_0_.refs_5_.refs_10_, bf16[6400,512]{1,0:T(8,128)(2,1)} %get-tuple-element.48.refs_2_.refs_1_.refs_6_.refs_11_, ...), custom_call_target="tpu_custom_call" | custom-call | flops 9093120000 | bytes 28467200 | tf_op jit(solution)/shard_map/pallas_call | solution.py:35
  231.7 5.5 all-to-all-start.1
  237.2 31.0 %shard_map.50 = f32[8,8,20000]{2,1,0:T(8,128)} custom-call(f32[8,200,800]{2,1,0:T(8,128)} %get-tuple-element.49.x_ref, bf16[6400,512]{1,0:T(8,128)(2,1)} %get-tuple-element.47.refs_1_.refs_0_.refs_5_.refs_10_, bf16[6400,512]{1,0:T(8,128)(2,1)} %get-tuple-element.48.refs_2_.refs_1_.refs_6_.refs_11_, f32[1,512]{1,0:T(1,128)} %bitcast.9, ...), custom_call_target="tpu_custom_call" | custom-call | flops 9093120000 | bytes 28467200 | tf_op jit(solution)/shard_map/pallas_call | solution.py:35
  268.2 29.1 %all-to-all-done.1.x_ref = f32[8,8,10400]{2,1,0:T(8,128)S(1)} async-done(((f32[8,8,10400]{2,1,0:T(8,128)}), f32[8,8,10400]{2,1,0:T(8,128)S(1)}, u32[]{:S(2)}, u32[]{:S(2)}) %all-to-all-start.1) | async-done | bytes 2662432 | tf_op jit(solution)/shard_map/all_to_all | solution.py:275
  297.4 59.9 %all_to_all.20.x_ref = f32[8,24,3200]{2,1,0:T(8,128)} all-to-all(f32[8,24,3200]{2,1,0:T(8,128)} %get-tuple-element.52), channel_id=1, replica_groups=mesh['row'=8,'col'=4] {'row'}, dimensions={0} | all-to-all | bytes 4915200 | tf_op jit(solution)/shard_map/all_to_all | solution.py:275
  357.3 4.8 all-to-all-start.3
  362.0 3.2 collective-permute-start
  365.3 0.3 collective-permute-start.1
  365.6 0.2 collective-permute-start.2
  365.7 0.5 neg.13
  366.3 26.7 %collective-permute-done.refs_2_ = f32[8,40000]{1,0:T(8,128)S(1)} collective-permute-done((f32[8,40000]{1,0:T(8,128)}, f32[8,40000]{1,0:T(8,128)S(1)}, u32[]{:S(2)}, u32[]{:S(2)}) %collective-permute-start) | collective-permute-done | bytes 1280032 | tf_op jit(solution)/shard_map/ppermute | solution.py:266
  393.0 28.5 %collective-permute-done.1.refs_3_ = f32[8,40000]{1,0:T(8,128)S(1)} collective-permute-done((f32[8,40000]{1,0:T(8,128)}, f32[8,40000]{1,0:T(8,128)S(1)}, u32[]{:S(2)}, u32[]{:S(2)}) %collective-permute-start.1) | collective-permute-done | bytes 1280032 | tf_op jit(solution)/shard_map/ppermute | solution.py:266
  421.5 0.6 collective-permute-done.2.refs_4_
  422.1 5.0 shard_map.52
  427.1 0.0 collective-permute-start.3
  427.1 1.2 collective-permute-start.4
  428.3 0.8 collective-permute-start.5
  429.1 28.3 %shard_map.51.refs_1_ = f32[4,200,1600]{2,1,0:T(8,128)} custom-call(s32[1]{0:T(128)} %bitcast.me_ref.refs_0_, f32[8,40000]{1,0:T(8,128)} %get-tuple-element.54.refs_1_, f32[8,40000]{1,0:T(8,128)} %copy-done.6, f32[8,40000]{1,0:T(8,128)} %copy-done.7, f32[8,40000]{1,0:T(8,128)} %collective-permute-done.2.refs_4_, ...), custom_call_target="tpu_custom_call" | custom-call | flops 9093120000 | bytes 28467200 | tf_op jit(solution)/shard_map/pallas_call | solution.py:35
  457.3 4.7 shard_map.53
  462.0 1.0 collective-permute-start.6
  463.0 0.4 collective-permute-start.7
  463.4 0.0 collective-permute-done.3.refs_3_
  463.4 0.2 collective-permute-start.8
  463.6 12.8 %collective-permute-done.6.refs_7_ = f32[200,768]{1,0:T(8,128)S(1)} collective-permute-done((f32[200,768]{1,0:T(8,128)}, f32[200,768]{1,0:T(8,128)S(1)}, u32[]{:S(2)}, u32[]{:S(2)}) %collective-permute-start.6) | collective-permute-done | bytes 614432 | tf_op jit(solution)/shard_map/ppermute | solution.py:266
  476.5 13.4 %collective-permute-done.7.refs_8_ = f32[200,768]{1,0:T(8,128)S(1)} collective-permute-done((f32[200,768]{1,0:T(8,128)}, f32[200,768]{1,0:T(8,128)S(1)}, u32[]{:S(2)}, u32[]{:S(2)}) %collective-permute-start.7) | collective-permute-done | bytes 614432 | tf_op jit(solution)/shard_map/ppermute | solution.py:266
  489.8 1.1 collective-permute-done.8.refs_9_
  490.9 0.8 copy-done.12
  491.7 32.6 %shard_map.54 = (f32[8,40000]{1,0:T(8,128)}, f32[8,40000]{1,0:T(8,128)}, f32[8,40000]{1,0:T(8,128)}, f32[8,40000]{1,0:T(8,128)}) custom-call(s32[1]{0:T(128)} %bitcast.me_ref.refs_0_, f32[4,200,1600]{2,1,0:T(8,128)} %shard_map.51.refs_1_, f32[8,20800]{1,0:T(8,128)} %get-tuple-element.58.refs_2_, f32[8,20800]{1,0:T(8,128)} %copy-done.8, ...), custom_call_target="tpu_custom_call" | custom-call | flops 9093120000 | bytes 28467200 | tf_op jit(solution)/shard_map/pallas_call | solution.py:35
  524.3 1.1 collective-permute-start.10
  525.4 0.9 collective-permute-start.11
  526.4 24.1 %collective-permute-done.9.refs_1_ = f32[8,40000]{1,0:T(8,128)S(1)} collective-permute-done((f32[8,40000]{1,0:T(8,128)}, f32[8,40000]{1,0:T(8,128)S(1)}, u32[]{:S(2)}, u32[]{:S(2)}) %collective-permute-start.9) | collective-permute-done | bytes 1280032 | tf_op jit(solution)/shard_map/ppermute | solution.py:266
  550.5 29.6 %collective-permute-done.10.refs_2_ = f32[8,40000]{1,0:T(8,128)S(1)} collective-permute-done((f32[8,40000]{1,0:T(8,128)}, f32[8,40000]{1,0:T(8,128)S(1)}, u32[]{:S(2)}, u32[]{:S(2)}) %collective-permute-start.10) | collective-permute-done | bytes 1280032 | tf_op jit(solution)/shard_map/ppermute | solution.py:266
  580.0 1.5 collective-permute-done.11.refs_3_
  581.6 14.6 %shard_map.55 = f32[800,1600]{1,0:T(8,128)} custom-call(s32[1]{0:T(128)} %bitcast.me_ref.refs_0_, f32[800,1600]{1,0:T(8,128)} %x_ref.3, f32[8,8,20000]{2,1,0:T(8,128)} %all-to-all-done.3.crossed_ref, f32[8,40000]{1,0:T(8,128)} %get-tuple-element.67.refs_0_, f32[8,40000]{1,0:T(8,128)} %copy-done.1, f32[8,40000]{1,0:T(8,128)} %copy-done.2, ...), custom_call_target="tpu_custom_call" | custom-call | bytes 20480000 | tf_op jit(solution)/shard_map/pallas_call | solution.py:35
  (31 shorter events, 0.1 us)
Async XLA Ops:
  6.5 10.6 %copy-start.3 = (f32[10,20,512]{2,1,0:T(8,128)S(1)}, f32[10,20,512]{2,1,0:T(8,128)}, u32[]{:S(2)}) copy-start(f32[10,20,512]{2,1,0:T(8,128)} %param.6) | copy-start | bytes 1228804
  6.5 74.7 %all-gather.4.cloned.1.call-start = ((), (), s32[]{:S(2)}) async-start(), calls=%async_computation.4 | async-start | bytes 3686400 | tf_op jit(solution)/shard_map/all_gather | solution.py:304
  17.9 149.9 %all-gather.6.cloned.1.call-start = ((), (), s32[]{:S(2)}) async-start(), calls=%async_computation.5 | async-start | bytes 16384000 | tf_op jit(solution)/shard_map/all_gather | solution.py:305
  81.3 4.7 copy-start.4
  81.3 116.8 %all-to-all-start = ((f32[8,8,20000]{2,1,0:T(8,128)}), f32[8,8,20000]{2,1,0:T(8,128)}, u32[]{:S(2)}, u32[]{:S(2)}) async-start(f32[8,8,20000]{2,1,0:T(8,128)} %get-tuple-element.38), calls=%async_computation | async-start | bytes 10289152 | tf_op jit(solution)/shard_map/all_to_all | solution.py:275
  231.7 65.7 %all-to-all-start.1 = ((f32[8,8,10400]{2,1,0:T(8,128)}), f32[8,8,10400]{2,1,0:T(8,128)S(1)}, u32[]{:S(2)}, u32[]{:S(2)}) async-start(f32[8,8,10400]{2,1,0:T(8,128)} %get-tuple-element.51), calls=%async_computation.1 | async-start | bytes 5373952 | tf_op jit(solution)/shard_map/all_to_all | solution.py:275
  297.4 59.9 %copy-start = (f32[8,8,10400]{2,1,0:T(8,128)}, f32[8,8,10400]{2,1,0:T(8,128)S(1)}, u32[]{:S(2)}) copy-start(f32[8,8,10400]{2,1,0:T(8,128)S(1)} %all-to-all-done.1.x_ref) | copy-start | bytes 7987204
  357.3 8.5 %copy-start.5 = (f32[512]{0:T(512)S(1)}, f32[512]{0:T(512)}, u32[]{:S(2)}) copy-start(f32[512]{0:T(512)} %param.7) | copy-start | bytes 6148
  357.3 224.3 %all-to-all-start.3 = ((f32[8,8,20000]{2,1,0:T(8,128)}), f32[8,8,20000]{2,1,0:T(8,128)}, u32[]{:S(2)}, u32[]{:S(2)}) async-start(f32[8,8,20000]{2,1,0:T(8,128)} %shard_map.50), calls=%async_computation.3 | async-start | bytes 10289152 | tf_op jit(solution)/shard_map/all_to_all | solution.py:275
  362.0 30.9 %collective-permute-start = (f32[8,40000]{1,0:T(8,128)}, f32[8,40000]{1,0:T(8,128)S(1)}, u32[]{:S(2)}, u32[]{:S(2)}) collective-permute-start(f32[8,40000]{1,0:T(8,128)} %get-tuple-element.43), channel_id=1, source_target_pairs={{0,1},{1,2},{2,3},{3,0},{4,5},{5,6},{6,7},{7,4},{8,9},{9,10},{10,1... | collective-permute-start | bytes 3840008 | tf_op jit(solution)/shard_map/ppermute | solution.py:266
  365.3 56.2 %collective-permute-start.1 = (f32[8,40000]{1,0:T(8,128)}, f32[8,40000]{1,0:T(8,128)S(1)}, u32[]{:S(2)}, u32[]{:S(2)}) collective-permute-start(f32[8,40000]{1,0:T(8,128)} %get-tuple-element.44), channel_id=1, source_target_pairs={{0,2},{1,3},{2,0},{3,1},{4,6},{5,7},{6,4},{7,5},{8,10},{9,11},{10,... | collective-permute-start | bytes 3840008 | tf_op jit(solution)/shard_map/ppermute | solution.py:266
  365.6 56.5 %collective-permute-start.2 = (f32[8,40000]{1,0:T(8,128)}, f32[8,40000]{1,0:T(8,128)}, u32[]{:S(2)}, u32[]{:S(2)}) collective-permute-start(f32[8,40000]{1,0:T(8,128)} %get-tuple-element.45), channel_id=1, source_target_pairs={{0,3},{1,0},{2,1},{3,2},{4,7},{5,4},{6,5},{7,6},{8,11},{9,8},{10,9... | collective-permute-start | bytes 3840008 | tf_op jit(solution)/shard_map/ppermute | solution.py:266
  393.0 36.1 %copy-start.6 = (f32[8,40000]{1,0:T(8,128)}, f32[8,40000]{1,0:T(8,128)S(1)}, u32[]{:S(2)}) copy-start(f32[8,40000]{1,0:T(8,128)S(1)} %collective-permute-done.refs_2_) | copy-start | bytes 3840004
  421.5 7.6 %copy-start.7 = (f32[8,40000]{1,0:T(8,128)}, f32[8,40000]{1,0:T(8,128)S(1)}, u32[]{:S(2)}) copy-start(f32[8,40000]{1,0:T(8,128)S(1)} %collective-permute-done.1.refs_3_) | copy-start | bytes 3840004
  427.1 36.3 %collective-permute-start.3 = (f32[8,20800]{1,0:T(8,128)}, f32[8,20800]{1,0:T(8,128)S(1)}, u32[]{:S(2)}, u32[]{:S(2)}) collective-permute-start(f32[8,20800]{1,0:T(8,128)} %get-tuple-element.59), channel_id=1, source_target_pairs={{0,1},{1,2},{2,3},{3,0},{4,5},{5,6},{6,7},{7,4},{8,9},{9,10},{10,1... | collective-permute-start | bytes 1996808 | tf_op jit(solution)/shard_map/ppermute | solution.py:266
  427.1 36.5 %collective-permute-start.4 = (f32[8,20800]{1,0:T(8,128)}, f32[8,20800]{1,0:T(8,128)S(1)}, u32[]{:S(2)}, u32[]{:S(2)}) collective-permute-start(f32[8,20800]{1,0:T(8,128)} %get-tuple-element.60), channel_id=1, source_target_pairs={{0,2},{1,3},{2,0},{3,1},{4,6},{5,7},{6,4},{7,5},{8,10},{9,11},{10,... | collective-permute-start | bytes 1996808 | tf_op jit(solution)/shard_map/ppermute | solution.py:266
  428.3 35.4 %collective-permute-start.5 = (f32[8,20800]{1,0:T(8,128)}, f32[8,20800]{1,0:T(8,128)}, u32[]{:S(2)}, u32[]{:S(2)}) collective-permute-start(f32[8,20800]{1,0:T(8,128)} %get-tuple-element.61), channel_id=1, source_target_pairs={{0,3},{1,0},{2,1},{3,2},{4,7},{5,4},{6,5},{7,6},{8,11},{9,8},{10,9... | collective-permute-start | bytes 1996808 | tf_op jit(solution)/shard_map/ppermute | solution.py:266
  462.0 14.4 %collective-permute-start.6 = (f32[200,768]{1,0:T(8,128)}, f32[200,768]{1,0:T(8,128)S(1)}, u32[]{:S(2)}, u32[]{:S(2)}) collective-permute-start(f32[200,768]{1,0:T(8,128)} %get-tuple-element.64), channel_id=1, source_target_pairs={{0,1},{1,2},{2,3},{3,0},{4,5},{5,6},{6,7},{7,4},{8,9},{9,10},{10,1... | collective-permute-start | bytes 1843208 | tf_op jit(solution)/shard_map/ppermute | solution.py:266
  463.0 26.8 %collective-permute-start.7 = (f32[200,768]{1,0:T(8,128)}, f32[200,768]{1,0:T(8,128)S(1)}, u32[]{:S(2)}, u32[]{:S(2)}) collective-permute-start(f32[200,768]{1,0:T(8,128)} %get-tuple-element.65), channel_id=1, source_target_pairs={{0,2},{1,3},{2,0},{3,1},{4,6},{5,7},{6,4},{7,5},{8,10},{9,11},{10,... | collective-permute-start | bytes 1843208 | tf_op jit(solution)/shard_map/ppermute | solution.py:266
  463.4 27.5 %copy-start.8 = (f32[8,20800]{1,0:T(8,128)}, f32[8,20800]{1,0:T(8,128)S(1)}, u32[]{:S(2)}) copy-start(f32[8,20800]{1,0:T(8,128)S(1)} %collective-permute-done.3.refs_3_) | copy-start | bytes 1996804
  463.4 27.5 %collective-permute-start.8 = (f32[200,768]{1,0:T(8,128)}, f32[200,768]{1,0:T(8,128)S(1)}, u32[]{:S(2)}, u32[]{:S(2)}) collective-permute-start(f32[200,768]{1,0:T(8,128)} %get-tuple-element.66), channel_id=1, source_target_pairs={{0,3},{1,0},{2,1},{3,2},{4,7},{5,4},{6,5},{7,6},{8,11},{9,8},{10,9... | collective-permute-start | bytes 1843208 | tf_op jit(solution)/shard_map/ppermute | solution.py:266
  463.6 27.3 %copy-start.9 = (f32[8,20800]{1,0:T(8,128)}, f32[8,20800]{1,0:T(8,128)S(1)}, u32[]{:S(2)}) copy-start(f32[8,20800]{1,0:T(8,128)S(1)} %collective-permute-done.4.refs_4_) | copy-start | bytes 1996804
  476.5 14.5 %copy-start.10 = (f32[200,768]{1,0:T(8,128)}, f32[200,768]{1,0:T(8,128)S(1)}, u32[]{:S(2)}) copy-start(f32[200,768]{1,0:T(8,128)S(1)} %collective-permute-done.6.refs_7_) | copy-start | bytes 1843204
  489.8 1.1 copy-start.11
  490.9 0.8 copy-start.12
  524.3 26.2 %collective-permute-start.9 = (f32[8,40000]{1,0:T(8,128)}, f32[8,40000]{1,0:T(8,128)S(1)}, u32[]{:S(2)}, u32[]{:S(2)}) collective-permute-start(f32[8,40000]{1,0:T(8,128)} %get-tuple-element.68), channel_id=1, source_target_pairs={{0,1},{1,2},{2,3},{3,0},{4,5},{5,6},{6,7},{7,4},{8,9},{9,10},{10,1... | collective-permute-start | bytes 3840008 | tf_op jit(solution)/shard_map/ppermute | solution.py:266
  524.3 55.8 %collective-permute-start.10 = (f32[8,40000]{1,0:T(8,128)}, f32[8,40000]{1,0:T(8,128)S(1)}, u32[]{:S(2)}, u32[]{:S(2)}) collective-permute-start(f32[8,40000]{1,0:T(8,128)} %get-tuple-element.69), channel_id=1, source_target_pairs={{0,2},{1,3},{2,0},{3,1},{4,6},{5,7},{6,4},{7,5},{8,10},{9,11},{10,... | collective-permute-start | bytes 3840008 | tf_op jit(solution)/shard_map/ppermute | solution.py:266
  525.4 56.1 %collective-permute-start.11 = (f32[8,40000]{1,0:T(8,128)}, f32[8,40000]{1,0:T(8,128)}, u32[]{:S(2)}, u32[]{:S(2)}) collective-permute-start(f32[8,40000]{1,0:T(8,128)} %get-tuple-element.70), channel_id=1, source_target_pairs={{0,3},{1,0},{2,1},{3,2},{4,7},{5,4},{6,5},{7,6},{8,11},{9,8},{10,9... | collective-permute-start | bytes 3840008 | tf_op jit(solution)/shard_map/ppermute | solution.py:266
  550.5 31.1 %copy-start.1 = (f32[8,40000]{1,0:T(8,128)}, f32[8,40000]{1,0:T(8,128)S(1)}, u32[]{:S(2)}) copy-start(f32[8,40000]{1,0:T(8,128)S(1)} %collective-permute-done.9.refs_1_) | copy-start | bytes 3840004
  580.0 1.5 copy-start.2
Sparse Core Ops, SparseCore 0:
  18.1 63.1 all-gather.3
  82.8 84.9 all-gather.5

commit v5 on v4

--- a/solution.py
+++ b/solution.py
@@ -302,12 +302,10 @@
 
     aux = after(aux, mine)
     whole = lax.all_gather(aux.reshape(-1, naux), "row", axis=0, tiled=True)
-    whole = lax.all_gather(whole, "col", axis=0, tiled=False)
     mine = exchange(mine, "row")
-    turned = call(
-        turn_body, col_wires(local_cols), [me, after(crossed, whole)], [col_stage], moved=8 * size
-    )
+    turned = call(turn_body, col_wires(local_cols), [me, crossed], [col_stage], moved=8 * size)
     theirs = shift(turned, "col")
+    whole = lax.all_gather(after(whole, theirs), "col", axis=0, tiled=False)
     group = 8 if n % 8 == 0 else n
     shape = jax.ShapeDtypeStruct((n * n, naux), bf16)
     high, low = pl.pallas_call(
@@ -343,7 +341,7 @@
 
     first, *parts = operator(
         lambda n, *refs: left_body(n, spans, *refs),
-        [after(mine, turned)], row_consts,
+        [mine], row_consts,
         [jax.ShapeDtypeStruct(row_block, f32)] + [row_wire(b - a) for a, b in spans], row_block,
     )
     double = operator(left_again_body, [first], row_consts, row_wire(row_block[1]), row_block)
@@ -353,10 +351,11 @@
     )
     arriving, part = [], double
     for h, (start, stop) in enumerate(spans):
-        part = exchange(after(parts[h], (part, double)) if h else parts[h], "row")
+        part = exchange(after(parts[h], (part, base)) if h else parts[h], "row")
         if h + 1 == len(spans):
             double = after(double, part)
-            part = after(part, base)
+        if h:
+            part = after(part, turned)
         turned = call(
             turn_arriving_body, col_wires(rows * (stop - start)), [me, part],
             [

time: 612 us -> 554 us (0.905)
  waiting for transfers between devices: 322 us -> 257 us
    all_gather x1, waiting for transfers between devices: 63.3 us -> 0.01 us  [shards(): whole = lax.all_gather(aux.reshape(-1, naux), 'row', axis=0, tiled=True)]
    all_to_all x3, waiting for transfers between devices: 39.5 us -> 20.3 us  [exchange(): return lax.all_to_all(x, axis, split_axis=0, concat_axis=0, tiled=True)]
    ppermute x12, waiting for transfers between devices: 138 us -> 157 us  [shift(): lax.ppermute(parts[s], axis, [(d, (d + s) % n) for d in range(n)])]
  transfers between devices with their start and end apart: 17 -> 17, of which waited for: 13 -> 14; matrix products, arithmetic and copies ran while one was open for 0% -> 0% of each run, Pallas kernels for 20% -> 22%
where the time goes in v5:
time: 554 us; the launch traced here: 545 us
  waiting for transfers between devices  257 us (46%)
  Pallas kernels  180 us (32%)
  blocking collectives  60.5 us (11%)
  starting transfers between devices  29 us (5%)
  between operations  14 us (3%)
    pallas_call x9, Pallas kernels, call(): pl.pallas_call(body, in_specs=[smem if x.dtype == jnp.int32 else vmem for...  167 us
    ppermute x12, waiting for transfers between devices, shift(): lax.ppermute(parts[s], axis, [(d, (d + s) % n) for d in range(n)])  157 us
    all_gather x1, waiting for transfers between devices, shards(): whole = lax.all_gather(after(whole, theirs), 'col', axis=0, tiled=False)  80 us
    all_to_all x1, blocking collectives, exchange(): return lax.all_to_all(x, axis, split_axis=0, concat_axis=0, tiled=True)  60.5 us
    all_to_all x3, waiting for transfers between devices, exchange(): return lax.all_to_all(x, axis, split_axis=0, concat_axis=0, tiled=True)  20.3 us
    all_to_all x3, starting transfers between devices, exchange(): return lax.all_to_all(x, axis, split_axis=0, concat_axis=0, tiled=True)  15 us
    ppermute x12, starting transfers between devices, shift(): lax.ppermute(parts[s], axis, [(d, (d + s) % n) for d in range(n)])  14 us
    pallas_call x1, Pallas kernels, shards(): pl.pallas_call(functools.partial(split_body, n), grid=(n // group,), in_s...  13.1 us
  transfers between devices with their start and end apart: 17, of which 14 were waited for; matrix products, arithmetic and copies ran while one was open for 0% of the time, Pallas kernels for 22%

profile of v5, /device:TPU:1, one launch (start us, length us, event | category | flops | bytes accessed | tf_op | source)
XLA Modules:
  0.0 545.2 jit_solution(18384360701657369431)
XLA Ops:
  6.5 10.6 %shard_map.46 = (f32[1600,800]{1,0:T(8,128)}, f32[8,8,20000]{2,1,0:T(8,128)}) custom-call(f32[800,1600]{1,0:T(8,128)} %x_ref.3), custom_call_target="tpu_custom_call" | custom-call | bytes 15360000 | tf_op jit(solution)/shard_map/pallas_call | solution.py:35
  17.1 0.8 reshape.11
  17.9 0.0 all-gather.4.cloned.1.call-update
  18.0 0.0 all-gather.6.cloned.1.call-start
  18.0 6.9 %shard_map.47 = (f32[8,40000]{1,0:T(8,128)}, f32[8,40000]{1,0:T(8,128)}, f32[8,40000]{1,0:T(8,128)}, f32[8,40000]{1,0:T(8,128)}) custom-call(s32[1]{0:T(128)} %bitcast.me_ref.refs_0_, f32[1600,800]{1,0:T(8,128)} %get-tuple-element.39.x_ref), custom_call_target="tpu_custom_call" | custom-call | bytes 10240000 | tf_op jit(solution)/shard_map/pallas_call | solution.py:35
  24.9 2.6 collective-permute-start
  27.5 0.4 collective-permute-start.2
  27.9 27.3 %collective-permute-done.refs_2_ = f32[8,40000]{1,0:T(8,128)} collective-permute-done((f32[8,40000]{1,0:T(8,128)}, f32[8,40000]{1,0:T(8,128)}, u32[]{:S(2)}, u32[]{:S(2)}) %collective-permute-start) | collective-permute-done | bytes 1280032 | tf_op jit(solution)/shard_map/ppermute | solution.py:266
  55.3 27.5 %collective-permute-done.1.refs_3_ = f32[8,40000]{1,0:T(8,128)} collective-permute-done((f32[8,40000]{1,0:T(8,128)}, f32[8,40000]{1,0:T(8,128)}, u32[]{:S(2)}, u32[]{:S(2)}) %collective-permute-start.1) | collective-permute-done | bytes 1280032 | tf_op jit(solution)/shard_map/ppermute | solution.py:266
  82.7 0.5 collective-permute-done.2.refs_4_
  83.2 0.0 all-gather.6.cloned.1.call-update
  83.3 0.0 copy-start.4
  83.3 6.3 %all-to-all-start = ((f32[8,8,20000]{2,1,0:T(8,128)}), f32[8,8,20000]{2,1,0:T(8,128)}, u32[]{:S(2)}, u32[]{:S(2)}) async-start(f32[8,8,20000]{2,1,0:T(8,128)} %get-tuple-element.37), calls=%async_computation | async-start | bytes 10289152 | tf_op jit(solution)/shard_map/all_to_all | solution.py:275
  89.6 0.1 copy.5
  89.7 0.7 pad_maximum_fusion
  90.4 80.0 %all-gather.6.cloned.1.call-done = f32[6400,512]{1,0:T(8,128)} async-done(((f32[1600,512]{1,0:T(8,128)}), f32[6400,512]{1,0:T(8,128)}) %all-gather.6.cloned.1.call-update) | async-done | bytes 13107216 | tf_op jit(solution)/shard_map/all_gather | solution.py:308
  170.4 13.1 %shard_map.48 = (bf16[6400,512]{1,0:T(8,128)(2,1)}, bf16[6400,512]{1,0:T(8,128)(2,1)}) custom-call(f32[4,1600,512]{2,1,0:T(8,128)} %bitcast.7), custom_call_target="tpu_custom_call" | custom-call | flops 6553600 | bytes 26214400 | tf_op jit(solution)/shard_map/pallas_call | solution.py:311
  183.5 19.9 %all-to-all-done.refs_0_ = f32[8,8,20000]{2,1,0:T(8,128)} async-done(((f32[8,8,20000]{2,1,0:T(8,128)}), f32[8,8,20000]{2,1,0:T(8,128)}, u32[]{:S(2)}, u32[]{:S(2)}) %all-to-all-start) | async-done | bytes 5120032 | tf_op jit(solution)/shard_map/all_to_all | solution.py:275
  203.4 33.6 %shard_map.49 = (f32[8,200,800]{2,1,0:T(8,128)}, f32[8,8,10400]{2,1,0:T(8,128)}, f32[8,24,3200]{2,1,0:T(8,128)}) custom-call(f32[8,8,20000]{2,1,0:T(8,128)} %all-to-all-done.refs_0_, bf16[6400,512]{1,0:T(8,128)(2,1)} %get-tuple-element.45.refs_1_.refs_0_.refs_5_.refs_10_, bf16[6400,512]{1,0:T(8,128)(2,1)} %get-tuple-element.46.refs_2_.refs_1_.refs_6_.refs_11_, ...), custom_call_target="tpu_custom_call" | custom-call | flops 9093120000 | bytes 28467200 | tf_op jit(solution)/shard_map/pallas_call | solution.py:35
  237.0 4.0 all-to-all-start.1
  241.0 0.6 neg.13
  241.6 31.0 %shard_map.50 = f32[8,8,20000]{2,1,0:T(8,128)} custom-call(f32[8,200,800]{2,1,0:T(8,128)} %get-tuple-element.47.x_ref, bf16[6400,512]{1,0:T(8,128)(2,1)} %get-tuple-element.45.refs_1_.refs_0_.refs_5_.refs_10_, bf16[6400,512]{1,0:T(8,128)(2,1)} %get-tuple-element.46.refs_2_.refs_1_.refs_6_.refs_11_, f32[1,512]{1,0:T(1,128)} %bitcast.9, ...), custom_call_target="tpu_custom_call" | custom-call | flops 9093120000 | bytes 28467200 | tf_op jit(solution)/shard_map/pallas_call | solution.py:35
  272.7 28.3 %shard_map.51.refs_1_ = f32[4,200,1600]{2,1,0:T(8,128)} custom-call(s32[1]{0:T(128)} %bitcast.me_ref.refs_0_, f32[8,40000]{1,0:T(8,128)} %get-tuple-element.50.refs_1_, f32[8,40000]{1,0:T(8,128)} %collective-permute-done.refs_2_, f32[8,40000]{1,0:T(8,128)} %collective-permute-done.1.refs_3_, f32[8,40000]{1,0:T(8,128)} %collective-permute-done.2.refs_4_, ...), custom_call_target="tpu_custom_call" | custom-call | flops 9093120000 | bytes 28467200 | tf_op jit(solution)/shard_map/pallas_call | solution.py:35
  300.9 0.4 all-to-all-done.1.x_ref
  301.3 60.5 %all_to_all.20.x_ref = f32[8,24,3200]{2,1,0:T(8,128)} all-to-all(f32[8,24,3200]{2,1,0:T(8,128)} %get-tuple-element.54), channel_id=1, replica_groups=mesh['row'=8,'col'=4] {'row'}, dimensions={0} | all-to-all | bytes 4915200 | tf_op jit(solution)/shard_map/all_to_all | solution.py:275
  361.8 4.6 all-to-all-start.3
  366.4 5.0 shard_map.52
  371.4 3.0 collective-permute-start.3
  374.4 0.4 collective-permute-start.4
  374.9 4.7 shard_map.53
  379.6 1.8 collective-permute-start.6
  381.4 1.0 collective-permute-start.7
  382.4 6.6 %collective-permute-done.3.refs_3_ = f32[8,20800]{1,0:T(8,128)S(1)} collective-permute-done((f32[8,20800]{1,0:T(8,128)}, f32[8,20800]{1,0:T(8,128)S(1)}, u32[]{:S(2)}, u32[]{:S(2)}) %collective-permute-start.3) | collective-permute-done | bytes 665632 | tf_op jit(solution)/shard_map/ppermute | solution.py:266
  389.0 1.6 collective-permute-start.8
  390.7 13.8 %collective-permute-done.4.refs_4_ = f32[8,20800]{1,0:T(8,128)S(1)} collective-permute-done((f32[8,20800]{1,0:T(8,128)}, f32[8,20800]{1,0:T(8,128)S(1)}, u32[]{:S(2)}, u32[]{:S(2)}) %collective-permute-start.4) | collective-permute-done | bytes 665632 | tf_op jit(solution)/shard_map/ppermute | solution.py:266
  404.5 1.1 collective-permute-done.5.refs_5_
  405.6 10.9 %collective-permute-done.6.refs_7_ = f32[200,768]{1,0:T(8,128)S(1)} collective-permute-done((f32[200,768]{1,0:T(8,128)}, f32[200,768]{1,0:T(8,128)S(1)}, u32[]{:S(2)}, u32[]{:S(2)}) %collective-permute-start.6) | collective-permute-done | bytes 614432 | tf_op jit(solution)/shard_map/ppermute | solution.py:266
  416.5 14.3 %collective-permute-done.7.refs_8_ = f32[200,768]{1,0:T(8,128)S(1)} collective-permute-done((f32[200,768]{1,0:T(8,128)}, f32[200,768]{1,0:T(8,128)S(1)}, u32[]{:S(2)}, u32[]{:S(2)}) %collective-permute-start.7) | collective-permute-done | bytes 614432 | tf_op jit(solution)/shard_map/ppermute | solution.py:266
  430.8 0.6 collective-permute-done.8.refs_9_
  431.4 0.3 copy-done.10
  431.7 0.5 copy-done.11
  432.2 32.7 %shard_map.54 = (f32[8,40000]{1,0:T(8,128)}, f32[8,40000]{1,0:T(8,128)}, f32[8,40000]{1,0:T(8,128)}, f32[8,40000]{1,0:T(8,128)}) custom-call(s32[1]{0:T(128)} %bitcast.me_ref.refs_0_, f32[4,200,1600]{2,1,0:T(8,128)} %shard_map.51.refs_1_, f32[8,20800]{1,0:T(8,128)} %get-tuple-element.56.refs_2_, f32[8,20800]{1,0:T(8,128)} %copy-done.6, ...), custom_call_target="tpu_custom_call" | custom-call | flops 9093120000 | bytes 28467200 | tf_op jit(solution)/shard_map/pallas_call | solution.py:35
  464.9 1.0 collective-permute-start.10
  465.9 2.0 collective-permute-start.9
  467.9 27.1 %collective-permute-done.10.refs_2_ = f32[8,40000]{1,0:T(8,128)S(1)} collective-permute-done((f32[8,40000]{1,0:T(8,128)}, f32[8,40000]{1,0:T(8,128)S(1)}, u32[]{:S(2)}, u32[]{:S(2)}) %collective-permute-start.10) | collective-permute-done | bytes 1280032 | tf_op jit(solution)/shard_map/ppermute | solution.py:266
  495.0 27.3 %collective-permute-done.11.refs_3_ = f32[8,40000]{1,0:T(8,128)S(1)} collective-permute-done((f32[8,40000]{1,0:T(8,128)}, f32[8,40000]{1,0:T(8,128)S(1)}, u32[]{:S(2)}, u32[]{:S(2)}) %collective-permute-start.11) | collective-permute-done | bytes 1280032 | tf_op jit(solution)/shard_map/ppermute | solution.py:266
  522.3 1.1 copy-done.2
  523.3 14.6 %shard_map.55 = f32[800,1600]{1,0:T(8,128)} custom-call(s32[1]{0:T(128)} %bitcast.me_ref.refs_0_, f32[800,1600]{1,0:T(8,128)} %x_ref.3, f32[8,8,20000]{2,1,0:T(8,128)} %all-to-all-done.3.crossed_ref, f32[8,40000]{1,0:T(8,128)} %get-tuple-element.65.refs_0_, f32[8,40000]{1,0:T(8,128)} %collective-permute-done.9.refs_1_, f32[8,40000]{1,0:T(8,128)} %copy-done.1, ...), custom_call_target="tpu_custom_call" | custom-call | bytes 20480000 | tf_op jit(solution)/shard_map/pallas_call | solution.py:35
  (29 shorter events, 0.1 us)
Async XLA Ops:
  6.5 10.6 %copy-start.3 = (f32[10,20,512]{2,1,0:T(8,128)S(1)}, f32[10,20,512]{2,1,0:T(8,128)}, u32[]{:S(2)}) copy-start(f32[10,20,512]{2,1,0:T(8,128)} %param.6) | copy-start | bytes 1228804
  6.5 76.7 %all-gather.4.cloned.1.call-start = ((), (), s32[]{:S(2)}) async-start(), calls=%async_computation.4 | async-start | bytes 3686400 | tf_op jit(solution)/shard_map/all_gather | solution.py:304
  18.0 152.4 %all-gather.6.cloned.1.call-start = ((), (), s32[]{:S(2)}) async-start(), calls=%async_computation.5 | async-start | bytes 16384000 | tf_op jit(solution)/shard_map/all_gather | solution.py:308
  24.9 30.4 %collective-permute-start = (f32[8,40000]{1,0:T(8,128)}, f32[8,40000]{1,0:T(8,128)}, u32[]{:S(2)}, u32[]{:S(2)}) collective-permute-start(f32[8,40000]{1,0:T(8,128)} %get-tuple-element.41), channel_id=1, source_target_pairs={{0,1},{1,2},{2,3},{3,0},{4,5},{5,6},{6,7},{7,4},{8,9},{9,10},{10,1... | collective-permute-start | bytes 3840008 | tf_op jit(solution)/shard_map/ppermute | solution.py:266
  27.5 55.2 %collective-permute-start.1 = (f32[8,40000]{1,0:T(8,128)}, f32[8,40000]{1,0:T(8,128)}, u32[]{:S(2)}, u32[]{:S(2)}) collective-permute-start(f32[8,40000]{1,0:T(8,128)} %get-tuple-element.42), channel_id=1, source_target_pairs={{0,2},{1,3},{2,0},{3,1},{4,6},{5,7},{6,4},{7,5},{8,10},{9,11},{10,... | collective-permute-start | bytes 3840008 | tf_op jit(solution)/shard_map/ppermute | solution.py:266
  27.5 55.7 %collective-permute-start.2 = (f32[8,40000]{1,0:T(8,128)}, f32[8,40000]{1,0:T(8,128)}, u32[]{:S(2)}, u32[]{:S(2)}) collective-permute-start(f32[8,40000]{1,0:T(8,128)} %get-tuple-element.43), channel_id=1, source_target_pairs={{0,3},{1,0},{2,1},{3,2},{4,7},{5,4},{6,5},{7,6},{8,11},{9,8},{10,9... | collective-permute-start | bytes 3840008 | tf_op jit(solution)/shard_map/ppermute | solution.py:266
  83.3 6.3 %copy-start.4 = (f32[80,80]{1,0:T(8,128)S(1)}, f32[80,80]{1,0:T(8,128)}, u32[]{:S(2)}) copy-start(f32[80,80]{1,0:T(8,128)} %param.5) | copy-start | bytes 76804
  83.3 120.1 %all-to-all-start = ((f32[8,8,20000]{2,1,0:T(8,128)}), f32[8,8,20000]{2,1,0:T(8,128)}, u32[]{:S(2)}, u32[]{:S(2)}) async-start(f32[8,8,20000]{2,1,0:T(8,128)} %get-tuple-element.37), calls=%async_computation | async-start | bytes 10289152 | tf_op jit(solution)/shard_map/all_to_all | solution.py:275
  237.0 4.0 copy-start.5
  237.0 64.3 %all-to-all-start.1 = ((f32[8,8,10400]{2,1,0:T(8,128)}), f32[8,8,10400]{2,1,0:T(8,128)S(1)}, u32[]{:S(2)}, u32[]{:S(2)}) async-start(f32[8,8,10400]{2,1,0:T(8,128)} %get-tuple-element.49), calls=%async_computation.1 | async-start | bytes 5373952 | tf_op jit(solution)/shard_map/all_to_all | solution.py:275
  301.3 60.5 %copy-start = (f32[8,8,10400]{2,1,0:T(8,128)}, f32[8,8,10400]{2,1,0:T(8,128)S(1)}, u32[]{:S(2)}) copy-start(f32[8,8,10400]{2,1,0:T(8,128)S(1)} %all-to-all-done.1.x_ref) | copy-start | bytes 7987204
  361.8 160.4 %all-to-all-start.3 = ((f32[8,8,20000]{2,1,0:T(8,128)}), f32[8,8,20000]{2,1,0:T(8,128)}, u32[]{:S(2)}, u32[]{:S(2)}) async-start(f32[8,8,20000]{2,1,0:T(8,128)} %shard_map.50), calls=%async_computation.3 | async-start | bytes 10289152 | tf_op jit(solution)/shard_map/all_to_all | solution.py:275
  371.4 17.6 %collective-permute-start.3 = (f32[8,20800]{1,0:T(8,128)}, f32[8,20800]{1,0:T(8,128)S(1)}, u32[]{:S(2)}, u32[]{:S(2)}) collective-permute-start(f32[8,20800]{1,0:T(8,128)} %get-tuple-element.57), channel_id=1, source_target_pairs={{0,1},{1,2},{2,3},{3,0},{4,5},{5,6},{6,7},{7,4},{8,9},{9,10},{10,1... | collective-permute-start | bytes 1996808 | tf_op jit(solution)/shard_map/ppermute | solution.py:266
  374.4 30.1 %collective-permute-start.4 = (f32[8,20800]{1,0:T(8,128)}, f32[8,20800]{1,0:T(8,128)S(1)}, u32[]{:S(2)}, u32[]{:S(2)}) collective-permute-start(f32[8,20800]{1,0:T(8,128)} %get-tuple-element.58), channel_id=1, source_target_pairs={{0,2},{1,3},{2,0},{3,1},{4,6},{5,7},{6,4},{7,5},{8,10},{9,11},{10,... | collective-permute-start | bytes 1996808 | tf_op jit(solution)/shard_map/ppermute | solution.py:266
  374.9 30.7 %collective-permute-start.5 = (f32[8,20800]{1,0:T(8,128)}, f32[8,20800]{1,0:T(8,128)S(1)}, u32[]{:S(2)}, u32[]{:S(2)}) collective-permute-start(f32[8,20800]{1,0:T(8,128)} %get-tuple-element.59), channel_id=1, source_target_pairs={{0,3},{1,0},{2,1},{3,2},{4,7},{5,4},{6,5},{7,6},{8,11},{9,8},{10,9... | collective-permute-start | bytes 1996808 | tf_op jit(solution)/shard_map/ppermute | solution.py:266
  379.6 36.9 %collective-permute-start.6 = (f32[200,768]{1,0:T(8,128)}, f32[200,768]{1,0:T(8,128)S(1)}, u32[]{:S(2)}, u32[]{:S(2)}) collective-permute-start(f32[200,768]{1,0:T(8,128)} %get-tuple-element.62), channel_id=1, source_target_pairs={{0,1},{1,2},{2,3},{3,0},{4,5},{5,6},{6,7},{7,4},{8,9},{9,10},{10,1... | collective-permute-start | bytes 1843208 | tf_op jit(solution)/shard_map/ppermute | solution.py:266
  381.4 49.5 %collective-permute-start.7 = (f32[200,768]{1,0:T(8,128)}, f32[200,768]{1,0:T(8,128)S(1)}, u32[]{:S(2)}, u32[]{:S(2)}) collective-permute-start(f32[200,768]{1,0:T(8,128)} %get-tuple-element.63), channel_id=1, source_target_pairs={{0,2},{1,3},{2,0},{3,1},{4,6},{5,7},{6,4},{7,5},{8,10},{9,11},{10,... | collective-permute-start | bytes 1843208 | tf_op jit(solution)/shard_map/ppermute | solution.py:266
  389.0 42.4 %copy-start.6 = (f32[8,20800]{1,0:T(8,128)}, f32[8,20800]{1,0:T(8,128)S(1)}, u32[]{:S(2)}) copy-start(f32[8,20800]{1,0:T(8,128)S(1)} %collective-permute-done.3.refs_3_) | copy-start | bytes 1996804
  389.0 42.4 %collective-permute-start.8 = (f32[200,768]{1,0:T(8,128)}, f32[200,768]{1,0:T(8,128)S(1)}, u32[]{:S(2)}, u32[]{:S(2)}) collective-permute-start(f32[200,768]{1,0:T(8,128)} %get-tuple-element.64), channel_id=1, source_target_pairs={{0,3},{1,0},{2,1},{3,2},{4,7},{5,4},{6,5},{7,6},{8,11},{9,8},{10,9... | collective-permute-start | bytes 1843208 | tf_op jit(solution)/shard_map/ppermute | solution.py:266
  404.5 26.9 %copy-start.7 = (f32[8,20800]{1,0:T(8,128)}, f32[8,20800]{1,0:T(8,128)S(1)}, u32[]{:S(2)}) copy-start(f32[8,20800]{1,0:T(8,128)S(1)} %collective-permute-done.4.refs_4_) | copy-start | bytes 1996804
  405.6 25.8 %copy-start.8 = (f32[8,20800]{1,0:T(8,128)}, f32[8,20800]{1,0:T(8,128)S(1)}, u32[]{:S(2)}) copy-start(f32[8,20800]{1,0:T(8,128)S(1)} %collective-permute-done.5.refs_5_) | copy-start | bytes 1996804
  416.5 14.9 %copy-start.9 = (f32[200,768]{1,0:T(8,128)}, f32[200,768]{1,0:T(8,128)S(1)}, u32[]{:S(2)}) copy-start(f32[200,768]{1,0:T(8,128)S(1)} %collective-permute-done.6.refs_7_) | copy-start | bytes 1843204
  430.8 0.9 copy-start.10
  431.4 0.8 copy-start.11
  464.9 30.1 %collective-permute-start.10 = (f32[8,40000]{1,0:T(8,128)}, f32[8,40000]{1,0:T(8,128)S(1)}, u32[]{:S(2)}, u32[]{:S(2)}) collective-permute-start(f32[8,40000]{1,0:T(8,128)} %get-tuple-element.67), channel_id=1, source_target_pairs={{0,2},{1,3},{2,0},{3,1},{4,6},{5,7},{6,4},{7,5},{8,10},{9,11},{10,... | collective-permute-start | bytes 3840008 | tf_op jit(solution)/shard_map/ppermute | solution.py:266
  465.9 56.3 %collective-permute-start.11 = (f32[8,40000]{1,0:T(8,128)}, f32[8,40000]{1,0:T(8,128)S(1)}, u32[]{:S(2)}, u32[]{:S(2)}) collective-permute-start(f32[8,40000]{1,0:T(8,128)} %get-tuple-element.68), channel_id=1, source_target_pairs={{0,3},{1,0},{2,1},{3,2},{4,7},{5,4},{6,5},{7,6},{8,11},{9,8},{10,9... | collective-permute-start | bytes 3840008 | tf_op jit(solution)/shard_map/ppermute | solution.py:266
  465.9 56.3 %collective-permute-start.9 = (f32[8,40000]{1,0:T(8,128)}, f32[8,40000]{1,0:T(8,128)}, u32[]{:S(2)}, u32[]{:S(2)}) collective-permute-start(f32[8,40000]{1,0:T(8,128)} %get-tuple-element.66), channel_id=1, source_target_pairs={{0,1},{1,2},{2,3},{3,0},{4,5},{5,6},{6,7},{7,4},{8,9},{9,10},{10,1... | collective-permute-start | bytes 3840008 | tf_op jit(solution)/shard_map/ppermute | solution.py:266
  495.0 27.3 %copy-start.1 = (f32[8,40000]{1,0:T(8,128)}, f32[8,40000]{1,0:T(8,128)S(1)}, u32[]{:S(2)}) copy-start(f32[8,40000]{1,0:T(8,128)S(1)} %collective-permute-done.10.refs_2_) | copy-start | bytes 3840004
  522.2 1.1 copy-start.2
Sparse Core Ops, SparseCore 0:
  18.1 63.1 all-gather.3
  83.4 86.9 all-gather.5

commit v6 on v5

--- a/solution.py
+++ b/solution.py
@@ -355,7 +355,7 @@
         if h + 1 == len(spans):
             double = after(double, part)
         if h:
-            part = after(part, turned)
+            part = after(part, arriving)
         turned = call(
             turn_arriving_body, col_wires(rows * (stop - start)), [me, part],
             [

time: 554 us -> 560 us (1.011)
  waiting for transfers between devices: 257 us -> 266 us
    ppermute x12, waiting for transfers between devices: 157 us -> 166 us  [shift(): lax.ppermute(parts[s], axis, [(d, (d + s) % n) for d in range(n)])]
where the time goes in v6:
time: 560 us; the launch traced here: 552 us
  waiting for transfers between devices  266 us (48%)
  Pallas kernels  181 us (32%)
  blocking collectives  60.5 us (11%)
  starting transfers between devices  25.9 us (5%)
  between operations  14 us (2%)
    pallas_call x9, Pallas kernels, call(): pl.pallas_call(body, in_specs=[smem if x.dtype == jnp.int32 else vmem for...  168 us
    ppermute x12, waiting for transfers between devices, shift(): lax.ppermute(parts[s], axis, [(d, (d + s) % n) for d in range(n)])  166 us
    all_gather x1, waiting for transfers between devices, shards(): whole = lax.all_gather(after(whole, theirs), 'col', axis=0, tiled=False)  80 us
    all_to_all x1, blocking collectives, exchange(): return lax.all_to_all(x, axis, split_axis=0, concat_axis=0, tiled=True)  60.5 us
    all_to_all x3, waiting for transfers between devices, exchange(): return lax.all_to_all(x, axis, split_axis=0, concat_axis=0, tiled=True)  20.3 us
    all_to_all x3, starting transfers between devices, exchange(): return lax.all_to_all(x, axis, split_axis=0, concat_axis=0, tiled=True)  15 us
    pallas_call x1, Pallas kernels, shards(): pl.pallas_call(functools.partial(split_body, n), grid=(n // group,), in_s...  13.1 us
  transfers between devices with their start and end apart: 17, of which 14 were waited for; matrix products, arithmetic and copies ran while one was open for 0% of the time, Pallas kernels for 22%

profile of v6, /device:TPU:1, one launch (start us, length us, event | category | flops | bytes accessed | tf_op | source)
XLA Modules:
  0.0 551.5 jit_solution(12844629513536952346)
XLA Ops:
  6.5 10.6 %shard_map.46 = (f32[1600,800]{1,0:T(8,128)}, f32[8,8,20000]{2,1,0:T(8,128)}) custom-call(f32[800,1600]{1,0:T(8,128)} %x_ref.3), custom_call_target="tpu_custom_call" | custom-call | bytes 15360000 | tf_op jit(solution)/shard_map/pallas_call | solution.py:35
  17.1 0.8 reshape.11
  17.9 0.0 all-gather.4.cloned.1.call-update
  18.0 0.0 all-gather.6.cloned.1.call-start
  18.0 6.9 %shard_map.47 = (f32[8,40000]{1,0:T(8,128)}, f32[8,40000]{1,0:T(8,128)}, f32[8,40000]{1,0:T(8,128)}, f32[8,40000]{1,0:T(8,128)}) custom-call(s32[1]{0:T(128)} %bitcast.me_ref.refs_0_, f32[1600,800]{1,0:T(8,128)} %get-tuple-element.39.x_ref), custom_call_target="tpu_custom_call" | custom-call | bytes 10240000 | tf_op jit(solution)/shard_map/pallas_call | solution.py:35
  24.9 2.6 collective-permute-start
  27.5 0.4 collective-permute-start.2
  27.9 27.3 %collective-permute-done.refs_2_ = f32[8,40000]{1,0:T(8,128)} collective-permute-done((f32[8,40000]{1,0:T(8,128)}, f32[8,40000]{1,0:T(8,128)}, u32[]{:S(2)}, u32[]{:S(2)}) %collective-permute-start) | collective-permute-done | bytes 1280032 | tf_op jit(solution)/shard_map/ppermute | solution.py:266
  55.3 27.5 %collective-permute-done.1.refs_3_ = f32[8,40000]{1,0:T(8,128)} collective-permute-done((f32[8,40000]{1,0:T(8,128)}, f32[8,40000]{1,0:T(8,128)}, u32[]{:S(2)}, u32[]{:S(2)}) %collective-permute-start.1) | collective-permute-done | bytes 1280032 | tf_op jit(solution)/shard_map/ppermute | solution.py:266
  82.7 0.5 collective-permute-done.2.refs_4_
  83.2 0.0 all-gather.6.cloned.1.call-update
  83.3 0.0 copy-start.4
  83.3 6.3 %all-to-all-start = ((f32[8,8,20000]{2,1,0:T(8,128)}), f32[8,8,20000]{2,1,0:T(8,128)}, u32[]{:S(2)}, u32[]{:S(2)}) async-start(f32[8,8,20000]{2,1,0:T(8,128)} %get-tuple-element.37), calls=%async_computation | async-start | bytes 10289152 | tf_op jit(solution)/shard_map/all_to_all | solution.py:275
  89.6 0.1 copy.5
  89.7 0.7 pad_maximum_fusion
  90.4 80.0 %all-gather.6.cloned.1.call-done = f32[6400,512]{1,0:T(8,128)} async-done(((f32[1600,512]{1,0:T(8,128)}), f32[6400,512]{1,0:T(8,128)}) %all-gather.6.cloned.1.call-update) | async-done | bytes 13107216 | tf_op jit(solution)/shard_map/all_gather | solution.py:308
  170.4 13.1 %shard_map.48 = (bf16[6400,512]{1,0:T(8,128)(2,1)}, bf16[6400,512]{1,0:T(8,128)(2,1)}) custom-call(f32[4,1600,512]{2,1,0:T(8,128)} %bitcast.7), custom_call_target="tpu_custom_call" | custom-call | flops 6553600 | bytes 26214400 | tf_op jit(solution)/shard_map/pallas_call | solution.py:311
  183.5 19.9 %all-to-all-done.refs_0_ = f32[8,8,20000]{2,1,0:T(8,128)} async-done(((f32[8,8,20000]{2,1,0:T(8,128)}), f32[8,8,20000]{2,1,0:T(8,128)}, u32[]{:S(2)}, u32[]{:S(2)}) %all-to-all-start) | async-done | bytes 5120032 | tf_op jit(solution)/shard_map/all_to_all | solution.py:275
  203.4 33.6 %shard_map.49 = (f32[8,200,800]{2,1,0:T(8,128)}, f32[8,8,10400]{2,1,0:T(8,128)}, f32[8,24,3200]{2,1,0:T(8,128)}) custom-call(f32[8,8,20000]{2,1,0:T(8,128)} %all-to-all-done.refs_0_, bf16[6400,512]{1,0:T(8,128)(2,1)} %get-tuple-element.45.refs_1_.refs_0_.refs_5_.refs_10_, bf16[6400,512]{1,0:T(8,128)(2,1)} %get-tuple-element.46.refs_2_.refs_1_.refs_6_.refs_11_, ...), custom_call_target="tpu_custom_call" | custom-call | flops 9093120000 | bytes 28467200 | tf_op jit(solution)/shard_map/pallas_call | solution.py:35
  237.0 4.0 all-to-all-start.1
  241.0 0.6 neg.13
  241.6 31.0 %shard_map.50 = f32[8,8,20000]{2,1,0:T(8,128)} custom-call(f32[8,200,800]{2,1,0:T(8,128)} %get-tuple-element.47.x_ref, bf16[6400,512]{1,0:T(8,128)(2,1)} %get-tuple-element.45.refs_1_.refs_0_.refs_5_.refs_10_, bf16[6400,512]{1,0:T(8,128)(2,1)} %get-tuple-element.46.refs_2_.refs_1_.refs_6_.refs_11_, f32[1,512]{1,0:T(1,128)} %bitcast.9, ...), custom_call_target="tpu_custom_call" | custom-call | flops 9093120000 | bytes 28467200 | tf_op jit(solution)/shard_map/pallas_call | solution.py:35
  272.7 28.3 %shard_map.51.refs_1_ = f32[4,200,1600]{2,1,0:T(8,128)} custom-call(s32[1]{0:T(128)} %bitcast.me_ref.refs_0_, f32[8,40000]{1,0:T(8,128)} %get-tuple-element.50.refs_1_, f32[8,40000]{1,0:T(8,128)} %collective-permute-done.refs_2_, f32[8,40000]{1,0:T(8,128)} %collective-permute-done.1.refs_3_, f32[8,40000]{1,0:T(8,128)} %collective-permute-done.2.refs_4_, ...), custom_call_target="tpu_custom_call" | custom-call | flops 9093120000 | bytes 28467200 | tf_op jit(solution)/shard_map/pallas_call | solution.py:35
  300.9 0.4 all-to-all-done.1.x_ref
  301.3 60.5 %all_to_all.20.x_ref = f32[8,24,3200]{2,1,0:T(8,128)} all-to-all(f32[8,24,3200]{2,1,0:T(8,128)} %get-tuple-element.54), channel_id=1, replica_groups=mesh['row'=8,'col'=4] {'row'}, dimensions={0} | all-to-all | bytes 4915200 | tf_op jit(solution)/shard_map/all_to_all | solution.py:275
  361.8 4.6 all-to-all-start.3
  366.4 5.0 shard_map.52
  371.4 3.0 collective-permute-start.3
  374.4 0.4 collective-permute-start.4
  374.9 0.0 collective-permute-start.5
  374.9 14.1 %collective-permute-done.3.refs_3_ = f32[8,20800]{1,0:T(8,128)S(1)} collective-permute-done((f32[8,20800]{1,0:T(8,128)}, f32[8,20800]{1,0:T(8,128)S(1)}, u32[]{:S(2)}, u32[]{:S(2)}) %collective-permute-start.3) | collective-permute-done | bytes 665632 | tf_op jit(solution)/shard_map/ppermute | solution.py:266
  389.0 15.5 %collective-permute-done.4.refs_4_ = f32[8,20800]{1,0:T(8,128)S(1)} collective-permute-done((f32[8,20800]{1,0:T(8,128)}, f32[8,20800]{1,0:T(8,128)S(1)}, u32[]{:S(2)}, u32[]{:S(2)}) %collective-permute-start.4) | collective-permute-done | bytes 665632 | tf_op jit(solution)/shard_map/ppermute | solution.py:266
  404.5 0.6 collective-permute-done.5.refs_5_
  405.1 4.9 shard_map.53
  410.0 1.0 collective-permute-start.7
  411.0 1.0 collective-permute-start.8
  412.0 9.9 %collective-permute-done.6.refs_7_ = f32[200,768]{1,0:T(8,128)S(1)} collective-permute-done((f32[200,768]{1,0:T(8,128)}, f32[200,768]{1,0:T(8,128)S(1)}, u32[]{:S(2)}, u32[]{:S(2)}) %collective-permute-start.6) | collective-permute-done | bytes 614432 | tf_op jit(solution)/shard_map/ppermute | solution.py:266
  421.9 15.6 %collective-permute-done.7.refs_8_ = f32[200,768]{1,0:T(8,128)S(1)} collective-permute-done((f32[200,768]{1,0:T(8,128)}, f32[200,768]{1,0:T(8,128)S(1)}, u32[]{:S(2)}, u32[]{:S(2)}) %collective-permute-start.7) | collective-permute-done | bytes 614432 | tf_op jit(solution)/shard_map/ppermute | solution.py:266
  437.5 1.4 collective-permute-done.8.refs_9_
  439.0 0.8 copy-done.11
  439.8 32.7 %shard_map.54 = (f32[8,40000]{1,0:T(8,128)}, f32[8,40000]{1,0:T(8,128)}, f32[8,40000]{1,0:T(8,128)}, f32[8,40000]{1,0:T(8,128)}) custom-call(s32[1]{0:T(128)} %bitcast.me_ref.refs_0_, f32[4,200,1600]{2,1,0:T(8,128)} %shard_map.51.refs_1_, f32[8,20800]{1,0:T(8,128)} %get-tuple-element.56.refs_2_, f32[8,20800]{1,0:T(8,128)} %copy-done.6, ...), custom_call_target="tpu_custom_call" | custom-call | flops 9093120000 | bytes 28467200 | tf_op jit(solution)/shard_map/pallas_call | solution.py:35
  472.4 0.4 collective-permute-start.10
  472.9 2.0 collective-permute-start.9
  474.8 27.7 %collective-permute-done.10.refs_2_ = f32[8,40000]{1,0:T(8,128)S(1)} collective-permute-done((f32[8,40000]{1,0:T(8,128)}, f32[8,40000]{1,0:T(8,128)S(1)}, u32[]{:S(2)}, u32[]{:S(2)}) %collective-permute-start.10) | collective-permute-done | bytes 1280032 | tf_op jit(solution)/shard_map/ppermute | solution.py:266
  502.5 26.0 %collective-permute-done.11.refs_3_ = f32[8,40000]{1,0:T(8,128)S(1)} collective-permute-done((f32[8,40000]{1,0:T(8,128)}, f32[8,40000]{1,0:T(8,128)S(1)}, u32[]{:S(2)}, u32[]{:S(2)}) %collective-permute-start.11) | collective-permute-done | bytes 1280032 | tf_op jit(solution)/shard_map/ppermute | solution.py:266
  528.6 0.0 collective-permute-done.9.refs_1_
  528.6 1.1 copy-done.2
  529.6 14.6 %shard_map.55 = f32[800,1600]{1,0:T(8,128)} custom-call(s32[1]{0:T(128)} %bitcast.me_ref.refs_0_, f32[800,1600]{1,0:T(8,128)} %x_ref.3, f32[8,8,20000]{2,1,0:T(8,128)} %all-to-all-done.3.crossed_ref, f32[8,40000]{1,0:T(8,128)} %get-tuple-element.65.refs_0_, f32[8,40000]{1,0:T(8,128)} %collective-permute-done.9.refs_1_, f32[8,40000]{1,0:T(8,128)} %copy-done.1, ...), custom_call_target="tpu_custom_call" | custom-call | bytes 20480000 | tf_op jit(solution)/shard_map/pallas_call | solution.py:35
  (29 shorter events, 0.1 us)
Async XLA Ops:
  6.5 10.6 %copy-start.3 = (f32[10,20,512]{2,1,0:T(8,128)S(1)}, f32[10,20,512]{2,1,0:T(8,128)}, u32[]{:S(2)}) copy-start(f32[10,20,512]{2,1,0:T(8,128)} %param.6) | copy-start | bytes 1228804
  6.5 76.7 %all-gather.4.cloned.1.call-start = ((), (), s32[]{:S(2)}) async-start(), calls=%async_computation.4 | async-start | bytes 3686400 | tf_op jit(solution)/shard_map/all_gather | solution.py:304
  18.0 152.4 %all-gather.6.cloned.1.call-start = ((), (), s32[]{:S(2)}) async-start(), calls=%async_computation.5 | async-start | bytes 16384000 | tf_op jit(solution)/shard_map/all_gather | solution.py:308
  24.9 30.4 %collective-permute-start = (f32[8,40000]{1,0:T(8,128)}, f32[8,40000]{1,0:T(8,128)}, u32[]{:S(2)}, u32[]{:S(2)}) collective-permute-start(f32[8,40000]{1,0:T(8,128)} %get-tuple-element.41), channel_id=1, source_target_pairs={{0,1},{1,2},{2,3},{3,0},{4,5},{5,6},{6,7},{7,4},{8,9},{9,10},{10,1... | collective-permute-start | bytes 3840008 | tf_op jit(solution)/shard_map/ppermute | solution.py:266
  27.5 55.2 %collective-permute-start.1 = (f32[8,40000]{1,0:T(8,128)}, f32[8,40000]{1,0:T(8,128)}, u32[]{:S(2)}, u32[]{:S(2)}) collective-permute-start(f32[8,40000]{1,0:T(8,128)} %get-tuple-element.42), channel_id=1, source_target_pairs={{0,2},{1,3},{2,0},{3,1},{4,6},{5,7},{6,4},{7,5},{8,10},{9,11},{10,... | collective-permute-start | bytes 3840008 | tf_op jit(solution)/shard_map/ppermute | solution.py:266
  27.5 55.7 %collective-permute-start.2 = (f32[8,40000]{1,0:T(8,128)}, f32[8,40000]{1,0:T(8,128)}, u32[]{:S(2)}, u32[]{:S(2)}) collective-permute-start(f32[8,40000]{1,0:T(8,128)} %get-tuple-element.43), channel_id=1, source_target_pairs={{0,3},{1,0},{2,1},{3,2},{4,7},{5,4},{6,5},{7,6},{8,11},{9,8},{10,9... | collective-permute-start | bytes 3840008 | tf_op jit(solution)/shard_map/ppermute | solution.py:266
  83.3 6.3 %copy-start.4 = (f32[80,80]{1,0:T(8,128)S(1)}, f32[80,80]{1,0:T(8,128)}, u32[]{:S(2)}) copy-start(f32[80,80]{1,0:T(8,128)} %param.5) | copy-start | bytes 76804
  83.3 120.1 %all-to-all-start = ((f32[8,8,20000]{2,1,0:T(8,128)}), f32[8,8,20000]{2,1,0:T(8,128)}, u32[]{:S(2)}, u32[]{:S(2)}) async-start(f32[8,8,20000]{2,1,0:T(8,128)} %get-tuple-element.37), calls=%async_computation | async-start | bytes 10289152 | tf_op jit(solution)/shard_map/all_to_all | solution.py:275
  237.0 4.0 copy-start.5
  237.0 64.3 %all-to-all-start.1 = ((f32[8,8,10400]{2,1,0:T(8,128)}), f32[8,8,10400]{2,1,0:T(8,128)S(1)}, u32[]{:S(2)}, u32[]{:S(2)}) async-start(f32[8,8,10400]{2,1,0:T(8,128)} %get-tuple-element.49), calls=%async_computation.1 | async-start | bytes 5373952 | tf_op jit(solution)/shard_map/all_to_all | solution.py:275
  301.3 60.5 %copy-start = (f32[8,8,10400]{2,1,0:T(8,128)}, f32[8,8,10400]{2,1,0:T(8,128)S(1)}, u32[]{:S(2)}) copy-start(f32[8,8,10400]{2,1,0:T(8,128)S(1)} %all-to-all-done.1.x_ref) | copy-start | bytes 7987204
  361.8 166.8 %all-to-all-start.3 = ((f32[8,8,20000]{2,1,0:T(8,128)}), f32[8,8,20000]{2,1,0:T(8,128)}, u32[]{:S(2)}, u32[]{:S(2)}) async-start(f32[8,8,20000]{2,1,0:T(8,128)} %shard_map.50), calls=%async_computation.3 | async-start | bytes 10289152 | tf_op jit(solution)/shard_map/all_to_all | solution.py:275
  371.4 17.6 %collective-permute-start.3 = (f32[8,20800]{1,0:T(8,128)}, f32[8,20800]{1,0:T(8,128)S(1)}, u32[]{:S(2)}, u32[]{:S(2)}) collective-permute-start(f32[8,20800]{1,0:T(8,128)} %get-tuple-element.57), channel_id=1, source_target_pairs={{0,1},{1,2},{2,3},{3,0},{4,5},{5,6},{6,7},{7,4},{8,9},{9,10},{10,1... | collective-permute-start | bytes 1996808 | tf_op jit(solution)/shard_map/ppermute | solution.py:266
  374.4 30.1 %collective-permute-start.4 = (f32[8,20800]{1,0:T(8,128)}, f32[8,20800]{1,0:T(8,128)S(1)}, u32[]{:S(2)}, u32[]{:S(2)}) collective-permute-start(f32[8,20800]{1,0:T(8,128)} %get-tuple-element.58), channel_id=1, source_target_pairs={{0,2},{1,3},{2,0},{3,1},{4,6},{5,7},{6,4},{7,5},{8,10},{9,11},{10,... | collective-permute-start | bytes 1996808 | tf_op jit(solution)/shard_map/ppermute | solution.py:266
  374.9 30.2 %collective-permute-start.5 = (f32[8,20800]{1,0:T(8,128)}, f32[8,20800]{1,0:T(8,128)S(1)}, u32[]{:S(2)}, u32[]{:S(2)}) collective-permute-start(f32[8,20800]{1,0:T(8,128)} %get-tuple-element.59), channel_id=1, source_target_pairs={{0,3},{1,0},{2,1},{3,2},{4,7},{5,4},{6,5},{7,6},{8,11},{9,8},{10,9... | collective-permute-start | bytes 1996808 | tf_op jit(solution)/shard_map/ppermute | solution.py:266
  389.0 49.9 %copy-start.6 = (f32[8,20800]{1,0:T(8,128)}, f32[8,20800]{1,0:T(8,128)S(1)}, u32[]{:S(2)}) copy-start(f32[8,20800]{1,0:T(8,128)S(1)} %collective-permute-done.3.refs_3_) | copy-start | bytes 1996804
  404.5 34.4 %copy-start.7 = (f32[8,20800]{1,0:T(8,128)}, f32[8,20800]{1,0:T(8,128)S(1)}, u32[]{:S(2)}) copy-start(f32[8,20800]{1,0:T(8,128)S(1)} %collective-permute-done.4.refs_4_) | copy-start | bytes 1996804
  405.1 33.9 %copy-start.8 = (f32[8,20800]{1,0:T(8,128)}, f32[8,20800]{1,0:T(8,128)S(1)}, u32[]{:S(2)}) copy-start(f32[8,20800]{1,0:T(8,128)S(1)} %collective-permute-done.5.refs_5_) | copy-start | bytes 1996804
  410.0 11.9 %collective-permute-start.6 = (f32[200,768]{1,0:T(8,128)}, f32[200,768]{1,0:T(8,128)S(1)}, u32[]{:S(2)}, u32[]{:S(2)}) collective-permute-start(f32[200,768]{1,0:T(8,128)} %get-tuple-element.62), channel_id=1, source_target_pairs={{0,1},{1,2},{2,3},{3,0},{4,5},{5,6},{6,7},{7,4},{8,9},{9,10},{10,1... | collective-permute-start | bytes 1843208 | tf_op jit(solution)/shard_map/ppermute | solution.py:266
  410.0 27.5 %collective-permute-start.7 = (f32[200,768]{1,0:T(8,128)}, f32[200,768]{1,0:T(8,128)S(1)}, u32[]{:S(2)}, u32[]{:S(2)}) collective-permute-start(f32[200,768]{1,0:T(8,128)} %get-tuple-element.63), channel_id=1, source_target_pairs={{0,2},{1,3},{2,0},{3,1},{4,6},{5,7},{6,4},{7,5},{8,10},{9,11},{10,... | collective-permute-start | bytes 1843208 | tf_op jit(solution)/shard_map/ppermute | solution.py:266
  411.0 27.9 %collective-permute-start.8 = (f32[200,768]{1,0:T(8,128)}, f32[200,768]{1,0:T(8,128)S(1)}, u32[]{:S(2)}, u32[]{:S(2)}) collective-permute-start(f32[200,768]{1,0:T(8,128)} %get-tuple-element.64), channel_id=1, source_target_pairs={{0,3},{1,0},{2,1},{3,2},{4,7},{5,4},{6,5},{7,6},{8,11},{9,8},{10,9... | collective-permute-start | bytes 1843208 | tf_op jit(solution)/shard_map/ppermute | solution.py:266
  421.9 17.0 %copy-start.9 = (f32[200,768]{1,0:T(8,128)}, f32[200,768]{1,0:T(8,128)S(1)}, u32[]{:S(2)}) copy-start(f32[200,768]{1,0:T(8,128)S(1)} %collective-permute-done.6.refs_7_) | copy-start | bytes 1843204
  437.5 1.5 copy-start.10
  438.9 0.9 copy-start.11
  472.4 30.1 %collective-permute-start.10 = (f32[8,40000]{1,0:T(8,128)}, f32[8,40000]{1,0:T(8,128)S(1)}, u32[]{:S(2)}, u32[]{:S(2)}) collective-permute-start(f32[8,40000]{1,0:T(8,128)} %get-tuple-element.67), channel_id=1, source_target_pairs={{0,2},{1,3},{2,0},{3,1},{4,6},{5,7},{6,4},{7,5},{8,10},{9,11},{10,... | collective-permute-start | bytes 3840008 | tf_op jit(solution)/shard_map/ppermute | solution.py:266
  472.9 55.7 %collective-permute-start.11 = (f32[8,40000]{1,0:T(8,128)}, f32[8,40000]{1,0:T(8,128)S(1)}, u32[]{:S(2)}, u32[]{:S(2)}) collective-permute-start(f32[8,40000]{1,0:T(8,128)} %get-tuple-element.68), channel_id=1, source_target_pairs={{0,3},{1,0},{2,1},{3,2},{4,7},{5,4},{6,5},{7,6},{8,11},{9,8},{10,9... | collective-permute-start | bytes 3840008 | tf_op jit(solution)/shard_map/ppermute | solution.py:266
  472.9 55.7 %collective-permute-start.9 = (f32[8,40000]{1,0:T(8,128)}, f32[8,40000]{1,0:T(8,128)}, u32[]{:S(2)}, u32[]{:S(2)}) collective-permute-start(f32[8,40000]{1,0:T(8,128)} %get-tuple-element.66), channel_id=1, source_target_pairs={{0,1},{1,2},{2,3},{3,0},{4,5},{5,6},{6,7},{7,4},{8,9},{9,10},{10,1... | collective-permute-start | bytes 3840008 | tf_op jit(solution)/shard_map/ppermute | solution.py:266
  502.5 26.0 %copy-start.1 = (f32[8,40000]{1,0:T(8,128)}, f32[8,40000]{1,0:T(8,128)S(1)}, u32[]{:S(2)}) copy-start(f32[8,40000]{1,0:T(8,128)S(1)} %collective-permute-done.10.refs_2_) | copy-start | bytes 3840004
  528.6 1.1 copy-start.2
Sparse Core Ops, SparseCore 0:
  18.1 63.1 all-gather.3
  83.4 86.9 all-gather.5

commit v7 on v6

--- a/solution.py
+++ b/solution.py
@@ -353,7 +353,7 @@
     for h, (start, stop) in enumerate(spans):
         part = exchange(after(parts[h], (part, base)) if h else parts[h], "row")
         if h + 1 == len(spans):
-            double = after(double, part)
+            double = after(double, (part, arriving))
         if h:
             part = after(part, arriving)
         turned = call(

time: 560 us -> 526 us (0.939)
  blocking collectives: 60.5 us -> 0 us
  waiting for transfers between devices: 266 us -> 285 us
  starting transfers between devices: 25.9 us -> 32.6 us
    all_to_all x1 -> x0, blocking collectives: 60.5 us -> none  [exchange(): return lax.all_to_all(x, axis, split_axis=0, concat_axis=0, tiled=True)]
    all_to_all x3 -> x4, waiting for transfers between devices: 20.3 us -> 37.3 us  [exchange(): return lax.all_to_all(x, axis, split_axis=0, concat_axis=0, tiled=True)]
    all_to_all x3 -> x4, starting transfers between devices: 15 us -> 20.4 us  [exchange(): return lax.all_to_all(x, axis, split_axis=0, concat_axis=0, tiled=True)]
  transfers between devices with their start and end apart: 17 -> 18, of which waited for: 14 -> 15; matrix products, arithmetic and copies ran while one was open for 0% -> 0% of each run, Pallas kernels for 22% -> 24%
where the time goes in v7:
time: 526 us; the launch traced here: 517 us
  waiting for transfers between devices  285 us (54%)
  Pallas kernels  180 us (34%)
  starting transfers between devices  32.6 us (6%)
  between operations  13.9 us (3%)
    ppermute x12, waiting for transfers between devices, shift(): lax.ppermute(parts[s], axis, [(d, (d + s) % n) for d in range(n)])  167 us
    pallas_call x9, Pallas kernels, call(): pl.pallas_call(body, in_specs=[smem if x.dtype == jnp.int32 else vmem for...  167 us
    all_gather x1, waiting for transfers between devices, shards(): whole = lax.all_gather(after(whole, theirs), 'col', axis=0, tiled=False)  80 us
    all_to_all x4, waiting for transfers between devices, exchange(): return lax.all_to_all(x, axis, split_axis=0, concat_axis=0, tiled=True)  37.3 us
    all_to_all x4, starting transfers between devices, exchange(): return lax.all_to_all(x, axis, split_axis=0, concat_axis=0, tiled=True)  20.4 us
    pallas_call x1, Pallas kernels, shards(): pl.pallas_call(functools.partial(split_body, n), grid=(n // group,), in_s...  13.1 us
    ppermute x12, starting transfers between devices, shift(): lax.ppermute(parts[s], axis, [(d, (d + s) % n) for d in range(n)])  12.1 us
  transfers between devices with their start and end apart: 18, of which 15 were waited for; matrix products, arithmetic and copies ran while one was open for 0% of the time, Pallas kernels for 24%

profile of v7, /device:TPU:1, one launch (start us, length us, event | category | flops | bytes accessed | tf_op | source)
XLA Modules:
  0.0 517.3 jit_solution(10954606273366990059)
XLA Ops:
  6.5 10.6 %shard_map.46 = (f32[1600,800]{1,0:T(8,128)}, f32[8,8,20000]{2,1,0:T(8,128)}) custom-call(f32[800,1600]{1,0:T(8,128)} %x_ref.3), custom_call_target="tpu_custom_call" | custom-call | bytes 15360000 | tf_op jit(solution)/shard_map/pallas_call | solution.py:35
  17.1 0.8 reshape.11
  18.0 0.0 all-gather.6.cloned.1.call-start
  18.0 6.9 %shard_map.47 = (f32[8,40000]{1,0:T(8,128)}, f32[8,40000]{1,0:T(8,128)}, f32[8,40000]{1,0:T(8,128)}, f32[8,40000]{1,0:T(8,128)}) custom-call(s32[1]{0:T(128)} %bitcast.me_ref.refs_0_, f32[1600,800]{1,0:T(8,128)} %get-tuple-element.39.x_ref), custom_call_target="tpu_custom_call" | custom-call | bytes 10240000 | tf_op jit(solution)/shard_map/pallas_call | solution.py:35
  24.9 2.6 collective-permute-start
  27.5 0.4 collective-permute-start.2
  27.9 27.3 %collective-permute-done.refs_2_ = f32[8,40000]{1,0:T(8,128)} collective-permute-done((f32[8,40000]{1,0:T(8,128)}, f32[8,40000]{1,0:T(8,128)}, u32[]{:S(2)}, u32[]{:S(2)}) %collective-permute-start) | collective-permute-done | bytes 1280032 | tf_op jit(solution)/shard_map/ppermute | solution.py:266
  55.2 27.5 %collective-permute-done.1.refs_3_ = f32[8,40000]{1,0:T(8,128)} collective-permute-done((f32[8,40000]{1,0:T(8,128)}, f32[8,40000]{1,0:T(8,128)}, u32[]{:S(2)}, u32[]{:S(2)}) %collective-permute-start.1) | collective-permute-done | bytes 1280032 | tf_op jit(solution)/shard_map/ppermute | solution.py:266
  82.7 0.5 collective-permute-done.2.refs_4_
  83.2 0.0 all-gather.6.cloned.1.call-update
  83.2 6.3 %all-to-all-start = ((f32[8,8,20000]{2,1,0:T(8,128)}), f32[8,8,20000]{2,1,0:T(8,128)}, u32[]{:S(2)}, u32[]{:S(2)}) async-start(f32[8,8,20000]{2,1,0:T(8,128)} %get-tuple-element.37), calls=%async_computation | async-start | bytes 10289152 | tf_op jit(solution)/shard_map/all_to_all | solution.py:275
  89.6 0.1 copy.5
  89.7 0.7 pad_maximum_fusion
  90.4 80.0 %all-gather.6.cloned.1.call-done = f32[6400,512]{1,0:T(8,128)} async-done(((f32[1600,512]{1,0:T(8,128)}), f32[6400,512]{1,0:T(8,128)}) %all-gather.6.cloned.1.call-update) | async-done | bytes 13107216 | tf_op jit(solution)/shard_map/all_gather | solution.py:308
  170.4 13.1 %shard_map.48 = (bf16[6400,512]{1,0:T(8,128)(2,1)}, bf16[6400,512]{1,0:T(8,128)(2,1)}) custom-call(f32[4,1600,512]{2,1,0:T(8,128)} %bitcast.7), custom_call_target="tpu_custom_call" | custom-call | flops 6553600 | bytes 26214400 | tf_op jit(solution)/shard_map/pallas_call | solution.py:311
  183.5 19.9 %all-to-all-done.refs_0_ = f32[8,8,20000]{2,1,0:T(8,128)} async-done(((f32[8,8,20000]{2,1,0:T(8,128)}), f32[8,8,20000]{2,1,0:T(8,128)}, u32[]{:S(2)}, u32[]{:S(2)}) %all-to-all-start) | async-done | bytes 5120032 | tf_op jit(solution)/shard_map/all_to_all | solution.py:275
  203.4 33.6 %shard_map.49 = (f32[8,200,800]{2,1,0:T(8,128)}, f32[8,8,10400]{2,1,0:T(8,128)}, f32[8,24,3200]{2,1,0:T(8,128)}) custom-call(f32[8,8,20000]{2,1,0:T(8,128)} %all-to-all-done.refs_0_, bf16[6400,512]{1,0:T(8,128)(2,1)} %get-tuple-element.45.refs_1_.refs_0_.refs_5_.refs_10_, bf16[6400,512]{1,0:T(8,128)(2,1)} %get-tuple-element.46.refs_2_.refs_1_.refs_6_.refs_11_, ...), custom_call_target="tpu_custom_call" | custom-call | flops 9093120000 | bytes 28467200 | tf_op jit(solution)/shard_map/pallas_call | solution.py:35
  237.0 4.0 all-to-all-start.1
  241.0 0.6 neg.13
  241.6 31.0 %shard_map.50 = f32[8,8,20000]{2,1,0:T(8,128)} custom-call(f32[8,200,800]{2,1,0:T(8,128)} %get-tuple-element.47.x_ref, bf16[6400,512]{1,0:T(8,128)(2,1)} %get-tuple-element.45.refs_1_.refs_0_.refs_5_.refs_10_, bf16[6400,512]{1,0:T(8,128)(2,1)} %get-tuple-element.46.refs_2_.refs_1_.refs_6_.refs_11_, f32[1,512]{1,0:T(1,128)} %bitcast.9, ...), custom_call_target="tpu_custom_call" | custom-call | flops 9093120000 | bytes 28467200 | tf_op jit(solution)/shard_map/pallas_call | solution.py:35
  272.6 28.3 %shard_map.51.refs_1_ = f32[4,200,1600]{2,1,0:T(8,128)} custom-call(s32[1]{0:T(128)} %bitcast.me_ref.refs_0_, f32[8,40000]{1,0:T(8,128)} %get-tuple-element.50.refs_1_, f32[8,40000]{1,0:T(8,128)} %collective-permute-done.refs_2_, f32[8,40000]{1,0:T(8,128)} %collective-permute-done.1.refs_3_, f32[8,40000]{1,0:T(8,128)} %collective-permute-done.2.refs_4_, ...), custom_call_target="tpu_custom_call" | custom-call | flops 9093120000 | bytes 28467200 | tf_op jit(solution)/shard_map/pallas_call | solution.py:35
  300.9 0.3 all-to-all-done.1.x_ref
  301.2 1.5 copy-done
  302.7 5.1 all-to-all-start.2
  307.8 5.1 shard_map.52
  312.9 1.8 collective-permute-start.3
  314.7 0.8 collective-permute-start.4
  315.5 13.8 %collective-permute-done.3.refs_3_ = f32[8,20800]{1,0:T(8,128)S(1)} collective-permute-done((f32[8,20800]{1,0:T(8,128)}, f32[8,20800]{1,0:T(8,128)S(1)}, u32[]{:S(2)}, u32[]{:S(2)}) %collective-permute-start.3) | collective-permute-done | bytes 665632 | tf_op jit(solution)/shard_map/ppermute | solution.py:266
  329.3 15.9 %collective-permute-done.4.refs_4_ = f32[8,20800]{1,0:T(8,128)S(1)} collective-permute-done((f32[8,20800]{1,0:T(8,128)}, f32[8,20800]{1,0:T(8,128)S(1)}, u32[]{:S(2)}, u32[]{:S(2)}) %collective-permute-start.4) | collective-permute-done | bytes 665632 | tf_op jit(solution)/shard_map/ppermute | solution.py:266
  345.1 0.6 collective-permute-done.5.refs_5_
  345.7 17.0 %all-to-all-done.2.x_ref = f32[8,24,3200]{2,1,0:T(8,128)} async-done(((f32[8,24,3200]{2,1,0:T(8,128)}), f32[8,24,3200]{2,1,0:T(8,128)}, u32[]{:S(2)}, u32[]{:S(2)}) %all-to-all-start.2) | async-done | bytes 2457632 | tf_op jit(solution)/shard_map/all_to_all | solution.py:275
  362.7 5.0 all-to-all-start.3
  367.8 4.7 shard_map.53
  372.4 2.8 collective-permute-start.6
  375.2 0.4 collective-permute-start.7
  375.6 0.2 collective-permute-start.8
  375.8 12.8 %collective-permute-done.6.refs_7_ = f32[200,768]{1,0:T(8,128)S(1)} collective-permute-done((f32[200,768]{1,0:T(8,128)}, f32[200,768]{1,0:T(8,128)S(1)}, u32[]{:S(2)}, u32[]{:S(2)}) %collective-permute-start.6) | collective-permute-done | bytes 614432 | tf_op jit(solution)/shard_map/ppermute | solution.py:266
  388.6 14.3 %collective-permute-done.7.refs_8_ = f32[200,768]{1,0:T(8,128)S(1)} collective-permute-done((f32[200,768]{1,0:T(8,128)}, f32[200,768]{1,0:T(8,128)S(1)}, u32[]{:S(2)}, u32[]{:S(2)}) %collective-permute-start.7) | collective-permute-done | bytes 614432 | tf_op jit(solution)/shard_map/ppermute | solution.py:266
  402.9 0.6 collective-permute-done.8.refs_9_
  403.5 0.3 copy-done.10
  403.8 0.5 copy-done.11
  404.3 32.6 %shard_map.54 = (f32[8,40000]{1,0:T(8,128)}, f32[8,40000]{1,0:T(8,128)}, f32[8,40000]{1,0:T(8,128)}, f32[8,40000]{1,0:T(8,128)}) custom-call(s32[1]{0:T(128)} %bitcast.me_ref.refs_0_, f32[4,200,1600]{2,1,0:T(8,128)} %shard_map.51.refs_1_, f32[8,20800]{1,0:T(8,128)} %get-tuple-element.55.refs_2_, f32[8,20800]{1,0:T(8,128)} %copy-done.6, ...), custom_call_target="tpu_custom_call" | custom-call | flops 9093120000 | bytes 28467200 | tf_op jit(solution)/shard_map/pallas_call | solution.py:35
  436.9 1.1 collective-permute-start.10
  438.0 2.0 collective-permute-start.9
  440.0 27.0 %collective-permute-done.10.refs_2_ = f32[8,40000]{1,0:T(8,128)S(1)} collective-permute-done((f32[8,40000]{1,0:T(8,128)}, f32[8,40000]{1,0:T(8,128)S(1)}, u32[]{:S(2)}, u32[]{:S(2)}) %collective-permute-start.10) | collective-permute-done | bytes 1280032 | tf_op jit(solution)/shard_map/ppermute | solution.py:266
  467.0 27.4 %collective-permute-done.11.refs_3_ = f32[8,40000]{1,0:T(8,128)S(1)} collective-permute-done((f32[8,40000]{1,0:T(8,128)}, f32[8,40000]{1,0:T(8,128)S(1)}, u32[]{:S(2)}, u32[]{:S(2)}) %collective-permute-start.11) | collective-permute-done | bytes 1280032 | tf_op jit(solution)/shard_map/ppermute | solution.py:266
  494.4 1.0 copy-done.2
  495.5 14.6 %shard_map.55 = f32[800,1600]{1,0:T(8,128)} custom-call(s32[1]{0:T(128)} %bitcast.me_ref.refs_0_, f32[800,1600]{1,0:T(8,128)} %x_ref.3, f32[8,8,20000]{2,1,0:T(8,128)} %all-to-all-done.3.crossed_ref, f32[8,40000]{1,0:T(8,128)} %get-tuple-element.65.refs_0_, f32[8,40000]{1,0:T(8,128)} %collective-permute-done.9.refs_1_, f32[8,40000]{1,0:T(8,128)} %copy-done.1, ...), custom_call_target="tpu_custom_call" | custom-call | bytes 20480000 | tf_op jit(solution)/shard_map/pallas_call | solution.py:35
  (30 shorter events, 0.1 us)
Async XLA Ops:
  6.5 10.6 %copy-start.3 = (f32[10,20,512]{2,1,0:T(8,128)S(1)}, f32[10,20,512]{2,1,0:T(8,128)}, u32[]{:S(2)}) copy-start(f32[10,20,512]{2,1,0:T(8,128)} %param.6) | copy-start | bytes 1228804
  6.5 76.7 %all-gather.4.cloned.1.call-start = ((), (), s32[]{:S(2)}) async-start(), calls=%async_computation.4 | async-start | bytes 3686400 | tf_op jit(solution)/shard_map/all_gather | solution.py:304
  18.0 152.4 %all-gather.6.cloned.1.call-start = ((), (), s32[]{:S(2)}) async-start(), calls=%async_computation.5 | async-start | bytes 16384000 | tf_op jit(solution)/shard_map/all_gather | solution.py:308
  24.9 30.4 %collective-permute-start = (f32[8,40000]{1,0:T(8,128)}, f32[8,40000]{1,0:T(8,128)}, u32[]{:S(2)}, u32[]{:S(2)}) collective-permute-start(f32[8,40000]{1,0:T(8,128)} %get-tuple-element.41), channel_id=1, source_target_pairs={{0,1},{1,2},{2,3},{3,0},{4,5},{5,6},{6,7},{7,4},{8,9},{9,10},{10,1... | collective-permute-start | bytes 3840008 | tf_op jit(solution)/shard_map/ppermute | solution.py:266
  27.5 55.2 %collective-permute-start.1 = (f32[8,40000]{1,0:T(8,128)}, f32[8,40000]{1,0:T(8,128)}, u32[]{:S(2)}, u32[]{:S(2)}) collective-permute-start(f32[8,40000]{1,0:T(8,128)} %get-tuple-element.42), channel_id=1, source_target_pairs={{0,2},{1,3},{2,0},{3,1},{4,6},{5,7},{6,4},{7,5},{8,10},{9,11},{10,... | collective-permute-start | bytes 3840008 | tf_op jit(solution)/shard_map/ppermute | solution.py:266
  27.5 55.7 %collective-permute-start.2 = (f32[8,40000]{1,0:T(8,128)}, f32[8,40000]{1,0:T(8,128)}, u32[]{:S(2)}, u32[]{:S(2)}) collective-permute-start(f32[8,40000]{1,0:T(8,128)} %get-tuple-element.43), channel_id=1, source_target_pairs={{0,3},{1,0},{2,1},{3,2},{4,7},{5,4},{6,5},{7,6},{8,11},{9,8},{10,9... | collective-permute-start | bytes 3840008 | tf_op jit(solution)/shard_map/ppermute | solution.py:266
  83.2 6.3 %copy-start.4 = (f32[80,80]{1,0:T(8,128)S(1)}, f32[80,80]{1,0:T(8,128)}, u32[]{:S(2)}) copy-start(f32[80,80]{1,0:T(8,128)} %param.5) | copy-start | bytes 76804
  83.2 120.1 %all-to-all-start = ((f32[8,8,20000]{2,1,0:T(8,128)}), f32[8,8,20000]{2,1,0:T(8,128)}, u32[]{:S(2)}, u32[]{:S(2)}) async-start(f32[8,8,20000]{2,1,0:T(8,128)} %get-tuple-element.37), calls=%async_computation | async-start | bytes 10289152 | tf_op jit(solution)/shard_map/all_to_all | solution.py:275
  237.0 4.0 copy-start.5
  237.0 64.3 %all-to-all-start.1 = ((f32[8,8,10400]{2,1,0:T(8,128)}), f32[8,8,10400]{2,1,0:T(8,128)S(1)}, u32[]{:S(2)}, u32[]{:S(2)}) async-start(f32[8,8,10400]{2,1,0:T(8,128)} %get-tuple-element.49), calls=%async_computation.1 | async-start | bytes 5373952 | tf_op jit(solution)/shard_map/all_to_all | solution.py:275
  301.2 1.5 copy-start
  302.7 60.0 %all-to-all-start.2 = ((f32[8,24,3200]{2,1,0:T(8,128)}), f32[8,24,3200]{2,1,0:T(8,128)}, u32[]{:S(2)}, u32[]{:S(2)}) async-start(f32[8,24,3200]{2,1,0:T(8,128)} %get-tuple-element.54), calls=%async_computation.2 | async-start | bytes 4915200 | tf_op jit(solution)/shard_map/all_to_all | solution.py:275
  312.9 16.4 %collective-permute-start.3 = (f32[8,20800]{1,0:T(8,128)}, f32[8,20800]{1,0:T(8,128)S(1)}, u32[]{:S(2)}, u32[]{:S(2)}) collective-permute-start(f32[8,20800]{1,0:T(8,128)} %get-tuple-element.56), channel_id=1, source_target_pairs={{0,1},{1,2},{2,3},{3,0},{4,5},{5,6},{6,7},{7,4},{8,9},{9,10},{10,1... | collective-permute-start | bytes 1996808 | tf_op jit(solution)/shard_map/ppermute | solution.py:266
  314.7 30.4 %collective-permute-start.4 = (f32[8,20800]{1,0:T(8,128)}, f32[8,20800]{1,0:T(8,128)S(1)}, u32[]{:S(2)}, u32[]{:S(2)}) collective-permute-start(f32[8,20800]{1,0:T(8,128)} %get-tuple-element.57), channel_id=1, source_target_pairs={{0,2},{1,3},{2,0},{3,1},{4,6},{5,7},{6,4},{7,5},{8,10},{9,11},{10,... | collective-permute-start | bytes 1996808 | tf_op jit(solution)/shard_map/ppermute | solution.py:266
  315.5 30.2 %collective-permute-start.5 = (f32[8,20800]{1,0:T(8,128)}, f32[8,20800]{1,0:T(8,128)S(1)}, u32[]{:S(2)}, u32[]{:S(2)}) collective-permute-start(f32[8,20800]{1,0:T(8,128)} %get-tuple-element.58), channel_id=1, source_target_pairs={{0,3},{1,0},{2,1},{3,2},{4,7},{5,4},{6,5},{7,6},{8,11},{9,8},{10,9... | collective-permute-start | bytes 1996808 | tf_op jit(solution)/shard_map/ppermute | solution.py:266
  329.3 33.4 %copy-start.6 = (f32[8,20800]{1,0:T(8,128)}, f32[8,20800]{1,0:T(8,128)S(1)}, u32[]{:S(2)}) copy-start(f32[8,20800]{1,0:T(8,128)S(1)} %collective-permute-done.3.refs_3_) | copy-start | bytes 1996804
  345.1 17.6 %copy-start.7 = (f32[8,20800]{1,0:T(8,128)}, f32[8,20800]{1,0:T(8,128)S(1)}, u32[]{:S(2)}) copy-start(f32[8,20800]{1,0:T(8,128)S(1)} %collective-permute-done.4.refs_4_) | copy-start | bytes 1996804
  345.7 17.0 %copy-start.8 = (f32[8,20800]{1,0:T(8,128)}, f32[8,20800]{1,0:T(8,128)S(1)}, u32[]{:S(2)}) copy-start(f32[8,20800]{1,0:T(8,128)S(1)} %collective-permute-done.5.refs_5_) | copy-start | bytes 1996804
  362.7 131.7 %all-to-all-start.3 = ((f32[8,8,20000]{2,1,0:T(8,128)}), f32[8,8,20000]{2,1,0:T(8,128)}, u32[]{:S(2)}, u32[]{:S(2)}) async-start(f32[8,8,20000]{2,1,0:T(8,128)} %shard_map.50), calls=%async_computation.3 | async-start | bytes 10289152 | tf_op jit(solution)/shard_map/all_to_all | solution.py:275
  372.4 16.2 %collective-permute-start.6 = (f32[200,768]{1,0:T(8,128)}, f32[200,768]{1,0:T(8,128)S(1)}, u32[]{:S(2)}, u32[]{:S(2)}) collective-permute-start(f32[200,768]{1,0:T(8,128)} %get-tuple-element.62), channel_id=1, source_target_pairs={{0,1},{1,2},{2,3},{3,0},{4,5},{5,6},{6,7},{7,4},{8,9},{9,10},{10,1... | collective-permute-start | bytes 1843208 | tf_op jit(solution)/shard_map/ppermute | solution.py:266
  375.2 27.7 %collective-permute-start.7 = (f32[200,768]{1,0:T(8,128)}, f32[200,768]{1,0:T(8,128)S(1)}, u32[]{:S(2)}, u32[]{:S(2)}) collective-permute-start(f32[200,768]{1,0:T(8,128)} %get-tuple-element.63), channel_id=1, source_target_pairs={{0,2},{1,3},{2,0},{3,1},{4,6},{5,7},{6,4},{7,5},{8,10},{9,11},{10,... | collective-permute-start | bytes 1843208 | tf_op jit(solution)/shard_map/ppermute | solution.py:266
  375.6 27.9 %collective-permute-start.8 = (f32[200,768]{1,0:T(8,128)}, f32[200,768]{1,0:T(8,128)S(1)}, u32[]{:S(2)}, u32[]{:S(2)}) collective-permute-start(f32[200,768]{1,0:T(8,128)} %get-tuple-element.64), channel_id=1, source_target_pairs={{0,3},{1,0},{2,1},{3,2},{4,7},{5,4},{6,5},{7,6},{8,11},{9,8},{10,9... | collective-permute-start | bytes 1843208 | tf_op jit(solution)/shard_map/ppermute | solution.py:266
  388.6 14.8 %copy-start.9 = (f32[200,768]{1,0:T(8,128)}, f32[200,768]{1,0:T(8,128)S(1)}, u32[]{:S(2)}) copy-start(f32[200,768]{1,0:T(8,128)S(1)} %collective-permute-done.6.refs_7_) | copy-start | bytes 1843204
  402.9 0.9 copy-start.10
  403.5 0.8 copy-start.11
  436.9 30.1 %collective-permute-start.10 = (f32[8,40000]{1,0:T(8,128)}, f32[8,40000]{1,0:T(8,128)S(1)}, u32[]{:S(2)}, u32[]{:S(2)}) collective-permute-start(f32[8,40000]{1,0:T(8,128)} %get-tuple-element.67), channel_id=1, source_target_pairs={{0,2},{1,3},{2,0},{3,1},{4,6},{5,7},{6,4},{7,5},{8,10},{9,11},{10,... | collective-permute-start | bytes 3840008 | tf_op jit(solution)/shard_map/ppermute | solution.py:266
  438.0 56.4 %collective-permute-start.11 = (f32[8,40000]{1,0:T(8,128)}, f32[8,40000]{1,0:T(8,128)S(1)}, u32[]{:S(2)}, u32[]{:S(2)}) collective-permute-start(f32[8,40000]{1,0:T(8,128)} %get-tuple-element.68), channel_id=1, source_target_pairs={{0,3},{1,0},{2,1},{3,2},{4,7},{5,4},{6,5},{7,6},{8,11},{9,8},{10,9... | collective-permute-start | bytes 3840008 | tf_op jit(solution)/shard_map/ppermute | solution.py:266
  438.0 56.4 %collective-permute-start.9 = (f32[8,40000]{1,0:T(8,128)}, f32[8,40000]{1,0:T(8,128)}, u32[]{:S(2)}, u32[]{:S(2)}) collective-permute-start(f32[8,40000]{1,0:T(8,128)} %get-tuple-element.66), channel_id=1, source_target_pairs={{0,1},{1,2},{2,3},{3,0},{4,5},{5,6},{6,7},{7,4},{8,9},{9,10},{10,1... | collective-permute-start | bytes 3840008 | tf_op jit(solution)/shard_map/ppermute | solution.py:266
  467.0 27.4 %copy-start.1 = (f32[8,40000]{1,0:T(8,128)}, f32[8,40000]{1,0:T(8,128)S(1)}, u32[]{:S(2)}) copy-start(f32[8,40000]{1,0:T(8,128)S(1)} %collective-permute-done.10.refs_2_) | copy-start | bytes 3840004
  494.4 1.1 copy-start.2
Sparse Core Ops, SparseCore 0:
  18.1 63.1 all-gather.3
  83.4 86.9 all-gather.5

commit v8 on v7

--- a/solution.py
+++ b/solution.py
@@ -71,7 +71,7 @@
 
 
 def halved(batch):
-    cut = -(-batch // 16) * 8
+    cut = -(-batch * 16 // 25 // 8) * 8
     return [(0, cut), (cut, batch)] if cut < batch else [(0, batch)]
 
 
@@ -94,15 +94,16 @@
     return jnp.concatenate(parts, axis=0) if len(parts) > 1 else parts[0]
 
 
-def cross_body(n, x_ref, crossed_ref, out_ref):
+def cross_body(n, spans, x_ref, crossed_ref, *outs):
     rows = tiles(x_ref.shape[0], n)
     for k in tiles(x_ref.shape[1], n):
         crossed_ref[k, :] = jnp.concatenate([x_ref[i, k] for i in rows], axis=1)
-    count = out_ref.shape[0]
+    count = outs[0].shape[0]
     batch = crossed_ref.shape[0] // count
     for b in range(count):
-        block = crossed_ref[b * batch : (b + 1) * batch, :]
-        out_ref[b] = fold(block, out_ref.shape[1:])
+        for (start, stop), out_ref in zip(spans, outs):
+            block = crossed_ref[b * batch + start : b * batch + stop, :]
+            out_ref[b] = fold(block, out_ref.shape[1:])
 
 
 def turn_body(me_ref, x_ref, *refs):
@@ -127,14 +128,17 @@
     hand_out(me_ref, stage, outs)
 
 
-def finish_body(n, me_ref, x_ref, crossed_ref, *refs):
-    *ins, out_ref, arrived, stage, total = refs
+def finish_body(n, parts, me_ref, x_ref, crossed_ref, *refs):
+    stages, (arrived, total) = refs[-2 - parts : -2], refs[-2:]
+    *ins, out_ref = refs[: -2 - parts]
     for b in range(arrived.shape[0]):
         arrived[b] = unfold(crossed_ref.at[b], arrived.shape[2])
-    take_in(me_ref, ins, stage)
+    count = len(ins) // parts
+    for h, stage in enumerate(stages):
+        take_in(me_ref, ins[h * count : (h + 1) * count], stage)
     for strip in tiles(total.shape[0]):
-        turned = jnp.concatenate([stage[b, :, strip] for b in range(len(ins))], axis=0)
-        total[strip, :] = rows_of(arrived, strip) + turned.T
+        turned = [stage[b, :, strip] for b in range(count) for stage in stages]
+        total[strip, :] = rows_of(arrived, strip) + jnp.concatenate(turned, axis=0).T
     cols = tiles(x_ref.shape[1], n)
     for i in tiles(x_ref.shape[0], n):
         out_ref[i, :] = x_ref[i, :] + jnp.concatenate([total[k, i] for k in cols], axis=1)
@@ -207,25 +211,22 @@
     lax.fori_loop(0, blocks, result, 0)
 
 
-def send_left(spans, stage, outs):
-    for b in range(stage.shape[0]):
-        for (start, stop), out_ref in zip(spans, outs):
-            out_ref[b] = fold(stage[b, start:stop, :], out_ref.shape[1:])
-
-
-def left_body(n, spans, x_ref, *refs):
-    *consts, out_ref = refs[:6]
-    outs, (stage, xp, zp) = refs[6 : 6 + len(spans)], refs[6 + len(spans) :]
+def left_body(n, x_ref, *refs):
+    *consts, out_ref, sent_ref, stage, xp, zp = refs
     for b in range(stage.shape[0]):
         stage[b] = unfold(x_ref.at[b], stage.shape[2])
     apply_operator(n, 0.0, 1.0, stage, out_ref, *consts, xp, zp)
-    send_left(spans, out_ref, outs)
-
-
-def left_again_body(n, x_ref, *refs):
-    *consts, out_ref, stage, xp, zp = refs
-    apply_operator(n, time_step, time_step * time_step / 2.0, x_ref, stage, *consts, xp, zp)
-    send_left([(0, stage.shape[1])], stage, [out_ref])
+    for b in range(stage.shape[0]):
+        sent_ref[b] = fold(out_ref[b], sent_ref.shape[1:])
+
+
+def left_again_body(n, spans, *refs):
+    parts, (*consts, out_ref, stage, xp, zp) = refs[: len(spans)], refs[len(spans) :]
+    for (start, stop), part in zip(spans, parts):
+        stage[:, start:stop, :] = part[...]
+    apply_operator(n, time_step, time_step * time_step / 2.0, stage, stage, *consts, xp, zp)
+    for b in range(stage.shape[0]):
+        out_ref[b] = fold(stage[b], out_ref.shape[1:])
 
 
 def right_body(n, count, me_ref, *refs):
@@ -236,7 +237,7 @@
     )
 
 
-def right_again_body(n, count, rows, spans, me_ref, base_ref, *refs):
+def right_again_body(n, count, rows, spans, span, me_ref, base_ref, *refs):
     split = count * len(spans)
     ins, consts, outs = refs[:split], refs[split : split + 5], refs[split + 5 : split + 5 + count]
     stage, xp, zp, *arrived = refs[split + 5 + count :]
@@ -245,11 +246,11 @@
     sizes = [stop - start for start, stop in spans]
     for b in range(count):
         parts = [
-            part[b, :, r * size : (r + 1) * size]
+            part[b, span, r * size : (r + 1) * size]
             for r in range(rows)
             for part, size in zip(arrived, sizes)
         ]
-        stage[b] = base_ref[b] + (time_step * time_step) * jnp.concatenate(parts, axis=1)
+        stage[b] = base_ref[b, span] + (time_step * time_step) * jnp.concatenate(parts, axis=1)
     apply_operator(n, 0.0, 1.0, stage, stage, *consts, xp, zp)
     hand_out(me_ref, stage, outs)
 
@@ -294,15 +295,18 @@
 
     row_stage, col_stage = pltpu.VMEM(row_block, f32), pltpu.VMEM(col_block, f32)
 
-    crossed, mine = call(
-        functools.partial(cross_body, n),
-        [jax.ShapeDtypeStruct((local_cols, local_rows), f32), row_wire(row_block[1])],
+    crossed, *sent = call(
+        functools.partial(cross_body, n, spans),
+        [jax.ShapeDtypeStruct((local_cols, local_rows), f32)]
+        + [row_wire(b - a) for a, b in spans],
         [pairs], moved=12 * size,
     )
 
-    aux = after(aux, mine)
+    aux = after(aux, sent)
     whole = lax.all_gather(aux.reshape(-1, naux), "row", axis=0, tiled=True)
-    mine = exchange(mine, "row")
+    mine = []
+    for part in sent:
+        mine.append(exchange(after(part, mine) if mine else part, "row"))
     turned = call(turn_body, col_wires(local_cols), [me, crossed], [col_stage], moved=8 * size)
     theirs = shift(turned, "col")
     whole = lax.all_gather(after(whole, theirs), "col", axis=0, tiled=False)
@@ -339,12 +343,19 @@
     row_consts = [gain, left, right]
     col_consts = [-gain, right, left]
 
-    first, *parts = operator(
-        lambda n, *refs: left_body(n, spans, *refs),
-        [mine], row_consts,
-        [jax.ShapeDtypeStruct(row_block, f32)] + [row_wire(b - a) for a, b in spans], row_block,
-    )
-    double = operator(left_again_body, [first], row_consts, row_wire(row_block[1]), row_block)
+    first, parts = [], []
+    for (start, stop), part in zip(spans, mine):
+        block = (rows, stop - start, local_rows)
+        outs = [jax.ShapeDtypeStruct(block, f32), row_wire(stop - start)]
+        result, leaving = operator(
+            left_body, [after(part, parts) if parts else part], row_consts, outs, block
+        )
+        first.append(result)
+        parts.append(leaving)
+    double = operator(
+        lambda n, *refs: left_again_body(n, spans, *refs),
+        first, row_consts, row_wire(row_block[1]), row_block,
+    )
     base = operator(
         lambda n, *refs: right_body(n, cols, *refs),
         [me, *after(theirs, double)], col_consts, jax.ShapeDtypeStruct(col_block, f32), col_block,
@@ -366,18 +377,23 @@
         )
         arriving += shift(turned, "col")
     double = exchange(double, "row")
-    last = operator(
-        lambda n, *refs: right_again_body(n, cols, rows, spans, *refs),
-        [me, base, *arriving], col_consts, col_wires(local_cols), col_block,
-        [pltpu.VMEM((*col_block[:2], rows * (b - a)), f32) for a, b in spans],
-    )
-    last = shift(last, "col")
+    last, stages = [], []
+    for start, stop in [(0, col_block[1])]:
+        block = (cols, stop - start, local_cols)
+        outs = operator(
+            lambda n, *refs: right_again_body(n, cols, rows, spans, slice(start, stop), *refs),
+            [me, base, *arriving], col_consts,
+            [jax.ShapeDtypeStruct(wire(stop - start, local_cols), f32)] * cols, block,
+            [pltpu.VMEM((*col_block[:2], rows * (b - a)), f32) for a, b in spans],
+        )
+        last += shift(outs, "col")
+        stages.append(pltpu.VMEM(block, f32))
 
     return call(
-        functools.partial(finish_body, n),
+        functools.partial(finish_body, n, len(stages)),
         jax.ShapeDtypeStruct(pairs.shape, f32),
         [me, pairs, double, *last],
-        [row_stage, col_stage, pltpu.VMEM((local_cols, local_rows), f32)],
+        [*stages, row_stage, pltpu.VMEM((local_cols, local_rows), f32)],
         moved=16 * size,
     )
 

time: 526 us -> 508 us (0.966)
  waiting for transfers between devices: 285 us -> 169 us
  blocking collectives: 0 us -> 79.5 us
  Pallas kernels: 180 us -> 198 us
    all_to_all x0 -> x1, blocking collectives: none -> 79.5 us  [exchange(): return lax.all_to_all(x, axis, split_axis=0, concat_axis=0, tiled=True)]
    all_gather x1, waiting for transfers between devices: 80 us -> 2.45 us  [shards(): whole = lax.all_gather(after(whole, theirs), 'col', axis=0, tiled=False)]
    all_to_all x4, waiting for transfers between devices: 37.3 us -> 0.01 us  [exchange(): return lax.all_to_all(x, axis, split_axis=0, concat_axis=0, tiled=True)]
    pallas_call x9 -> x10, Pallas kernels: 167 us -> 185 us  [call(): pl.pallas_call(body, in_specs=[smem if x.dtype == jnp.int32 else vmem for...]
  transfers between devices with their start and end apart: 18 -> 18, of which waited for: 15 -> 12; matrix products, arithmetic and copies ran while one was open for 0% -> 0% of each run, Pallas kernels for 24% -> 35%
where the time goes in v8:
time: 508 us; the launch traced here: 500 us
  Pallas kernels  198 us (39%)
  waiting for transfers between devices  169 us (33%)
  blocking collectives  79.5 us (16%)
  starting transfers between devices  30.9 us (6%)
  between operations  14 us (3%)
  local copies, waits for them, and re-layouts  6.69 us (1%)
    pallas_call x10, Pallas kernels, call(): pl.pallas_call(body, in_specs=[smem if x.dtype == jnp.int32 else vmem for...  185 us
    ppermute x12, waiting for transfers between devices, shift(): lax.ppermute(parts[s], axis, [(d, (d + s) % n) for d in range(n)])  167 us
    all_to_all x1, blocking collectives, exchange(): return lax.all_to_all(x, axis, split_axis=0, concat_axis=0, tiled=True)  79.5 us
    all_to_all x4, starting transfers between devices, exchange(): return lax.all_to_all(x, axis, split_axis=0, concat_axis=0, tiled=True)  21.1 us
    pallas_call x1, Pallas kernels, shards(): pl.pallas_call(functools.partial(split_body, n), grid=(n // group,), in_s...  13.1 us
  transfers between devices with their start and end apart: 18, of which 12 were waited for; matrix products, arithmetic and copies ran while one was open for 0% of the time, Pallas kernels for 35%

profile of v8, /device:TPU:1, one launch (start us, length us, event | category | flops | bytes accessed | tf_op | source)
XLA Modules:
  0.0 499.7 jit_solution(17169180613898967786)
XLA Ops:
  6.5 10.3 %shard_map.46 = (f32[1600,800]{1,0:T(8,128)}, f32[8,32,3200]{2,1,0:T(8,128)}, f32[8,24,2400]{2,1,0:T(8,128)}) custom-call(f32[800,1600]{1,0:T(8,128)} %x_ref.3), custom_call_target="tpu_custom_call" | custom-call | bytes 15360000 | tf_op jit(solution)/shard_map/pallas_call | solution.py:35
  16.9 0.8 reshape.11
  17.7 0.0 all-gather.6.cloned.1.call-start
  17.8 6.9 %shard_map.47 = (f32[8,40000]{1,0:T(8,128)}, f32[8,40000]{1,0:T(8,128)}, f32[8,40000]{1,0:T(8,128)}, f32[8,40000]{1,0:T(8,128)}) custom-call(s32[1]{0:T(128)} %bitcast.me_ref.refs_0_, f32[1600,800]{1,0:T(8,128)} %get-tuple-element.44.x_ref), custom_call_target="tpu_custom_call" | custom-call | bytes 10240000 | tf_op jit(solution)/shard_map/pallas_call | solution.py:35
  24.7 2.6 collective-permute-start
  27.3 0.4 collective-permute-start.2
  27.7 27.3 %collective-permute-done.refs_2_ = f32[8,40000]{1,0:T(8,128)} collective-permute-done((f32[8,40000]{1,0:T(8,128)}, f32[8,40000]{1,0:T(8,128)}, u32[]{:S(2)}, u32[]{:S(2)}) %collective-permute-start) | collective-permute-done | bytes 1280032 | tf_op jit(solution)/shard_map/ppermute | solution.py:267
  55.0 27.5 %collective-permute-done.1.refs_3_ = f32[8,40000]{1,0:T(8,128)} collective-permute-done((f32[8,40000]{1,0:T(8,128)}, f32[8,40000]{1,0:T(8,128)}, u32[]{:S(2)}, u32[]{:S(2)}) %collective-permute-start.1) | collective-permute-done | bytes 1280032 | tf_op jit(solution)/shard_map/ppermute | solution.py:267
  82.5 0.5 collective-permute-done.2.refs_4_
  83.0 79.5 %all_to_all.25.x_ref = f32[8,32,3200]{2,1,0:T(8,128)} all-to-all(f32[8,32,3200]{2,1,0:T(8,128)S(1)} %copy-done.2), channel_id=1, replica_groups=mesh['row'=8,'col'=4] {'row'}, dimensions={0} | all-to-all | bytes 6553600 | tf_op jit(solution)/shard_map/all_to_all | solution.py:276
  162.6 4.3 all-to-all-start.1
  166.8 0.1 copy.5
  167.0 0.8 pad_maximum_fusion
  167.7 2.5 all-gather.6.cloned.1.call-done
  170.2 13.1 %shard_map.48 = (bf16[6400,512]{1,0:T(8,128)(2,1)}, bf16[6400,512]{1,0:T(8,128)(2,1)}) custom-call(f32[4,1600,512]{2,1,0:T(8,128)} %bitcast.7), custom_call_target="tpu_custom_call" | custom-call | flops 6553600 | bytes 26214400 | tf_op jit(solution)/shard_map/pallas_call | solution.py:315
  183.3 27.0 %shard_map.49 = (f32[8,128,800]{2,1,0:T(8,128)}, f32[8,32,3200]{2,1,0:T(8,128)}) custom-call(f32[8,32,3200]{2,1,0:T(8,128)} %all_to_all.25.x_ref, bf16[6400,512]{1,0:T(8,128)(2,1)} %get-tuple-element.50.refs_0_.refs_2_.refs_5_.refs_10_, bf16[6400,512]{1,0:T(8,128)(2,1)} %get-tuple-element.51.refs_1_.refs_3_.refs_6_.refs_11_, f32[1,512]{1,0:T(1,128)} %bitcast.8, ...), custom_call_target="tpu_custom_call" | custom-call | flops 5819596800 | bytes 28467200 | tf_op jit(solution)/shard_map/pallas_call | solution.py:35
  210.3 1.3 copy-done.1
  211.5 5.4 %all-to-all-start.2 = ((f32[8,32,3200]{2,1,0:T(8,128)}), f32[8,32,3200]{2,1,0:T(8,128)S(1)}, u32[]{:S(2)}, u32[]{:S(2)}) async-start(f32[8,32,3200]{2,1,0:T(8,128)} %get-tuple-element.54), calls=%async_computation.2 | async-start | bytes 6553600 | tf_op jit(solution)/shard_map/all_to_all | solution.py:276
  217.0 0.6 neg.13
  217.6 25.0 %shard_map.50 = (f32[8,72,800]{2,1,0:T(8,128)}, f32[8,24,2400]{2,1,0:T(8,128)}) custom-call(f32[8,24,2400]{2,1,0:T(8,128)} %copy-done.1, bf16[6400,512]{1,0:T(8,128)(2,1)} %get-tuple-element.50.refs_0_.refs_2_.refs_5_.refs_10_, bf16[6400,512]{1,0:T(8,128)(2,1)} %get-tuple-element.51.refs_1_.refs_3_.refs_6_.refs_11_, f32[1,512]{1,0:T(1,128)} %bitcast.9, ...), custom_call_target="tpu_custom_call" | custom-call | flops 3273523200 | bytes 28467200 | tf_op jit(solution)/shard_map/pallas_call | solution.py:35
  242.6 31.4 %shard_map.51 = f32[8,8,20000]{2,1,0:T(8,128)} custom-call(f32[8,128,800]{2,1,0:T(8,128)} %get-tuple-element.52.refs_0_, f32[8,72,800]{2,1,0:T(8,128)} %get-tuple-element.56.refs_1_, bf16[6400,512]{1,0:T(8,128)(2,1)} %get-tuple-element.50.refs_0_.refs_2_.refs_5_.refs_10_, bf16[6400,512]{1,0:T(8,128)(2,1)} %get-tuple-element.51.refs_1_.refs_3_.refs_6_.refs_11_, ...), custom_call_target="tpu_custom_call" | custom-call | flops 9093120000 | bytes 28467200 | tf_op jit(solution)/shard_map/pallas_call | solution.py:35
  274.0 28.5 %shard_map.52.refs_1_ = f32[4,200,1600]{2,1,0:T(8,128)} custom-call(s32[1]{0:T(128)} %bitcast.me_ref.refs_0_, f32[8,40000]{1,0:T(8,128)} %get-tuple-element.58.refs_1_, f32[8,40000]{1,0:T(8,128)} %collective-permute-done.refs_2_, f32[8,40000]{1,0:T(8,128)} %collective-permute-done.1.refs_3_, f32[8,40000]{1,0:T(8,128)} %collective-permute-done.2.refs_4_, ...), custom_call_target="tpu_custom_call" | custom-call | flops 9093120000 | bytes 28467200 | tf_op jit(solution)/shard_map/pallas_call | solution.py:35
  302.5 1.7 copy-done
  304.2 5.7 %all-to-all-start.3 = ((f32[8,24,2400]{2,1,0:T(8,128)}), f32[8,24,2400]{2,1,0:T(8,128)}, u32[]{:S(2)}, u32[]{:S(2)}) async-start(f32[8,24,2400]{2,1,0:T(8,128)} %get-tuple-element.62), calls=%async_computation.3 | async-start | bytes 3735552 | tf_op jit(solution)/shard_map/all_to_all | solution.py:276
  310.0 5.9 %shard_map.53 = (f32[200,1024]{1,0:T(8,128)}, f32[200,1024]{1,0:T(8,128)}, f32[200,1024]{1,0:T(8,128)}, f32[200,1024]{1,0:T(8,128)}) custom-call(s32[1]{0:T(128)} %bitcast.me_ref.refs_0_, f32[8,32,3200]{2,1,0:T(8,128)} %copy-done), custom_call_target="tpu_custom_call" | custom-call | bytes 5120000 | tf_op jit(solution)/shard_map/pallas_call | solution.py:35
  315.9 1.3 collective-permute-start.3
  317.1 1.2 collective-permute-start.4
  318.3 16.6 %collective-permute-done.3.refs_3_ = f32[200,1024]{1,0:T(8,128)S(1)} collective-permute-done((f32[200,1024]{1,0:T(8,128)}, f32[200,1024]{1,0:T(8,128)S(1)}, u32[]{:S(2)}, u32[]{:S(2)}) %collective-permute-start.3) | collective-permute-done | bytes 819232 | tf_op jit(solution)/shard_map/ppermute | solution.py:267
  334.9 19.1 %collective-permute-done.4.refs_4_ = f32[200,1024]{1,0:T(8,128)S(1)} collective-permute-done((f32[200,1024]{1,0:T(8,128)}, f32[200,1024]{1,0:T(8,128)S(1)}, u32[]{:S(2)}, u32[]{:S(2)}) %collective-permute-start.4) | collective-permute-done | bytes 819232 | tf_op jit(solution)/shard_map/ppermute | solution.py:267
  354.0 0.6 collective-permute-done.5.refs_5_
  354.6 0.3 copy-done.9
  354.9 0.6 copy-done.10
  355.5 5.7 %all-to-all-start.4 = ((f32[8,8,20000]{2,1,0:T(8,128)}), f32[8,8,20000]{2,1,0:T(8,128)}, u32[]{:S(2)}, u32[]{:S(2)}) async-start(f32[8,8,20000]{2,1,0:T(8,128)} %shard_map.51), calls=%async_computation.4 | async-start | bytes 10289152 | tf_op jit(solution)/shard_map/all_to_all | solution.py:276
  361.2 4.0 shard_map.54
  365.2 0.2 collective-permute-start.6
  365.4 0.3 collective-permute-start.7
  365.7 0.6 collective-permute-start.8
  366.3 8.8 %collective-permute-done.6.refs_7_ = f32[8,14400]{1,0:T(8,128)S(1)} collective-permute-done((f32[8,14400]{1,0:T(8,128)}, f32[8,14400]{1,0:T(8,128)S(1)}, u32[]{:S(2)}, u32[]{:S(2)}) %collective-permute-start.6) | collective-permute-done | bytes 460832 | tf_op jit(solution)/shard_map/ppermute | solution.py:267
  375.1 10.0 %collective-permute-done.7.refs_8_ = f32[8,14400]{1,0:T(8,128)S(1)} collective-permute-done((f32[8,14400]{1,0:T(8,128)}, f32[8,14400]{1,0:T(8,128)S(1)}, u32[]{:S(2)}, u32[]{:S(2)}) %collective-permute-start.7) | collective-permute-done | bytes 460832 | tf_op jit(solution)/shard_map/ppermute | solution.py:267
  385.1 2.0 collective-permute-done.8.refs_9_
  387.1 0.8 copy-done.13
  387.9 31.2 %shard_map.55 = (f32[8,40000]{1,0:T(8,128)}, f32[8,40000]{1,0:T(8,128)}, f32[8,40000]{1,0:T(8,128)}, f32[8,40000]{1,0:T(8,128)}) custom-call(s32[1]{0:T(128)} %bitcast.me_ref.refs_0_, f32[4,200,1600]{2,1,0:T(8,128)} %shard_map.52.refs_1_, f32[200,1024]{1,0:T(8,128)} %get-tuple-element.63.refs_2_, f32[200,1024]{1,0:T(8,128)} %copy-done.8, ...), custom_call_target="tpu_custom_call" | custom-call | flops 9093120000 | bytes 28467200 | tf_op jit(solution)/shard_map/pallas_call | solution.py:35
  419.2 1.2 collective-permute-start.10
  420.3 2.0 collective-permute-start.9
  422.3 26.9 %collective-permute-done.10.refs_2_ = f32[8,40000]{1,0:T(8,128)S(1)} collective-permute-done((f32[8,40000]{1,0:T(8,128)}, f32[8,40000]{1,0:T(8,128)S(1)}, u32[]{:S(2)}, u32[]{:S(2)}) %collective-permute-start.10) | collective-permute-done | bytes 1280032 | tf_op jit(solution)/shard_map/ppermute | solution.py:267
  449.3 27.5 %collective-permute-done.11.refs_3_ = f32[8,40000]{1,0:T(8,128)S(1)} collective-permute-done((f32[8,40000]{1,0:T(8,128)}, f32[8,40000]{1,0:T(8,128)S(1)}, u32[]{:S(2)}, u32[]{:S(2)}) %collective-permute-start.11) | collective-permute-done | bytes 1280032 | tf_op jit(solution)/shard_map/ppermute | solution.py:267
  476.8 1.0 copy-done.4
  477.9 14.6 %shard_map.56 = f32[800,1600]{1,0:T(8,128)} custom-call(s32[1]{0:T(128)} %bitcast.me_ref.refs_0_, f32[800,1600]{1,0:T(8,128)} %x_ref.3, f32[8,8,20000]{2,1,0:T(8,128)} %all-to-all-done.4.crossed_ref, f32[8,40000]{1,0:T(8,128)} %get-tuple-element.73.refs_0_, f32[8,40000]{1,0:T(8,128)} %collective-permute-done.9.refs_1_, f32[8,40000]{1,0:T(8,128)} %copy-done.3, ...), custom_call_target="tpu_custom_call" | custom-call | bytes 20480000 | tf_op jit(solution)/shard_map/pallas_call | solution.py:35
  (36 shorter events, 0.1 us)
Async XLA Ops:
  6.5 10.3 %copy-start.5 = (f32[10,20,512]{2,1,0:T(8,128)S(1)}, f32[10,20,512]{2,1,0:T(8,128)}, u32[]{:S(2)}) copy-start(f32[10,20,512]{2,1,0:T(8,128)} %param.6) | copy-start | bytes 1228804
  6.5 76.5 %all-gather.4.cloned.1.call-start = ((), (), s32[]{:S(2)}) async-start(), calls=%async_computation.5 | async-start | bytes 3686400 | tf_op jit(solution)/shard_map/all_gather | solution.py:306
  17.7 152.4 %all-gather.6.cloned.1.call-start = ((), (), s32[]{:S(2)}) async-start(), calls=%async_computation.6 | async-start | bytes 16384000 | tf_op jit(solution)/shard_map/all_gather | solution.py:312
  24.7 58.4 %copy-start.2 = (f32[8,32,3200]{2,1,0:T(8,128)S(1)}, f32[8,32,3200]{2,1,0:T(8,128)}, u32[]{:S(2)}) copy-start(f32[8,32,3200]{2,1,0:T(8,128)} %get-tuple-element.41) | copy-start | bytes 9830404
  24.7 30.4 %collective-permute-start = (f32[8,40000]{1,0:T(8,128)}, f32[8,40000]{1,0:T(8,128)}, u32[]{:S(2)}, u32[]{:S(2)}) collective-permute-start(f32[8,40000]{1,0:T(8,128)} %get-tuple-element.46), channel_id=1, source_target_pairs={{0,1},{1,2},{2,3},{3,0},{4,5},{5,6},{6,7},{7,4},{8,9},{9,10},{10,1... | collective-permute-start | bytes 3840008 | tf_op jit(solution)/shard_map/ppermute | solution.py:267
  27.3 55.2 %collective-permute-start.1 = (f32[8,40000]{1,0:T(8,128)}, f32[8,40000]{1,0:T(8,128)}, u32[]{:S(2)}, u32[]{:S(2)}) collective-permute-start(f32[8,40000]{1,0:T(8,128)} %get-tuple-element.47), channel_id=1, source_target_pairs={{0,2},{1,3},{2,0},{3,1},{4,6},{5,7},{6,4},{7,5},{8,10},{9,11},{10,... | collective-permute-start | bytes 3840008 | tf_op jit(solution)/shard_map/ppermute | solution.py:267
  27.3 55.7 %collective-permute-start.2 = (f32[8,40000]{1,0:T(8,128)}, f32[8,40000]{1,0:T(8,128)}, u32[]{:S(2)}, u32[]{:S(2)}) collective-permute-start(f32[8,40000]{1,0:T(8,128)} %get-tuple-element.48), channel_id=1, source_target_pairs={{0,3},{1,0},{2,1},{3,2},{4,7},{5,4},{6,5},{7,6},{8,11},{9,8},{10,9... | collective-permute-start | bytes 3840008 | tf_op jit(solution)/shard_map/ppermute | solution.py:267
  162.6 4.3 copy-start.6
  162.6 47.7 %all-to-all-start.1 = ((f32[8,24,2400]{2,1,0:T(8,128)}), f32[8,24,2400]{2,1,0:T(8,128)S(1)}, u32[]{:S(2)}, u32[]{:S(2)}) async-start(f32[8,24,2400]{2,1,0:T(8,128)} %get-tuple-element.53), calls=%async_computation.1 | async-start | bytes 3735552 | tf_op jit(solution)/shard_map/all_to_all | solution.py:276
  210.3 1.3 copy-start.1
  210.3 6.7 %copy-start.7 = (f32[512]{0:T(512)S(1)}, f32[512]{0:T(512)}, u32[]{:S(2)}) copy-start(f32[512]{0:T(512)} %param.7) | copy-start | bytes 6148
  211.5 90.9 %all-to-all-start.2 = ((f32[8,32,3200]{2,1,0:T(8,128)}), f32[8,32,3200]{2,1,0:T(8,128)S(1)}, u32[]{:S(2)}, u32[]{:S(2)}) async-start(f32[8,32,3200]{2,1,0:T(8,128)} %get-tuple-element.54), calls=%async_computation.2 | async-start | bytes 6553600 | tf_op jit(solution)/shard_map/all_to_all | solution.py:276
  302.5 1.8 copy-start
  304.2 50.3 %all-to-all-start.3 = ((f32[8,24,2400]{2,1,0:T(8,128)}), f32[8,24,2400]{2,1,0:T(8,128)}, u32[]{:S(2)}, u32[]{:S(2)}) async-start(f32[8,24,2400]{2,1,0:T(8,128)} %get-tuple-element.62), calls=%async_computation.3 | async-start | bytes 3735552 | tf_op jit(solution)/shard_map/all_to_all | solution.py:276
  315.9 19.1 %collective-permute-start.3 = (f32[200,1024]{1,0:T(8,128)}, f32[200,1024]{1,0:T(8,128)S(1)}, u32[]{:S(2)}, u32[]{:S(2)}) collective-permute-start(f32[200,1024]{1,0:T(8,128)} %get-tuple-element.64), channel_id=1, source_target_pairs={{0,1},{1,2},{2,3},{3,0},{4,5},{5,6},{6,7},{7,4},{8,9},{9,10},{10,1... | collective-permute-start | bytes 2457608 | tf_op jit(solution)/shard_map/ppermute | solution.py:267
  317.1 36.9 %collective-permute-start.4 = (f32[200,1024]{1,0:T(8,128)}, f32[200,1024]{1,0:T(8,128)S(1)}, u32[]{:S(2)}, u32[]{:S(2)}) collective-permute-start(f32[200,1024]{1,0:T(8,128)} %get-tuple-element.65), channel_id=1, source_target_pairs={{0,2},{1,3},{2,0},{3,1},{4,6},{5,7},{6,4},{7,5},{8,10},{9,11},{10,... | collective-permute-start | bytes 2457608 | tf_op jit(solution)/shard_map/ppermute | solution.py:267
  318.3 36.3 %collective-permute-start.5 = (f32[200,1024]{1,0:T(8,128)}, f32[200,1024]{1,0:T(8,128)S(1)}, u32[]{:S(2)}, u32[]{:S(2)}) collective-permute-start(f32[200,1024]{1,0:T(8,128)} %get-tuple-element.66), channel_id=1, source_target_pairs={{0,3},{1,0},{2,1},{3,2},{4,7},{5,4},{6,5},{7,6},{8,11},{9,8},{10,9... | collective-permute-start | bytes 2457608 | tf_op jit(solution)/shard_map/ppermute | solution.py:267
  334.9 19.6 %copy-start.8 = (f32[200,1024]{1,0:T(8,128)}, f32[200,1024]{1,0:T(8,128)S(1)}, u32[]{:S(2)}) copy-start(f32[200,1024]{1,0:T(8,128)S(1)} %collective-permute-done.3.refs_3_) | copy-start | bytes 2457604
  354.0 0.9 copy-start.9
  354.6 0.9 copy-start.10
  355.5 121.3 %all-to-all-start.4 = ((f32[8,8,20000]{2,1,0:T(8,128)}), f32[8,8,20000]{2,1,0:T(8,128)}, u32[]{:S(2)}, u32[]{:S(2)}) async-start(f32[8,8,20000]{2,1,0:T(8,128)} %shard_map.51), calls=%async_computation.4 | async-start | bytes 10289152 | tf_op jit(solution)/shard_map/all_to_all | solution.py:276
  365.2 9.9 %collective-permute-start.6 = (f32[8,14400]{1,0:T(8,128)}, f32[8,14400]{1,0:T(8,128)S(1)}, u32[]{:S(2)}, u32[]{:S(2)}) collective-permute-start(f32[8,14400]{1,0:T(8,128)} %get-tuple-element.70), channel_id=1, source_target_pairs={{0,1},{1,2},{2,3},{3,0},{4,5},{5,6},{6,7},{7,4},{8,9},{9,10},{10,1... | collective-permute-start | bytes 1382408 | tf_op jit(solution)/shard_map/ppermute | solution.py:267
  365.4 19.7 %collective-permute-start.7 = (f32[8,14400]{1,0:T(8,128)}, f32[8,14400]{1,0:T(8,128)S(1)}, u32[]{:S(2)}, u32[]{:S(2)}) collective-permute-start(f32[8,14400]{1,0:T(8,128)} %get-tuple-element.71), channel_id=1, source_target_pairs={{0,2},{1,3},{2,0},{3,1},{4,6},{5,7},{6,4},{7,5},{8,10},{9,11},{10,... | collective-permute-start | bytes 1382408 | tf_op jit(solution)/shard_map/ppermute | solution.py:267
  365.7 21.4 %collective-permute-start.8 = (f32[8,14400]{1,0:T(8,128)}, f32[8,14400]{1,0:T(8,128)S(1)}, u32[]{:S(2)}, u32[]{:S(2)}) collective-permute-start(f32[8,14400]{1,0:T(8,128)} %get-tuple-element.72), channel_id=1, source_target_pairs={{0,3},{1,0},{2,1},{3,2},{4,7},{5,4},{6,5},{7,6},{8,11},{9,8},{10,9... | collective-permute-start | bytes 1382408 | tf_op jit(solution)/shard_map/ppermute | solution.py:267
  375.1 12.0 %copy-start.11 = (f32[8,14400]{1,0:T(8,128)}, f32[8,14400]{1,0:T(8,128)S(1)}, u32[]{:S(2)}) copy-start(f32[8,14400]{1,0:T(8,128)S(1)} %collective-permute-done.6.refs_7_) | copy-start | bytes 1382404
  385.1 2.0 copy-start.12
  387.1 0.8 copy-start.13
  419.2 30.1 %collective-permute-start.10 = (f32[8,40000]{1,0:T(8,128)}, f32[8,40000]{1,0:T(8,128)S(1)}, u32[]{:S(2)}, u32[]{:S(2)}) collective-permute-start(f32[8,40000]{1,0:T(8,128)} %get-tuple-element.75), channel_id=1, source_target_pairs={{0,2},{1,3},{2,0},{3,1},{4,6},{5,7},{6,4},{7,5},{8,10},{9,11},{10,... | collective-permute-start | bytes 3840008 | tf_op jit(solution)/shard_map/ppermute | solution.py:267
  420.3 56.5 %collective-permute-start.11 = (f32[8,40000]{1,0:T(8,128)}, f32[8,40000]{1,0:T(8,128)S(1)}, u32[]{:S(2)}, u32[]{:S(2)}) collective-permute-start(f32[8,40000]{1,0:T(8,128)} %get-tuple-element.76), channel_id=1, source_target_pairs={{0,3},{1,0},{2,1},{3,2},{4,7},{5,4},{6,5},{7,6},{8,11},{9,8},{10,9... | collective-permute-start | bytes 3840008 | tf_op jit(solution)/shard_map/ppermute | solution.py:267
  420.3 56.5 %collective-permute-start.9 = (f32[8,40000]{1,0:T(8,128)}, f32[8,40000]{1,0:T(8,128)}, u32[]{:S(2)}, u32[]{:S(2)}) collective-permute-start(f32[8,40000]{1,0:T(8,128)} %get-tuple-element.74), channel_id=1, source_target_pairs={{0,1},{1,2},{2,3},{3,0},{4,5},{5,6},{6,7},{7,4},{8,9},{9,10},{10,1... | collective-permute-start | bytes 3840008 | tf_op jit(solution)/shard_map/ppermute | solution.py:267
  449.3 27.6 %copy-start.3 = (f32[8,40000]{1,0:T(8,128)}, f32[8,40000]{1,0:T(8,128)S(1)}, u32[]{:S(2)}) copy-start(f32[8,40000]{1,0:T(8,128)S(1)} %collective-permute-done.10.refs_2_) | copy-start | bytes 3840004
  476.8 1.0 copy-start.4
Sparse Core Ops, SparseCore 0:
  17.9 63.1 all-gather.3
  83.1 86.9 all-gather.5

commit v9 on v8

--- a/solution.py
+++ b/solution.py
@@ -352,21 +352,19 @@
         )
         first.append(result)
         parts.append(leaving)
-    double = operator(
-        lambda n, *refs: left_again_body(n, spans, *refs),
-        first, row_consts, row_wire(row_block[1]), row_block,
-    )
     base = operator(
         lambda n, *refs: right_body(n, cols, *refs),
-        [me, *after(theirs, double)], col_consts, jax.ShapeDtypeStruct(col_block, f32), col_block,
+        [me, *after(theirs, parts)], col_consts, jax.ShapeDtypeStruct(col_block, f32), col_block,
     )
-    arriving, part = [], double
+    arriving = []
     for h, (start, stop) in enumerate(spans):
         part = exchange(after(parts[h], (part, base)) if h else parts[h], "row")
         if h + 1 == len(spans):
-            double = after(double, (part, arriving))
-        if h:
-            part = after(part, arriving)
+            double = operator(
+                lambda n, *refs: left_again_body(n, spans, *refs),
+                after(first, turned) if h else first, row_consts, row_wire(row_block[1]), row_block,
+            )
+            part, double = after(part, (arriving, double)), after(double, (part, arriving))
         turned = call(
             turn_arriving_body, col_wires(rows * (stop - start)), [me, part],
             [

time: 508 us -> 493 us (0.970)
  waiting for transfers between devices: 169 us -> 157 us
    ppermute x12, waiting for transfers between devices: 167 us -> 135 us  [shift(): lax.ppermute(parts[s], axis, [(d, (d + s) % n) for d in range(n)])]
    all_to_all x4, waiting for transfers between devices: 0.01 us -> 18.9 us  [exchange(): return lax.all_to_all(x, axis, split_axis=0, concat_axis=0, tiled=True)]
  transfers between devices with their start and end apart: 18 -> 18, of which waited for: 12 -> 12; matrix products, arithmetic and copies ran while one was open for 0% -> 0% of each run, Pallas kernels for 35% -> 36%
where the time goes in v9:
time: 493 us; the launch traced here: 484 us
  Pallas kernels  198 us (40%)
  waiting for transfers between devices  157 us (32%)
  blocking collectives  79.5 us (16%)
  starting transfers between devices  29.9 us (6%)
  between operations  14 us (3%)
    pallas_call x10, Pallas kernels, call(): pl.pallas_call(body, in_specs=[smem if x.dtype == jnp.int32 else vmem for...  185 us
    ppermute x12, waiting for transfers between devices, shift(): lax.ppermute(parts[s], axis, [(d, (d + s) % n) for d in range(n)])  135 us
    all_to_all x1, blocking collectives, exchange(): return lax.all_to_all(x, axis, split_axis=0, concat_axis=0, tiled=True)  79.5 us
    all_to_all x4, starting transfers between devices, exchange(): return lax.all_to_all(x, axis, split_axis=0, concat_axis=0, tiled=True)  19.6 us
    all_to_all x4, waiting for transfers between devices, exchange(): return lax.all_to_all(x, axis, split_axis=0, concat_axis=0, tiled=True)  18.9 us
    pallas_call x1, Pallas kernels, shards(): pl.pallas_call(functools.partial(split_body, n), grid=(n // group,), in_s...  13.1 us
    ppermute x12, starting transfers between devices, shift(): lax.ppermute(parts[s], axis, [(d, (d + s) % n) for d in range(n)])  10.2 us
  transfers between devices with their start and end apart: 18, of which 12 were waited for; matrix products, arithmetic and copies ran while one was open for 0% of the time, Pallas kernels for 36%

profile of v9, /device:TPU:1, one launch (start us, length us, event | category | flops | bytes accessed | tf_op | source)
XLA Modules:
  0.0 484.3 jit_solution(14565155113297360920)
XLA Ops:
  6.5 10.3 %shard_map.46 = (f32[1600,800]{1,0:T(8,128)}, f32[8,32,3200]{2,1,0:T(8,128)}, f32[8,24,2400]{2,1,0:T(8,128)}) custom-call(f32[800,1600]{1,0:T(8,128)} %x_ref.3), custom_call_target="tpu_custom_call" | custom-call | bytes 15360000 | tf_op jit(solution)/shard_map/pallas_call | solution.py:35
  16.9 0.8 reshape.11
  17.7 0.0 all-gather.6.cloned.1.call-start
  17.8 6.9 %shard_map.47 = (f32[8,40000]{1,0:T(8,128)}, f32[8,40000]{1,0:T(8,128)}, f32[8,40000]{1,0:T(8,128)}, f32[8,40000]{1,0:T(8,128)}) custom-call(s32[1]{0:T(128)} %bitcast.me_ref.refs_0_, f32[1600,800]{1,0:T(8,128)} %get-tuple-element.46.x_ref), custom_call_target="tpu_custom_call" | custom-call | bytes 10240000 | tf_op jit(solution)/shard_map/pallas_call | solution.py:35
  24.7 2.6 collective-permute-start
  27.3 0.4 collective-permute-start.2
  27.7 27.3 %collective-permute-done.refs_2_ = f32[8,40000]{1,0:T(8,128)} collective-permute-done((f32[8,40000]{1,0:T(8,128)}, f32[8,40000]{1,0:T(8,128)}, u32[]{:S(2)}, u32[]{:S(2)}) %collective-permute-start) | collective-permute-done | bytes 1280032 | tf_op jit(solution)/shard_map/ppermute | solution.py:267
  55.0 27.5 %collective-permute-done.1.refs_3_ = f32[8,40000]{1,0:T(8,128)} collective-permute-done((f32[8,40000]{1,0:T(8,128)}, f32[8,40000]{1,0:T(8,128)}, u32[]{:S(2)}, u32[]{:S(2)}) %collective-permute-start.1) | collective-permute-done | bytes 1280032 | tf_op jit(solution)/shard_map/ppermute | solution.py:267
  82.5 0.5 collective-permute-done.2.refs_4_
  83.0 79.5 %all_to_all.25.x_ref = f32[8,32,3200]{2,1,0:T(8,128)} all-to-all(f32[8,32,3200]{2,1,0:T(8,128)S(1)} %copy-done.2), channel_id=1, replica_groups=mesh['row'=8,'col'=4] {'row'}, dimensions={0} | all-to-all | bytes 6553600 | tf_op jit(solution)/shard_map/all_to_all | solution.py:276
  162.6 4.3 all-to-all-start.1
  166.8 0.1 copy.5
  167.0 0.8 pad_maximum_fusion
  167.7 2.5 all-gather.6.cloned.1.call-done
  170.2 13.1 %shard_map.48 = (bf16[6400,512]{1,0:T(8,128)(2,1)}, bf16[6400,512]{1,0:T(8,128)(2,1)}) custom-call(f32[4,1600,512]{2,1,0:T(8,128)} %bitcast.7), custom_call_target="tpu_custom_call" | custom-call | flops 6553600 | bytes 26214400 | tf_op jit(solution)/shard_map/pallas_call | solution.py:315
  183.3 26.9 %shard_map.49 = (f32[8,128,800]{2,1,0:T(8,128)}, f32[8,32,3200]{2,1,0:T(8,128)}) custom-call(f32[8,32,3200]{2,1,0:T(8,128)} %all_to_all.25.x_ref, bf16[6400,512]{1,0:T(8,128)(2,1)} %get-tuple-element.52.refs_0_.refs_2_.refs_5_.refs_10_, bf16[6400,512]{1,0:T(8,128)(2,1)} %get-tuple-element.53.refs_1_.refs_3_.refs_6_.refs_11_, f32[1,512]{1,0:T(1,128)} %bitcast.8, ...), custom_call_target="tpu_custom_call" | custom-call | flops 5819596800 | bytes 28467200 | tf_op jit(solution)/shard_map/pallas_call | solution.py:35
  210.1 1.2 copy-done.1
  211.4 5.4 %all-to-all-start.2 = ((f32[8,32,3200]{2,1,0:T(8,128)}), f32[8,32,3200]{2,1,0:T(8,128)S(1)}, u32[]{:S(2)}, u32[]{:S(2)}) async-start(f32[8,32,3200]{2,1,0:T(8,128)} %get-tuple-element.56), calls=%async_computation.2 | async-start | bytes 6553600 | tf_op jit(solution)/shard_map/all_to_all | solution.py:276
  216.8 0.6 neg.13
  217.4 25.1 %shard_map.50 = (f32[8,72,800]{2,1,0:T(8,128)}, f32[8,24,2400]{2,1,0:T(8,128)}) custom-call(f32[8,24,2400]{2,1,0:T(8,128)} %copy-done.1, bf16[6400,512]{1,0:T(8,128)(2,1)} %get-tuple-element.52.refs_0_.refs_2_.refs_5_.refs_10_, bf16[6400,512]{1,0:T(8,128)(2,1)} %get-tuple-element.53.refs_1_.refs_3_.refs_6_.refs_11_, f32[1,512]{1,0:T(1,128)} %bitcast.9, ...), custom_call_target="tpu_custom_call" | custom-call | flops 3273523200 | bytes 28467200 | tf_op jit(solution)/shard_map/pallas_call | solution.py:35
  242.5 28.5 %shard_map.53.refs_1_ = f32[4,200,1600]{2,1,0:T(8,128)} custom-call(s32[1]{0:T(128)} %bitcast.me_ref.refs_0_, f32[8,40000]{1,0:T(8,128)} %get-tuple-element.66.refs_1_, f32[8,40000]{1,0:T(8,128)} %collective-permute-done.refs_2_, f32[8,40000]{1,0:T(8,128)} %collective-permute-done.1.refs_3_, f32[8,40000]{1,0:T(8,128)} %collective-permute-done.2.refs_4_, ...), custom_call_target="tpu_custom_call" | custom-call | flops 9093120000 | bytes 28467200 | tf_op jit(solution)/shard_map/pallas_call | solution.py:35
  271.0 18.9 %all-to-all-done.2.x_ref = f32[8,32,3200]{2,1,0:T(8,128)S(1)} async-done(((f32[8,32,3200]{2,1,0:T(8,128)}), f32[8,32,3200]{2,1,0:T(8,128)S(1)}, u32[]{:S(2)}, u32[]{:S(2)}) %all-to-all-start.2) | async-done | bytes 3276832 | tf_op jit(solution)/shard_map/all_to_all | solution.py:276
  289.9 4.3 all-to-all-start.3
  294.2 6.0 %shard_map.51 = (f32[200,1024]{1,0:T(8,128)}, f32[200,1024]{1,0:T(8,128)}, f32[200,1024]{1,0:T(8,128)}, f32[200,1024]{1,0:T(8,128)}) custom-call(s32[1]{0:T(128)} %bitcast.me_ref.refs_0_, f32[8,32,3200]{2,1,0:T(8,128)} %copy-done), custom_call_target="tpu_custom_call" | custom-call | bytes 5120000 | tf_op jit(solution)/shard_map/pallas_call | solution.py:35
  300.2 1.5 collective-permute-start.3
  301.7 1.2 collective-permute-start.4
  302.9 0.2 collective-permute-start.5
  303.1 31.3 %shard_map.52 = f32[8,8,20000]{2,1,0:T(8,128)} custom-call(f32[8,128,800]{2,1,0:T(8,128)} %get-tuple-element.63.refs_0_, f32[8,72,800]{2,1,0:T(8,128)} %get-tuple-element.64.refs_1_, bf16[6400,512]{1,0:T(8,128)(2,1)} %get-tuple-element.52.refs_0_.refs_2_.refs_5_.refs_10_, bf16[6400,512]{1,0:T(8,128)(2,1)} %get-tuple-element.53.refs_1_.refs_3_.refs_6_.refs_11_, ...), custom_call_target="tpu_custom_call" | custom-call | flops 9093120000 | bytes 28467200 | tf_op jit(solution)/shard_map/pallas_call | solution.py:35
  334.4 4.2 collective-permute-done.4.refs_4_
  338.6 0.6 collective-permute-done.5.refs_5_
  339.2 0.4 copy-done.9
  339.5 0.5 copy-done.10
  340.1 5.6 %all-to-all-start.4 = ((f32[8,8,20000]{2,1,0:T(8,128)}), f32[8,8,20000]{2,1,0:T(8,128)}, u32[]{:S(2)}, u32[]{:S(2)}) async-start(f32[8,8,20000]{2,1,0:T(8,128)} %shard_map.52), calls=%async_computation.4 | async-start | bytes 10289152 | tf_op jit(solution)/shard_map/all_to_all | solution.py:276
  345.7 4.1 shard_map.54
  349.8 0.2 collective-permute-start.6
  350.0 0.3 collective-permute-start.7
  350.2 0.6 collective-permute-start.8
  350.8 8.9 %collective-permute-done.6.refs_7_ = f32[8,14400]{1,0:T(8,128)S(1)} collective-permute-done((f32[8,14400]{1,0:T(8,128)}, f32[8,14400]{1,0:T(8,128)S(1)}, u32[]{:S(2)}, u32[]{:S(2)}) %collective-permute-start.6) | collective-permute-done | bytes 460832 | tf_op jit(solution)/shard_map/ppermute | solution.py:267
  359.7 9.9 %collective-permute-done.7.refs_8_ = f32[8,14400]{1,0:T(8,128)S(1)} collective-permute-done((f32[8,14400]{1,0:T(8,128)}, f32[8,14400]{1,0:T(8,128)S(1)}, u32[]{:S(2)}, u32[]{:S(2)}) %collective-permute-start.7) | collective-permute-done | bytes 460832 | tf_op jit(solution)/shard_map/ppermute | solution.py:267
  369.6 2.0 collective-permute-done.8.refs_9_
  371.7 0.8 copy-done.13
  372.4 31.3 %shard_map.55 = (f32[8,40000]{1,0:T(8,128)}, f32[8,40000]{1,0:T(8,128)}, f32[8,40000]{1,0:T(8,128)}, f32[8,40000]{1,0:T(8,128)}) custom-call(s32[1]{0:T(128)} %bitcast.me_ref.refs_0_, f32[4,200,1600]{2,1,0:T(8,128)} %shard_map.53.refs_1_, f32[200,1024]{1,0:T(8,128)} %get-tuple-element.59.refs_2_, f32[200,1024]{1,0:T(8,128)} %copy-done.8, ...), custom_call_target="tpu_custom_call" | custom-call | flops 9093120000 | bytes 28467200 | tf_op jit(solution)/shard_map/pallas_call | solution.py:35
  403.7 1.2 collective-permute-start.10
  404.9 2.0 collective-permute-start.9
  406.9 26.9 %collective-permute-done.10.refs_2_ = f32[8,40000]{1,0:T(8,128)S(1)} collective-permute-done((f32[8,40000]{1,0:T(8,128)}, f32[8,40000]{1,0:T(8,128)S(1)}, u32[]{:S(2)}, u32[]{:S(2)}) %collective-permute-start.10) | collective-permute-done | bytes 1280032 | tf_op jit(solution)/shard_map/ppermute | solution.py:267
  433.8 27.6 %collective-permute-done.11.refs_3_ = f32[8,40000]{1,0:T(8,128)S(1)} collective-permute-done((f32[8,40000]{1,0:T(8,128)}, f32[8,40000]{1,0:T(8,128)S(1)}, u32[]{:S(2)}, u32[]{:S(2)}) %collective-permute-start.11) | collective-permute-done | bytes 1280032 | tf_op jit(solution)/shard_map/ppermute | solution.py:267
  461.4 1.0 copy-done.4
  462.5 14.6 %shard_map.56 = f32[800,1600]{1,0:T(8,128)} custom-call(s32[1]{0:T(128)} %bitcast.me_ref.refs_0_, f32[800,1600]{1,0:T(8,128)} %x_ref.3, f32[8,8,20000]{2,1,0:T(8,128)} %all-to-all-done.4.crossed_ref, f32[8,40000]{1,0:T(8,128)} %get-tuple-element.77.refs_0_, f32[8,40000]{1,0:T(8,128)} %collective-permute-done.9.refs_1_, f32[8,40000]{1,0:T(8,128)} %copy-done.3, ...), custom_call_target="tpu_custom_call" | custom-call | bytes 20480000 | tf_op jit(solution)/shard_map/pallas_call | solution.py:35
  (36 shorter events, 0.1 us)
Async XLA Ops:
  6.5 10.3 %copy-start.5 = (f32[10,20,512]{2,1,0:T(8,128)S(1)}, f32[10,20,512]{2,1,0:T(8,128)}, u32[]{:S(2)}) copy-start(f32[10,20,512]{2,1,0:T(8,128)} %param.6) | copy-start | bytes 1228804
  6.5 76.5 %all-gather.4.cloned.1.call-start = ((), (), s32[]{:S(2)}) async-start(), calls=%async_computation.5 | async-start | bytes 3686400 | tf_op jit(solution)/shard_map/all_gather | solution.py:306
  17.7 152.4 %all-gather.6.cloned.1.call-start = ((), (), s32[]{:S(2)}) async-start(), calls=%async_computation.6 | async-start | bytes 16384000 | tf_op jit(solution)/shard_map/all_gather | solution.py:312
  24.7 58.4 %copy-start.2 = (f32[8,32,3200]{2,1,0:T(8,128)S(1)}, f32[8,32,3200]{2,1,0:T(8,128)}, u32[]{:S(2)}) copy-start(f32[8,32,3200]{2,1,0:T(8,128)} %get-tuple-element.43) | copy-start | bytes 9830404
  24.7 30.4 %collective-permute-start = (f32[8,40000]{1,0:T(8,128)}, f32[8,40000]{1,0:T(8,128)}, u32[]{:S(2)}, u32[]{:S(2)}) collective-permute-start(f32[8,40000]{1,0:T(8,128)} %get-tuple-element.48), channel_id=1, source_target_pairs={{0,1},{1,2},{2,3},{3,0},{4,5},{5,6},{6,7},{7,4},{8,9},{9,10},{10,1... | collective-permute-start | bytes 3840008 | tf_op jit(solution)/shard_map/ppermute | solution.py:267
  27.3 55.2 %collective-permute-start.1 = (f32[8,40000]{1,0:T(8,128)}, f32[8,40000]{1,0:T(8,128)}, u32[]{:S(2)}, u32[]{:S(2)}) collective-permute-start(f32[8,40000]{1,0:T(8,128)} %get-tuple-element.49), channel_id=1, source_target_pairs={{0,2},{1,3},{2,0},{3,1},{4,6},{5,7},{6,4},{7,5},{8,10},{9,11},{10,... | collective-permute-start | bytes 3840008 | tf_op jit(solution)/shard_map/ppermute | solution.py:267
  27.3 55.7 %collective-permute-start.2 = (f32[8,40000]{1,0:T(8,128)}, f32[8,40000]{1,0:T(8,128)}, u32[]{:S(2)}, u32[]{:S(2)}) collective-permute-start(f32[8,40000]{1,0:T(8,128)} %get-tuple-element.50), channel_id=1, source_target_pairs={{0,3},{1,0},{2,1},{3,2},{4,7},{5,4},{6,5},{7,6},{8,11},{9,8},{10,9... | collective-permute-start | bytes 3840008 | tf_op jit(solution)/shard_map/ppermute | solution.py:267
  162.6 4.3 copy-start.6
  162.6 47.6 %all-to-all-start.1 = ((f32[8,24,2400]{2,1,0:T(8,128)}), f32[8,24,2400]{2,1,0:T(8,128)S(1)}, u32[]{:S(2)}, u32[]{:S(2)}) async-start(f32[8,24,2400]{2,1,0:T(8,128)} %get-tuple-element.55), calls=%async_computation.1 | async-start | bytes 3735552 | tf_op jit(solution)/shard_map/all_to_all | solution.py:276
  210.1 1.2 copy-start.1
  210.1 6.7 %copy-start.7 = (f32[512]{0:T(512)S(1)}, f32[512]{0:T(512)}, u32[]{:S(2)}) copy-start(f32[512]{0:T(512)} %param.7) | copy-start | bytes 6148
  211.4 78.5 %all-to-all-start.2 = ((f32[8,32,3200]{2,1,0:T(8,128)}), f32[8,32,3200]{2,1,0:T(8,128)S(1)}, u32[]{:S(2)}, u32[]{:S(2)}) async-start(f32[8,32,3200]{2,1,0:T(8,128)} %get-tuple-element.56), calls=%async_computation.2 | async-start | bytes 6553600 | tf_op jit(solution)/shard_map/all_to_all | solution.py:276
  289.9 4.3 copy-start
  289.9 49.3 %all-to-all-start.3 = ((f32[8,24,2400]{2,1,0:T(8,128)}), f32[8,24,2400]{2,1,0:T(8,128)}, u32[]{:S(2)}, u32[]{:S(2)}) async-start(f32[8,24,2400]{2,1,0:T(8,128)} %get-tuple-element.70), calls=%async_computation.3 | async-start | bytes 3735552 | tf_op jit(solution)/shard_map/all_to_all | solution.py:276
  300.2 34.2 %collective-permute-start.3 = (f32[200,1024]{1,0:T(8,128)}, f32[200,1024]{1,0:T(8,128)S(1)}, u32[]{:S(2)}, u32[]{:S(2)}) collective-permute-start(f32[200,1024]{1,0:T(8,128)} %get-tuple-element.60), channel_id=1, source_target_pairs={{0,1},{1,2},{2,3},{3,0},{4,5},{5,6},{6,7},{7,4},{8,9},{9,10},{10,1... | collective-permute-start | bytes 2457608 | tf_op jit(solution)/shard_map/ppermute | solution.py:267
  301.7 36.9 %collective-permute-start.4 = (f32[200,1024]{1,0:T(8,128)}, f32[200,1024]{1,0:T(8,128)S(1)}, u32[]{:S(2)}, u32[]{:S(2)}) collective-permute-start(f32[200,1024]{1,0:T(8,128)} %get-tuple-element.61), channel_id=1, source_target_pairs={{0,2},{1,3},{2,0},{3,1},{4,6},{5,7},{6,4},{7,5},{8,10},{9,11},{10,... | collective-permute-start | bytes 2457608 | tf_op jit(solution)/shard_map/ppermute | solution.py:267
  302.9 36.3 %collective-permute-start.5 = (f32[200,1024]{1,0:T(8,128)}, f32[200,1024]{1,0:T(8,128)S(1)}, u32[]{:S(2)}, u32[]{:S(2)}) collective-permute-start(f32[200,1024]{1,0:T(8,128)} %get-tuple-element.62), channel_id=1, source_target_pairs={{0,3},{1,0},{2,1},{3,2},{4,7},{5,4},{6,5},{7,6},{8,11},{9,8},{10,9... | collective-permute-start | bytes 2457608 | tf_op jit(solution)/shard_map/ppermute | solution.py:267
  334.4 4.7 copy-start.8
  338.6 0.9 copy-start.9
  339.2 0.9 copy-start.10
  340.1 121.3 %all-to-all-start.4 = ((f32[8,8,20000]{2,1,0:T(8,128)}), f32[8,8,20000]{2,1,0:T(8,128)}, u32[]{:S(2)}, u32[]{:S(2)}) async-start(f32[8,8,20000]{2,1,0:T(8,128)} %shard_map.52), calls=%async_computation.4 | async-start | bytes 10289152 | tf_op jit(solution)/shard_map/all_to_all | solution.py:276
  349.8 9.9 %collective-permute-start.6 = (f32[8,14400]{1,0:T(8,128)}, f32[8,14400]{1,0:T(8,128)S(1)}, u32[]{:S(2)}, u32[]{:S(2)}) collective-permute-start(f32[8,14400]{1,0:T(8,128)} %get-tuple-element.74), channel_id=1, source_target_pairs={{0,1},{1,2},{2,3},{3,0},{4,5},{5,6},{6,7},{7,4},{8,9},{9,10},{10,1... | collective-permute-start | bytes 1382408 | tf_op jit(solution)/shard_map/ppermute | solution.py:267
  350.0 19.7 %collective-permute-start.7 = (f32[8,14400]{1,0:T(8,128)}, f32[8,14400]{1,0:T(8,128)S(1)}, u32[]{:S(2)}, u32[]{:S(2)}) collective-permute-start(f32[8,14400]{1,0:T(8,128)} %get-tuple-element.75), channel_id=1, source_target_pairs={{0,2},{1,3},{2,0},{3,1},{4,6},{5,7},{6,4},{7,5},{8,10},{9,11},{10,... | collective-permute-start | bytes 1382408 | tf_op jit(solution)/shard_map/ppermute | solution.py:267
  350.2 21.4 %collective-permute-start.8 = (f32[8,14400]{1,0:T(8,128)}, f32[8,14400]{1,0:T(8,128)S(1)}, u32[]{:S(2)}, u32[]{:S(2)}) collective-permute-start(f32[8,14400]{1,0:T(8,128)} %get-tuple-element.76), channel_id=1, source_target_pairs={{0,3},{1,0},{2,1},{3,2},{4,7},{5,4},{6,5},{7,6},{8,11},{9,8},{10,9... | collective-permute-start | bytes 1382408 | tf_op jit(solution)/shard_map/ppermute | solution.py:267
  359.7 12.0 %copy-start.11 = (f32[8,14400]{1,0:T(8,128)}, f32[8,14400]{1,0:T(8,128)S(1)}, u32[]{:S(2)}) copy-start(f32[8,14400]{1,0:T(8,128)S(1)} %collective-permute-done.6.refs_7_) | copy-start | bytes 1382404
  369.6 2.0 copy-start.12
  371.6 0.8 copy-start.13
  403.7 30.1 %collective-permute-start.10 = (f32[8,40000]{1,0:T(8,128)}, f32[8,40000]{1,0:T(8,128)S(1)}, u32[]{:S(2)}, u32[]{:S(2)}) collective-permute-start(f32[8,40000]{1,0:T(8,128)} %get-tuple-element.79), channel_id=1, source_target_pairs={{0,2},{1,3},{2,0},{3,1},{4,6},{5,7},{6,4},{7,5},{8,10},{9,11},{10,... | collective-permute-start | bytes 3840008 | tf_op jit(solution)/shard_map/ppermute | solution.py:267
  404.9 56.5 %collective-permute-start.11 = (f32[8,40000]{1,0:T(8,128)}, f32[8,40000]{1,0:T(8,128)S(1)}, u32[]{:S(2)}, u32[]{:S(2)}) collective-permute-start(f32[8,40000]{1,0:T(8,128)} %get-tuple-element.80), channel_id=1, source_target_pairs={{0,3},{1,0},{2,1},{3,2},{4,7},{5,4},{6,5},{7,6},{8,11},{9,8},{10,9... | collective-permute-start | bytes 3840008 | tf_op jit(solution)/shard_map/ppermute | solution.py:267
  404.9 56.5 %collective-permute-start.9 = (f32[8,40000]{1,0:T(8,128)}, f32[8,40000]{1,0:T(8,128)}, u32[]{:S(2)}, u32[]{:S(2)}) collective-permute-start(f32[8,40000]{1,0:T(8,128)} %get-tuple-element.78), channel_id=1, source_target_pairs={{0,1},{1,2},{2,3},{3,0},{4,5},{5,6},{6,7},{7,4},{8,9},{9,10},{10,1... | collective-permute-start | bytes 3840008 | tf_op jit(solution)/shard_map/ppermute | solution.py:267
  433.8 27.6 %copy-start.3 = (f32[8,40000]{1,0:T(8,128)}, f32[8,40000]{1,0:T(8,128)S(1)}, u32[]{:S(2)}) copy-start(f32[8,40000]{1,0:T(8,128)S(1)} %collective-permute-done.10.refs_2_) | copy-start | bytes 3840004
  461.4 1.0 copy-start.4
Sparse Core Ops, SparseCore 0:
  17.9 63.1 all-gather.3
  83.1 86.9 all-gather.5

commit v10 on v9

--- a/solution.py
+++ b/solution.py
@@ -302,14 +302,13 @@
         [pairs], moved=12 * size,
     )
 
-    aux = after(aux, sent)
     whole = lax.all_gather(aux.reshape(-1, naux), "row", axis=0, tiled=True)
     mine = []
     for part in sent:
         mine.append(exchange(after(part, mine) if mine else part, "row"))
     turned = call(turn_body, col_wires(local_cols), [me, crossed], [col_stage], moved=8 * size)
     theirs = shift(turned, "col")
-    whole = lax.all_gather(after(whole, theirs), "col", axis=0, tiled=False)
+    whole = lax.all_gather(after(whole, theirs[:-1]), "col", axis=0, tiled=False)
     group = 8 if n % 8 == 0 else n
     shape = jax.ShapeDtypeStruct((n * n, naux), bf16)
     high, low = pl.pallas_call(

time: 493 us -> 481 us (0.976)
  waiting for transfers between devices: 157 us -> 148 us
    ppermute x12, waiting for transfers between devices: 135 us -> 122 us  [shift(): lax.ppermute(parts[s], axis, [(d, (d + s) % n) for d in range(n)])]
  transfers between devices with their start and end apart: 18 -> 18, of which waited for: 12 -> 12; matrix products, arithmetic and copies ran while one was open for 0% -> 0% of each run, Pallas kernels for 36% -> 39%
where the time goes in v10:
time: 481 us; the launch traced here: 473 us
  Pallas kernels  198 us (41%)
  waiting for transfers between devices  148 us (31%)
  blocking collectives  76.4 us (16%)
  starting transfers between devices  29.9 us (6%)
  between operations  14 us (3%)
  local copies, waits for them, and re-layouts  5.88 us (1%)
    pallas_call x10, Pallas kernels, call(): pl.pallas_call(body, in_specs=[smem if x.dtype == jnp.int32 else vmem for...  185 us
    ppermute x12, waiting for transfers between devices, shift(): lax.ppermute(parts[s], axis, [(d, (d + s) % n) for d in range(n)])  122 us
    all_to_all x1, blocking collectives, exchange(): return lax.all_to_all(x, axis, split_axis=0, concat_axis=0, tiled=True)  76.4 us
    all_to_all x4, starting transfers between devices, exchange(): return lax.all_to_all(x, axis, split_axis=0, concat_axis=0, tiled=True)  19.6 us
    all_to_all x4, waiting for transfers between devices, exchange(): return lax.all_to_all(x, axis, split_axis=0, concat_axis=0, tiled=True)  18.3 us
    pallas_call x1, Pallas kernels, shards(): pl.pallas_call(functools.partial(split_body, n), grid=(n // group,), in_s...  13.1 us
    ppermute x12, starting transfers between devices, shift(): lax.ppermute(parts[s], axis, [(d, (d + s) % n) for d in range(n)])  10.3 us
  transfers between devices with their start and end apart: 18, of which 12 were waited for; matrix products, arithmetic and copies ran while one was open for 0% of the time, Pallas kernels for 39%

profile of v10, /device:TPU:1, one launch (start us, length us, event | category | flops | bytes accessed | tf_op | source)
XLA Modules:
  0.0 473.3 jit_solution(18186510546944294138)
XLA Ops:
  6.5 1.9 reshape.11
  8.4 0.0 all-gather.6.cloned.1.call-start
  8.5 10.3 %shard_map.46 = (f32[1600,800]{1,0:T(8,128)}, f32[8,32,3200]{2,1,0:T(8,128)}, f32[8,24,2400]{2,1,0:T(8,128)}) custom-call(f32[800,1600]{1,0:T(8,128)} %x_ref.3), custom_call_target="tpu_custom_call" | custom-call | bytes 15360000 | tf_op jit(solution)/shard_map/pallas_call | solution.py:35
  18.8 7.1 %shard_map.47 = (f32[8,40000]{1,0:T(8,128)}, f32[8,40000]{1,0:T(8,128)}, f32[8,40000]{1,0:T(8,128)}, f32[8,40000]{1,0:T(8,128)}) custom-call(s32[1]{0:T(128)} %bitcast.me_ref.refs_0_, f32[1600,800]{1,0:T(8,128)} %get-tuple-element.43.x_ref), custom_call_target="tpu_custom_call" | custom-call | bytes 10240000 | tf_op jit(solution)/shard_map/pallas_call | solution.py:35
  25.9 2.5 collective-permute-start
  28.4 27.7 %collective-permute-done.refs_2_ = f32[8,40000]{1,0:T(8,128)} collective-permute-done((f32[8,40000]{1,0:T(8,128)}, f32[8,40000]{1,0:T(8,128)}, u32[]{:S(2)}, u32[]{:S(2)}) %collective-permute-start) | collective-permute-done | bytes 1280032 | tf_op jit(solution)/shard_map/ppermute | solution.py:267
  56.1 14.6 %collective-permute-done.1.refs_3_ = f32[8,40000]{1,0:T(8,128)} collective-permute-done((f32[8,40000]{1,0:T(8,128)}, f32[8,40000]{1,0:T(8,128)}, u32[]{:S(2)}, u32[]{:S(2)}) %collective-permute-start.1) | collective-permute-done | bytes 1280032 | tf_op jit(solution)/shard_map/ppermute | solution.py:267
  70.7 2.0 all-gather.4.cloned.1.call-done
  72.8 76.4 %all_to_all.25.x_ref = f32[8,32,3200]{2,1,0:T(8,128)} all-to-all(f32[8,32,3200]{2,1,0:T(8,128)S(1)} %copy-done.2), channel_id=1, replica_groups=mesh['row'=8,'col'=4] {'row'}, dimensions={0} | all-to-all | bytes 6553600 | tf_op jit(solution)/shard_map/all_to_all | solution.py:276
  149.2 4.4 all-to-all-start.1
  153.6 0.1 copy.5
  153.7 0.8 pad_maximum_fusion
  154.5 4.8 %all-gather.6.cloned.1.call-done = f32[6400,512]{1,0:T(8,128)} async-done(((f32[1600,512]{1,0:T(8,128)}), f32[6400,512]{1,0:T(8,128)}) %all-gather.6.cloned.1.call-update) | async-done | bytes 13107216 | tf_op jit(solution)/shard_map/all_gather | solution.py:311
  159.3 13.1 %shard_map.48 = (bf16[6400,512]{1,0:T(8,128)(2,1)}, bf16[6400,512]{1,0:T(8,128)(2,1)}) custom-call(f32[4,1600,512]{2,1,0:T(8,128)} %bitcast.7), custom_call_target="tpu_custom_call" | custom-call | flops 6553600 | bytes 26214400 | tf_op jit(solution)/shard_map/pallas_call | solution.py:314
  172.4 26.9 %shard_map.49 = (f32[8,128,800]{2,1,0:T(8,128)}, f32[8,32,3200]{2,1,0:T(8,128)}) custom-call(f32[8,32,3200]{2,1,0:T(8,128)} %all_to_all.25.x_ref, bf16[6400,512]{1,0:T(8,128)(2,1)} %get-tuple-element.48.refs_0_.refs_2_.refs_5_.refs_10_, bf16[6400,512]{1,0:T(8,128)(2,1)} %get-tuple-element.49.refs_1_.refs_3_.refs_6_.refs_11_, f32[1,512]{1,0:T(1,128)} %bitcast.8, ...), custom_call_target="tpu_custom_call" | custom-call | flops 5819596800 | bytes 28467200 | tf_op jit(solution)/shard_map/pallas_call | solution.py:35
  199.3 1.2 copy-done.1
  200.5 5.2 %all-to-all-start.2 = ((f32[8,32,3200]{2,1,0:T(8,128)}), f32[8,32,3200]{2,1,0:T(8,128)S(1)}, u32[]{:S(2)}, u32[]{:S(2)}) async-start(f32[8,32,3200]{2,1,0:T(8,128)} %get-tuple-element.53), calls=%async_computation.2 | async-start | bytes 6553600 | tf_op jit(solution)/shard_map/all_to_all | solution.py:276
  205.8 0.7 collective-permute-start.2
  206.4 0.6 neg.13
  207.0 25.1 %shard_map.50 = (f32[8,72,800]{2,1,0:T(8,128)}, f32[8,24,2400]{2,1,0:T(8,128)}) custom-call(f32[8,24,2400]{2,1,0:T(8,128)} %copy-done.1, bf16[6400,512]{1,0:T(8,128)(2,1)} %get-tuple-element.48.refs_0_.refs_2_.refs_5_.refs_10_, bf16[6400,512]{1,0:T(8,128)(2,1)} %get-tuple-element.49.refs_1_.refs_3_.refs_6_.refs_11_, f32[1,512]{1,0:T(1,128)} %bitcast.9, ...), custom_call_target="tpu_custom_call" | custom-call | flops 3273523200 | bytes 28467200 | tf_op jit(solution)/shard_map/pallas_call | solution.py:35
  232.1 28.4 %shard_map.53.refs_1_ = f32[4,200,1600]{2,1,0:T(8,128)} custom-call(s32[1]{0:T(128)} %bitcast.me_ref.refs_0_, f32[8,40000]{1,0:T(8,128)} %get-tuple-element.64.refs_1_, f32[8,40000]{1,0:T(8,128)} %collective-permute-done.refs_2_, f32[8,40000]{1,0:T(8,128)} %collective-permute-done.1.refs_3_, f32[8,40000]{1,0:T(8,128)} %collective-permute-done.2.refs_4_, ...), custom_call_target="tpu_custom_call" | custom-call | flops 9093120000 | bytes 28467200 | tf_op jit(solution)/shard_map/pallas_call | solution.py:35
  260.6 18.3 %all-to-all-done.2.x_ref = f32[8,32,3200]{2,1,0:T(8,128)S(1)} async-done(((f32[8,32,3200]{2,1,0:T(8,128)}), f32[8,32,3200]{2,1,0:T(8,128)S(1)}, u32[]{:S(2)}, u32[]{:S(2)}) %all-to-all-start.2) | async-done | bytes 3276832 | tf_op jit(solution)/shard_map/all_to_all | solution.py:276
  278.9 4.3 all-to-all-start.3
  283.2 6.0 %shard_map.51 = (f32[200,1024]{1,0:T(8,128)}, f32[200,1024]{1,0:T(8,128)}, f32[200,1024]{1,0:T(8,128)}, f32[200,1024]{1,0:T(8,128)}) custom-call(s32[1]{0:T(128)} %bitcast.me_ref.refs_0_, f32[8,32,3200]{2,1,0:T(8,128)} %copy-done), custom_call_target="tpu_custom_call" | custom-call | bytes 5120000 | tf_op jit(solution)/shard_map/pallas_call | solution.py:35
  289.2 1.5 collective-permute-start.3
  290.7 1.2 collective-permute-start.4
  291.9 0.2 collective-permute-start.5
  292.1 31.3 %shard_map.52 = f32[8,8,20000]{2,1,0:T(8,128)} custom-call(f32[8,128,800]{2,1,0:T(8,128)} %get-tuple-element.60.refs_0_, f32[8,72,800]{2,1,0:T(8,128)} %get-tuple-element.61.refs_1_, bf16[6400,512]{1,0:T(8,128)(2,1)} %get-tuple-element.48.refs_0_.refs_2_.refs_5_.refs_10_, bf16[6400,512]{1,0:T(8,128)(2,1)} %get-tuple-element.49.refs_1_.refs_3_.refs_6_.refs_11_, ...), custom_call_target="tpu_custom_call" | custom-call | flops 9093120000 | bytes 28467200 | tf_op jit(solution)/shard_map/pallas_call | solution.py:35
  323.4 4.2 collective-permute-done.4.refs_4_
  327.6 0.6 collective-permute-done.5.refs_5_
  328.2 0.3 copy-done.8
  328.5 0.5 copy-done.9
  329.1 5.6 %all-to-all-start.4 = ((f32[8,8,20000]{2,1,0:T(8,128)}), f32[8,8,20000]{2,1,0:T(8,128)}, u32[]{:S(2)}, u32[]{:S(2)}) async-start(f32[8,8,20000]{2,1,0:T(8,128)} %shard_map.52), calls=%async_computation.4 | async-start | bytes 10289152 | tf_op jit(solution)/shard_map/all_to_all | solution.py:276
  334.7 4.0 shard_map.54
  338.7 0.2 collective-permute-start.6
  338.9 0.3 collective-permute-start.7
  339.2 0.6 collective-permute-start.8
  339.8 8.9 %collective-permute-done.6.refs_7_ = f32[8,14400]{1,0:T(8,128)S(1)} collective-permute-done((f32[8,14400]{1,0:T(8,128)}, f32[8,14400]{1,0:T(8,128)S(1)}, u32[]{:S(2)}, u32[]{:S(2)}) %collective-permute-start.6) | collective-permute-done | bytes 460832 | tf_op jit(solution)/shard_map/ppermute | solution.py:267
  348.6 9.9 %collective-permute-done.7.refs_8_ = f32[8,14400]{1,0:T(8,128)S(1)} collective-permute-done((f32[8,14400]{1,0:T(8,128)}, f32[8,14400]{1,0:T(8,128)S(1)}, u32[]{:S(2)}, u32[]{:S(2)}) %collective-permute-start.7) | collective-permute-done | bytes 460832 | tf_op jit(solution)/shard_map/ppermute | solution.py:267
  358.6 2.0 collective-permute-done.8.refs_9_
  360.6 0.8 copy-done.12
  361.4 31.3 %shard_map.55 = (f32[8,40000]{1,0:T(8,128)}, f32[8,40000]{1,0:T(8,128)}, f32[8,40000]{1,0:T(8,128)}, f32[8,40000]{1,0:T(8,128)}) custom-call(s32[1]{0:T(128)} %bitcast.me_ref.refs_0_, f32[4,200,1600]{2,1,0:T(8,128)} %shard_map.53.refs_1_, f32[200,1024]{1,0:T(8,128)} %get-tuple-element.56.refs_2_, f32[200,1024]{1,0:T(8,128)} %copy-done.7, ...), custom_call_target="tpu_custom_call" | custom-call | flops 9093120000 | bytes 28467200 | tf_op jit(solution)/shard_map/pallas_call | solution.py:35
  392.7 1.2 collective-permute-start.10
  393.9 2.0 collective-permute-start.9
  395.8 26.9 %collective-permute-done.10.refs_2_ = f32[8,40000]{1,0:T(8,128)S(1)} collective-permute-done((f32[8,40000]{1,0:T(8,128)}, f32[8,40000]{1,0:T(8,128)S(1)}, u32[]{:S(2)}, u32[]{:S(2)}) %collective-permute-start.10) | collective-permute-done | bytes 1280032 | tf_op jit(solution)/shard_map/ppermute | solution.py:267
  422.8 27.6 %collective-permute-done.11.refs_3_ = f32[8,40000]{1,0:T(8,128)S(1)} collective-permute-done((f32[8,40000]{1,0:T(8,128)}, f32[8,40000]{1,0:T(8,128)S(1)}, u32[]{:S(2)}, u32[]{:S(2)}) %collective-permute-start.11) | collective-permute-done | bytes 1280032 | tf_op jit(solution)/shard_map/ppermute | solution.py:267
  450.4 1.0 copy-done.4
  451.4 14.6 %shard_map.56 = f32[800,1600]{1,0:T(8,128)} custom-call(s32[1]{0:T(128)} %bitcast.me_ref.refs_0_, f32[800,1600]{1,0:T(8,128)} %x_ref.3, f32[8,8,20000]{2,1,0:T(8,128)} %all-to-all-done.4.crossed_ref, f32[8,40000]{1,0:T(8,128)} %get-tuple-element.75.refs_0_, f32[8,40000]{1,0:T(8,128)} %collective-permute-done.9.refs_1_, f32[8,40000]{1,0:T(8,128)} %copy-done.3, ...), custom_call_target="tpu_custom_call" | custom-call | bytes 20480000 | tf_op jit(solution)/shard_map/pallas_call | solution.py:35
  (34 shorter events, 0.1 us)
Async XLA Ops:
  6.5 66.2 %all-gather.4.cloned.1.call-start = ((), (), s32[]{:S(2)}) async-start(), calls=%async_computation.5 | async-start | bytes 3686400 | tf_op jit(solution)/shard_map/all_gather | solution.py:305
  8.4 150.9 %all-gather.6.cloned.1.call-start = ((), (), s32[]{:S(2)}) async-start(), calls=%async_computation.6 | async-start | bytes 16384000 | tf_op jit(solution)/shard_map/all_gather | solution.py:311
  25.9 46.9 %copy-start.2 = (f32[8,32,3200]{2,1,0:T(8,128)S(1)}, f32[8,32,3200]{2,1,0:T(8,128)}, u32[]{:S(2)}) copy-start(f32[8,32,3200]{2,1,0:T(8,128)} %get-tuple-element.42) | copy-start | bytes 9830404
  25.9 30.2 %collective-permute-start = (f32[8,40000]{1,0:T(8,128)}, f32[8,40000]{1,0:T(8,128)}, u32[]{:S(2)}, u32[]{:S(2)}) collective-permute-start(f32[8,40000]{1,0:T(8,128)} %get-tuple-element.45), channel_id=1, source_target_pairs={{0,1},{1,2},{2,3},{3,0},{4,5},{5,6},{6,7},{7,4},{8,9},{9,10},{10,1... | collective-permute-start | bytes 3840008 | tf_op jit(solution)/shard_map/ppermute | solution.py:267
  28.4 42.3 %collective-permute-start.1 = (f32[8,40000]{1,0:T(8,128)}, f32[8,40000]{1,0:T(8,128)}, u32[]{:S(2)}, u32[]{:S(2)}) collective-permute-start(f32[8,40000]{1,0:T(8,128)} %get-tuple-element.46), channel_id=1, source_target_pairs={{0,2},{1,3},{2,0},{3,1},{4,6},{5,7},{6,4},{7,5},{8,10},{9,11},{10,... | collective-permute-start | bytes 3840008 | tf_op jit(solution)/shard_map/ppermute | solution.py:267
  149.2 4.4 copy-start.5
  149.2 50.1 %all-to-all-start.1 = ((f32[8,24,2400]{2,1,0:T(8,128)}), f32[8,24,2400]{2,1,0:T(8,128)S(1)}, u32[]{:S(2)}, u32[]{:S(2)}) async-start(f32[8,24,2400]{2,1,0:T(8,128)} %get-tuple-element.52), calls=%async_computation.1 | async-start | bytes 3735552 | tf_op jit(solution)/shard_map/all_to_all | solution.py:276
  199.3 1.2 copy-start.1
  199.3 7.2 %copy-start.6 = (f32[512]{0:T(512)S(1)}, f32[512]{0:T(512)}, u32[]{:S(2)}) copy-start(f32[512]{0:T(512)} %param.7) | copy-start | bytes 6148
  200.5 78.4 %all-to-all-start.2 = ((f32[8,32,3200]{2,1,0:T(8,128)}), f32[8,32,3200]{2,1,0:T(8,128)S(1)}, u32[]{:S(2)}, u32[]{:S(2)}) async-start(f32[8,32,3200]{2,1,0:T(8,128)} %get-tuple-element.53), calls=%async_computation.2 | async-start | bytes 6553600 | tf_op jit(solution)/shard_map/all_to_all | solution.py:276
  205.8 26.4 %collective-permute-start.2 = (f32[8,40000]{1,0:T(8,128)}, f32[8,40000]{1,0:T(8,128)}, u32[]{:S(2)}, u32[]{:S(2)}) collective-permute-start(f32[8,40000]{1,0:T(8,128)} %get-tuple-element.63), channel_id=1, source_target_pairs={{0,3},{1,0},{2,1},{3,2},{4,7},{5,4},{6,5},{7,6},{8,11},{9,8},{10,9... | collective-permute-start | bytes 3840008 | tf_op jit(solution)/shard_map/ppermute | solution.py:267
  278.9 4.3 copy-start
  278.9 49.3 %all-to-all-start.3 = ((f32[8,24,2400]{2,1,0:T(8,128)}), f32[8,24,2400]{2,1,0:T(8,128)}, u32[]{:S(2)}, u32[]{:S(2)}) async-start(f32[8,24,2400]{2,1,0:T(8,128)} %get-tuple-element.68), calls=%async_computation.3 | async-start | bytes 3735552 | tf_op jit(solution)/shard_map/all_to_all | solution.py:276
  289.2 34.2 %collective-permute-start.3 = (f32[200,1024]{1,0:T(8,128)}, f32[200,1024]{1,0:T(8,128)S(1)}, u32[]{:S(2)}, u32[]{:S(2)}) collective-permute-start(f32[200,1024]{1,0:T(8,128)} %get-tuple-element.57), channel_id=1, source_target_pairs={{0,1},{1,2},{2,3},{3,0},{4,5},{5,6},{6,7},{7,4},{8,9},{9,10},{10,1... | collective-permute-start | bytes 2457608 | tf_op jit(solution)/shard_map/ppermute | solution.py:267
  290.7 36.9 %collective-permute-start.4 = (f32[200,1024]{1,0:T(8,128)}, f32[200,1024]{1,0:T(8,128)S(1)}, u32[]{:S(2)}, u32[]{:S(2)}) collective-permute-start(f32[200,1024]{1,0:T(8,128)} %get-tuple-element.58), channel_id=1, source_target_pairs={{0,2},{1,3},{2,0},{3,1},{4,6},{5,7},{6,4},{7,5},{8,10},{9,11},{10,... | collective-permute-start | bytes 2457608 | tf_op jit(solution)/shard_map/ppermute | solution.py:267
  291.9 36.3 %collective-permute-start.5 = (f32[200,1024]{1,0:T(8,128)}, f32[200,1024]{1,0:T(8,128)S(1)}, u32[]{:S(2)}, u32[]{:S(2)}) collective-permute-start(f32[200,1024]{1,0:T(8,128)} %get-tuple-element.59), channel_id=1, source_target_pairs={{0,3},{1,0},{2,1},{3,2},{4,7},{5,4},{6,5},{7,6},{8,11},{9,8},{10,9... | collective-permute-start | bytes 2457608 | tf_op jit(solution)/shard_map/ppermute | solution.py:267
  323.4 4.8 %copy-start.7 = (f32[200,1024]{1,0:T(8,128)}, f32[200,1024]{1,0:T(8,128)S(1)}, u32[]{:S(2)}) copy-start(f32[200,1024]{1,0:T(8,128)S(1)} %collective-permute-done.3.refs_3_) | copy-start | bytes 2457604
  327.6 0.9 copy-start.8
  328.2 0.9 copy-start.9
  329.1 121.3 %all-to-all-start.4 = ((f32[8,8,20000]{2,1,0:T(8,128)}), f32[8,8,20000]{2,1,0:T(8,128)}, u32[]{:S(2)}, u32[]{:S(2)}) async-start(f32[8,8,20000]{2,1,0:T(8,128)} %shard_map.52), calls=%async_computation.4 | async-start | bytes 10289152 | tf_op jit(solution)/shard_map/all_to_all | solution.py:276
  338.7 9.9 %collective-permute-start.6 = (f32[8,14400]{1,0:T(8,128)}, f32[8,14400]{1,0:T(8,128)S(1)}, u32[]{:S(2)}, u32[]{:S(2)}) collective-permute-start(f32[8,14400]{1,0:T(8,128)} %get-tuple-element.72), channel_id=1, source_target_pairs={{0,1},{1,2},{2,3},{3,0},{4,5},{5,6},{6,7},{7,4},{8,9},{9,10},{10,1... | collective-permute-start | bytes 1382408 | tf_op jit(solution)/shard_map/ppermute | solution.py:267
  338.9 19.7 %collective-permute-start.7 = (f32[8,14400]{1,0:T(8,128)}, f32[8,14400]{1,0:T(8,128)S(1)}, u32[]{:S(2)}, u32[]{:S(2)}) collective-permute-start(f32[8,14400]{1,0:T(8,128)} %get-tuple-element.73), channel_id=1, source_target_pairs={{0,2},{1,3},{2,0},{3,1},{4,6},{5,7},{6,4},{7,5},{8,10},{9,11},{10,... | collective-permute-start | bytes 1382408 | tf_op jit(solution)/shard_map/ppermute | solution.py:267
  339.2 21.4 %collective-permute-start.8 = (f32[8,14400]{1,0:T(8,128)}, f32[8,14400]{1,0:T(8,128)S(1)}, u32[]{:S(2)}, u32[]{:S(2)}) collective-permute-start(f32[8,14400]{1,0:T(8,128)} %get-tuple-element.74), channel_id=1, source_target_pairs={{0,3},{1,0},{2,1},{3,2},{4,7},{5,4},{6,5},{7,6},{8,11},{9,8},{10,9... | collective-permute-start | bytes 1382408 | tf_op jit(solution)/shard_map/ppermute | solution.py:267
  348.6 12.0 %copy-start.10 = (f32[8,14400]{1,0:T(8,128)}, f32[8,14400]{1,0:T(8,128)S(1)}, u32[]{:S(2)}) copy-start(f32[8,14400]{1,0:T(8,128)S(1)} %collective-permute-done.6.refs_7_) | copy-start | bytes 1382404
  358.6 2.0 copy-start.11
  360.6 0.8 copy-start.12
  392.7 30.1 %collective-permute-start.10 = (f32[8,40000]{1,0:T(8,128)}, f32[8,40000]{1,0:T(8,128)S(1)}, u32[]{:S(2)}, u32[]{:S(2)}) collective-permute-start(f32[8,40000]{1,0:T(8,128)} %get-tuple-element.77), channel_id=1, source_target_pairs={{0,2},{1,3},{2,0},{3,1},{4,6},{5,7},{6,4},{7,5},{8,10},{9,11},{10,... | collective-permute-start | bytes 3840008 | tf_op jit(solution)/shard_map/ppermute | solution.py:267
  393.9 56.5 %collective-permute-start.11 = (f32[8,40000]{1,0:T(8,128)}, f32[8,40000]{1,0:T(8,128)S(1)}, u32[]{:S(2)}, u32[]{:S(2)}) collective-permute-start(f32[8,40000]{1,0:T(8,128)} %get-tuple-element.78), channel_id=1, source_target_pairs={{0,3},{1,0},{2,1},{3,2},{4,7},{5,4},{6,5},{7,6},{8,11},{9,8},{10,9... | collective-permute-start | bytes 3840008 | tf_op jit(solution)/shard_map/ppermute | solution.py:267
  393.9 56.5 %collective-permute-start.9 = (f32[8,40000]{1,0:T(8,128)}, f32[8,40000]{1,0:T(8,128)}, u32[]{:S(2)}, u32[]{:S(2)}) collective-permute-start(f32[8,40000]{1,0:T(8,128)} %get-tuple-element.76), channel_id=1, source_target_pairs={{0,1},{1,2},{2,3},{3,0},{4,5},{5,6},{6,7},{7,4},{8,9},{9,10},{10,1... | collective-permute-start | bytes 3840008 | tf_op jit(solution)/shard_map/ppermute | solution.py:267
  422.8 27.6 %copy-start.3 = (f32[8,40000]{1,0:T(8,128)}, f32[8,40000]{1,0:T(8,128)S(1)}, u32[]{:S(2)}) copy-start(f32[8,40000]{1,0:T(8,128)S(1)} %collective-permute-done.10.refs_2_) | copy-start | bytes 3840004
  450.3 1.1 copy-start.4
Sparse Core Ops, SparseCore 0:
  9.5 63.1 all-gather.3
  74.3 84.9 all-gather.5

commit v11 on v10

--- a/solution.py
+++ b/solution.py
@@ -309,7 +309,7 @@
     turned = call(turn_body, col_wires(local_cols), [me, crossed], [col_stage], moved=8 * size)
     theirs = shift(turned, "col")
     whole = lax.all_gather(after(whole, theirs[:-1]), "col", axis=0, tiled=False)
-    group = 8 if n % 8 == 0 else n
+    group = 16 if n % 16 == 0 else n
     shape = jax.ShapeDtypeStruct((n * n, naux), bf16)
     high, low = pl.pallas_call(
         functools.partial(split_body, n),

time: 481 us -> 480 us (level)
  no operation moved by 1% of the time
where the time goes in v11:
time: 480 us; the launch traced here: 472 us
  Pallas kernels  197 us (41%)
  waiting for transfers between devices  148 us (31%)
  blocking collectives  76.4 us (16%)
  starting transfers between devices  29.9 us (6%)
  between operations  14 us (3%)
  local copies, waits for them, and re-layouts  5.88 us (1%)
    pallas_call x10, Pallas kernels, call(): pl.pallas_call(body, in_specs=[smem if x.dtype == jnp.int32 else vmem for...  185 us
    ppermute x12, waiting for transfers between devices, shift(): lax.ppermute(parts[s], axis, [(d, (d + s) % n) for d in range(n)])  122 us
    all_to_all x1, blocking collectives, exchange(): return lax.all_to_all(x, axis, split_axis=0, concat_axis=0, tiled=True)  76.4 us
    all_to_all x4, starting transfers between devices, exchange(): return lax.all_to_all(x, axis, split_axis=0, concat_axis=0, tiled=True)  19.6 us
    all_to_all x4, waiting for transfers between devices, exchange(): return lax.all_to_all(x, axis, split_axis=0, concat_axis=0, tiled=True)  18.3 us
    pallas_call x1, Pallas kernels, shards(): pl.pallas_call(functools.partial(split_body, n), grid=(n // group,), in_s...  11.9 us
    ppermute x12, starting transfers between devices, shift(): lax.ppermute(parts[s], axis, [(d, (d + s) % n) for d in range(n)])  10.3 us
  transfers between devices with their start and end apart: 18, of which 12 were waited for; matrix products, arithmetic and copies ran while one was open for 0% of the time, Pallas kernels for 39%

profile of v11, /device:TPU:1, one launch (start us, length us, event | category | flops | bytes accessed | tf_op | source)
XLA Modules:
  0.0 472.1 jit_solution(6946484717440952788)
XLA Ops:
  6.5 1.9 reshape.11
  8.4 0.0 all-gather.6.cloned.1.call-start
  8.5 10.3 %shard_map.46 = (f32[1600,800]{1,0:T(8,128)}, f32[8,32,3200]{2,1,0:T(8,128)}, f32[8,24,2400]{2,1,0:T(8,128)}) custom-call(f32[800,1600]{1,0:T(8,128)} %x_ref.3), custom_call_target="tpu_custom_call" | custom-call | bytes 15360000 | tf_op jit(solution)/shard_map/pallas_call | solution.py:35
  18.8 7.1 %shard_map.47 = (f32[8,40000]{1,0:T(8,128)}, f32[8,40000]{1,0:T(8,128)}, f32[8,40000]{1,0:T(8,128)}, f32[8,40000]{1,0:T(8,128)}) custom-call(s32[1]{0:T(128)} %bitcast.me_ref.refs_0_, f32[1600,800]{1,0:T(8,128)} %get-tuple-element.43.x_ref), custom_call_target="tpu_custom_call" | custom-call | bytes 10240000 | tf_op jit(solution)/shard_map/pallas_call | solution.py:35
  25.9 2.5 collective-permute-start
  28.4 27.7 %collective-permute-done.refs_2_ = f32[8,40000]{1,0:T(8,128)} collective-permute-done((f32[8,40000]{1,0:T(8,128)}, f32[8,40000]{1,0:T(8,128)}, u32[]{:S(2)}, u32[]{:S(2)}) %collective-permute-start) | collective-permute-done | bytes 1280032 | tf_op jit(solution)/shard_map/ppermute | solution.py:267
  56.1 14.6 %collective-permute-done.1.refs_3_ = f32[8,40000]{1,0:T(8,128)} collective-permute-done((f32[8,40000]{1,0:T(8,128)}, f32[8,40000]{1,0:T(8,128)}, u32[]{:S(2)}, u32[]{:S(2)}) %collective-permute-start.1) | collective-permute-done | bytes 1280032 | tf_op jit(solution)/shard_map/ppermute | solution.py:267
  70.7 2.0 all-gather.4.cloned.1.call-done
  72.8 76.4 %all_to_all.25.x_ref = f32[8,32,3200]{2,1,0:T(8,128)} all-to-all(f32[8,32,3200]{2,1,0:T(8,128)S(1)} %copy-done.2), channel_id=1, replica_groups=mesh['row'=8,'col'=4] {'row'}, dimensions={0} | all-to-all | bytes 6553600 | tf_op jit(solution)/shard_map/all_to_all | solution.py:276
  149.2 4.4 all-to-all-start.1
  153.6 0.1 copy.5
  153.7 0.8 pad_maximum_fusion
  154.5 4.8 %all-gather.6.cloned.1.call-done = f32[6400,512]{1,0:T(8,128)} async-done(((f32[1600,512]{1,0:T(8,128)}), f32[6400,512]{1,0:T(8,128)}) %all-gather.6.cloned.1.call-update) | async-done | bytes 13107216 | tf_op jit(solution)/shard_map/all_gather | solution.py:311
  159.3 11.9 %shard_map.48 = (bf16[6400,512]{1,0:T(8,128)(2,1)}, bf16[6400,512]{1,0:T(8,128)(2,1)}) custom-call(f32[4,1600,512]{2,1,0:T(8,128)} %bitcast.7), custom_call_target="tpu_custom_call" | custom-call | flops 6553600 | bytes 26214400 | tf_op jit(solution)/shard_map/pallas_call | solution.py:314
  171.2 26.9 %shard_map.49 = (f32[8,128,800]{2,1,0:T(8,128)}, f32[8,32,3200]{2,1,0:T(8,128)}) custom-call(f32[8,32,3200]{2,1,0:T(8,128)} %all_to_all.25.x_ref, bf16[6400,512]{1,0:T(8,128)(2,1)} %get-tuple-element.48.refs_0_.refs_2_.refs_5_.refs_10_, bf16[6400,512]{1,0:T(8,128)(2,1)} %get-tuple-element.49.refs_1_.refs_3_.refs_6_.refs_11_, f32[1,512]{1,0:T(1,128)} %bitcast.8, ...), custom_call_target="tpu_custom_call" | custom-call | flops 5819596800 | bytes 28467200 | tf_op jit(solution)/shard_map/pallas_call | solution.py:35
  198.1 1.2 copy-done.1
  199.3 5.2 %all-to-all-start.2 = ((f32[8,32,3200]{2,1,0:T(8,128)}), f32[8,32,3200]{2,1,0:T(8,128)S(1)}, u32[]{:S(2)}, u32[]{:S(2)}) async-start(f32[8,32,3200]{2,1,0:T(8,128)} %get-tuple-element.53), calls=%async_computation.2 | async-start | bytes 6553600 | tf_op jit(solution)/shard_map/all_to_all | solution.py:276
  204.6 0.7 collective-permute-start.2
  205.3 0.6 neg.13
  205.8 25.1 %shard_map.50 = (f32[8,72,800]{2,1,0:T(8,128)}, f32[8,24,2400]{2,1,0:T(8,128)}) custom-call(f32[8,24,2400]{2,1,0:T(8,128)} %copy-done.1, bf16[6400,512]{1,0:T(8,128)(2,1)} %get-tuple-element.48.refs_0_.refs_2_.refs_5_.refs_10_, bf16[6400,512]{1,0:T(8,128)(2,1)} %get-tuple-element.49.refs_1_.refs_3_.refs_6_.refs_11_, f32[1,512]{1,0:T(1,128)} %bitcast.9, ...), custom_call_target="tpu_custom_call" | custom-call | flops 3273523200 | bytes 28467200 | tf_op jit(solution)/shard_map/pallas_call | solution.py:35
  231.0 28.4 %shard_map.53.refs_1_ = f32[4,200,1600]{2,1,0:T(8,128)} custom-call(s32[1]{0:T(128)} %bitcast.me_ref.refs_0_, f32[8,40000]{1,0:T(8,128)} %get-tuple-element.64.refs_1_, f32[8,40000]{1,0:T(8,128)} %collective-permute-done.refs_2_, f32[8,40000]{1,0:T(8,128)} %collective-permute-done.1.refs_3_, f32[8,40000]{1,0:T(8,128)} %collective-permute-done.2.refs_4_, ...), custom_call_target="tpu_custom_call" | custom-call | flops 9093120000 | bytes 28467200 | tf_op jit(solution)/shard_map/pallas_call | solution.py:35
  259.4 18.3 %all-to-all-done.2.x_ref = f32[8,32,3200]{2,1,0:T(8,128)S(1)} async-done(((f32[8,32,3200]{2,1,0:T(8,128)}), f32[8,32,3200]{2,1,0:T(8,128)S(1)}, u32[]{:S(2)}, u32[]{:S(2)}) %all-to-all-start.2) | async-done | bytes 3276832 | tf_op jit(solution)/shard_map/all_to_all | solution.py:276
  277.7 4.3 all-to-all-start.3
  282.0 6.0 %shard_map.51 = (f32[200,1024]{1,0:T(8,128)}, f32[200,1024]{1,0:T(8,128)}, f32[200,1024]{1,0:T(8,128)}, f32[200,1024]{1,0:T(8,128)}) custom-call(s32[1]{0:T(128)} %bitcast.me_ref.refs_0_, f32[8,32,3200]{2,1,0:T(8,128)} %copy-done), custom_call_target="tpu_custom_call" | custom-call | bytes 5120000 | tf_op jit(solution)/shard_map/pallas_call | solution.py:35
  288.0 1.5 collective-permute-start.3
  289.5 1.2 collective-permute-start.4
  290.7 0.2 collective-permute-start.5
  290.9 31.3 %shard_map.52 = f32[8,8,20000]{2,1,0:T(8,128)} custom-call(f32[8,128,800]{2,1,0:T(8,128)} %get-tuple-element.60.refs_0_, f32[8,72,800]{2,1,0:T(8,128)} %get-tuple-element.61.refs_1_, bf16[6400,512]{1,0:T(8,128)(2,1)} %get-tuple-element.48.refs_0_.refs_2_.refs_5_.refs_10_, bf16[6400,512]{1,0:T(8,128)(2,1)} %get-tuple-element.49.refs_1_.refs_3_.refs_6_.refs_11_, ...), custom_call_target="tpu_custom_call" | custom-call | flops 9093120000 | bytes 28467200 | tf_op jit(solution)/shard_map/pallas_call | solution.py:35
  322.2 4.2 collective-permute-done.4.refs_4_
  326.4 0.6 collective-permute-done.5.refs_5_
  327.0 0.3 copy-done.8
  327.3 0.5 copy-done.9
  327.9 5.6 %all-to-all-start.4 = ((f32[8,8,20000]{2,1,0:T(8,128)}), f32[8,8,20000]{2,1,0:T(8,128)}, u32[]{:S(2)}, u32[]{:S(2)}) async-start(f32[8,8,20000]{2,1,0:T(8,128)} %shard_map.52), calls=%async_computation.4 | async-start | bytes 10289152 | tf_op jit(solution)/shard_map/all_to_all | solution.py:276
  333.5 4.0 shard_map.54
  337.5 0.2 collective-permute-start.6
  337.8 0.3 collective-permute-start.7
  338.0 0.6 collective-permute-start.8
  338.6 8.9 %collective-permute-done.6.refs_7_ = f32[8,14400]{1,0:T(8,128)S(1)} collective-permute-done((f32[8,14400]{1,0:T(8,128)}, f32[8,14400]{1,0:T(8,128)S(1)}, u32[]{:S(2)}, u32[]{:S(2)}) %collective-permute-start.6) | collective-permute-done | bytes 460832 | tf_op jit(solution)/shard_map/ppermute | solution.py:267
  347.5 9.9 %collective-permute-done.7.refs_8_ = f32[8,14400]{1,0:T(8,128)S(1)} collective-permute-done((f32[8,14400]{1,0:T(8,128)}, f32[8,14400]{1,0:T(8,128)S(1)}, u32[]{:S(2)}, u32[]{:S(2)}) %collective-permute-start.7) | collective-permute-done | bytes 460832 | tf_op jit(solution)/shard_map/ppermute | solution.py:267
  357.4 2.0 collective-permute-done.8.refs_9_
  359.4 0.8 copy-done.12
  360.2 31.3 %shard_map.55 = (f32[8,40000]{1,0:T(8,128)}, f32[8,40000]{1,0:T(8,128)}, f32[8,40000]{1,0:T(8,128)}, f32[8,40000]{1,0:T(8,128)}) custom-call(s32[1]{0:T(128)} %bitcast.me_ref.refs_0_, f32[4,200,1600]{2,1,0:T(8,128)} %shard_map.53.refs_1_, f32[200,1024]{1,0:T(8,128)} %get-tuple-element.56.refs_2_, f32[200,1024]{1,0:T(8,128)} %copy-done.7, ...), custom_call_target="tpu_custom_call" | custom-call | flops 9093120000 | bytes 28467200 | tf_op jit(solution)/shard_map/pallas_call | solution.py:35
  391.5 1.2 collective-permute-start.10
  392.7 2.0 collective-permute-start.9
  394.7 26.9 %collective-permute-done.10.refs_2_ = f32[8,40000]{1,0:T(8,128)S(1)} collective-permute-done((f32[8,40000]{1,0:T(8,128)}, f32[8,40000]{1,0:T(8,128)S(1)}, u32[]{:S(2)}, u32[]{:S(2)}) %collective-permute-start.10) | collective-permute-done | bytes 1280032 | tf_op jit(solution)/shard_map/ppermute | solution.py:267
  421.6 27.6 %collective-permute-done.11.refs_3_ = f32[8,40000]{1,0:T(8,128)S(1)} collective-permute-done((f32[8,40000]{1,0:T(8,128)}, f32[8,40000]{1,0:T(8,128)S(1)}, u32[]{:S(2)}, u32[]{:S(2)}) %collective-permute-start.11) | collective-permute-done | bytes 1280032 | tf_op jit(solution)/shard_map/ppermute | solution.py:267
  449.2 1.0 copy-done.4
  450.2 14.6 %shard_map.56 = f32[800,1600]{1,0:T(8,128)} custom-call(s32[1]{0:T(128)} %bitcast.me_ref.refs_0_, f32[800,1600]{1,0:T(8,128)} %x_ref.3, f32[8,8,20000]{2,1,0:T(8,128)} %all-to-all-done.4.crossed_ref, f32[8,40000]{1,0:T(8,128)} %get-tuple-element.75.refs_0_, f32[8,40000]{1,0:T(8,128)} %collective-permute-done.9.refs_1_, f32[8,40000]{1,0:T(8,128)} %copy-done.3, ...), custom_call_target="tpu_custom_call" | custom-call | bytes 20480000 | tf_op jit(solution)/shard_map/pallas_call | solution.py:35
  (34 shorter events, 0.1 us)
Async XLA Ops:
  6.5 66.2 %all-gather.4.cloned.1.call-start = ((), (), s32[]{:S(2)}) async-start(), calls=%async_computation.5 | async-start | bytes 3686400 | tf_op jit(solution)/shard_map/all_gather | solution.py:305
  8.4 150.9 %all-gather.6.cloned.1.call-start = ((), (), s32[]{:S(2)}) async-start(), calls=%async_computation.6 | async-start | bytes 16384000 | tf_op jit(solution)/shard_map/all_gather | solution.py:311
  25.9 46.9 %copy-start.2 = (f32[8,32,3200]{2,1,0:T(8,128)S(1)}, f32[8,32,3200]{2,1,0:T(8,128)}, u32[]{:S(2)}) copy-start(f32[8,32,3200]{2,1,0:T(8,128)} %get-tuple-element.42) | copy-start | bytes 9830404
  25.9 30.2 %collective-permute-start = (f32[8,40000]{1,0:T(8,128)}, f32[8,40000]{1,0:T(8,128)}, u32[]{:S(2)}, u32[]{:S(2)}) collective-permute-start(f32[8,40000]{1,0:T(8,128)} %get-tuple-element.45), channel_id=1, source_target_pairs={{0,1},{1,2},{2,3},{3,0},{4,5},{5,6},{6,7},{7,4},{8,9},{9,10},{10,1... | collective-permute-start | bytes 3840008 | tf_op jit(solution)/shard_map/ppermute | solution.py:267
  28.4 42.3 %collective-permute-start.1 = (f32[8,40000]{1,0:T(8,128)}, f32[8,40000]{1,0:T(8,128)}, u32[]{:S(2)}, u32[]{:S(2)}) collective-permute-start(f32[8,40000]{1,0:T(8,128)} %get-tuple-element.46), channel_id=1, source_target_pairs={{0,2},{1,3},{2,0},{3,1},{4,6},{5,7},{6,4},{7,5},{8,10},{9,11},{10,... | collective-permute-start | bytes 3840008 | tf_op jit(solution)/shard_map/ppermute | solution.py:267
  149.2 4.4 copy-start.5
  149.2 48.9 %all-to-all-start.1 = ((f32[8,24,2400]{2,1,0:T(8,128)}), f32[8,24,2400]{2,1,0:T(8,128)S(1)}, u32[]{:S(2)}, u32[]{:S(2)}) async-start(f32[8,24,2400]{2,1,0:T(8,128)} %get-tuple-element.52), calls=%async_computation.1 | async-start | bytes 3735552 | tf_op jit(solution)/shard_map/all_to_all | solution.py:276
  198.1 1.2 copy-start.1
  198.1 7.2 %copy-start.6 = (f32[512]{0:T(512)S(1)}, f32[512]{0:T(512)}, u32[]{:S(2)}) copy-start(f32[512]{0:T(512)} %param.7) | copy-start | bytes 6148
  199.3 78.4 %all-to-all-start.2 = ((f32[8,32,3200]{2,1,0:T(8,128)}), f32[8,32,3200]{2,1,0:T(8,128)S(1)}, u32[]{:S(2)}, u32[]{:S(2)}) async-start(f32[8,32,3200]{2,1,0:T(8,128)} %get-tuple-element.53), calls=%async_computation.2 | async-start | bytes 6553600 | tf_op jit(solution)/shard_map/all_to_all | solution.py:276
  204.6 26.4 %collective-permute-start.2 = (f32[8,40000]{1,0:T(8,128)}, f32[8,40000]{1,0:T(8,128)}, u32[]{:S(2)}, u32[]{:S(2)}) collective-permute-start(f32[8,40000]{1,0:T(8,128)} %get-tuple-element.63), channel_id=1, source_target_pairs={{0,3},{1,0},{2,1},{3,2},{4,7},{5,4},{6,5},{7,6},{8,11},{9,8},{10,9... | collective-permute-start | bytes 3840008 | tf_op jit(solution)/shard_map/ppermute | solution.py:267
  277.7 4.3 copy-start
  277.7 49.3 %all-to-all-start.3 = ((f32[8,24,2400]{2,1,0:T(8,128)}), f32[8,24,2400]{2,1,0:T(8,128)}, u32[]{:S(2)}, u32[]{:S(2)}) async-start(f32[8,24,2400]{2,1,0:T(8,128)} %get-tuple-element.68), calls=%async_computation.3 | async-start | bytes 3735552 | tf_op jit(solution)/shard_map/all_to_all | solution.py:276
  288.0 34.2 %collective-permute-start.3 = (f32[200,1024]{1,0:T(8,128)}, f32[200,1024]{1,0:T(8,128)S(1)}, u32[]{:S(2)}, u32[]{:S(2)}) collective-permute-start(f32[200,1024]{1,0:T(8,128)} %get-tuple-element.57), channel_id=1, source_target_pairs={{0,1},{1,2},{2,3},{3,0},{4,5},{5,6},{6,7},{7,4},{8,9},{9,10},{10,1... | collective-permute-start | bytes 2457608 | tf_op jit(solution)/shard_map/ppermute | solution.py:267
  289.5 36.9 %collective-permute-start.4 = (f32[200,1024]{1,0:T(8,128)}, f32[200,1024]{1,0:T(8,128)S(1)}, u32[]{:S(2)}, u32[]{:S(2)}) collective-permute-start(f32[200,1024]{1,0:T(8,128)} %get-tuple-element.58), channel_id=1, source_target_pairs={{0,2},{1,3},{2,0},{3,1},{4,6},{5,7},{6,4},{7,5},{8,10},{9,11},{10,... | collective-permute-start | bytes 2457608 | tf_op jit(solution)/shard_map/ppermute | solution.py:267
  290.7 36.3 %collective-permute-start.5 = (f32[200,1024]{1,0:T(8,128)}, f32[200,1024]{1,0:T(8,128)S(1)}, u32[]{:S(2)}, u32[]{:S(2)}) collective-permute-start(f32[200,1024]{1,0:T(8,128)} %get-tuple-element.59), channel_id=1, source_target_pairs={{0,3},{1,0},{2,1},{3,2},{4,7},{5,4},{6,5},{7,6},{8,11},{9,8},{10,9... | collective-permute-start | bytes 2457608 | tf_op jit(solution)/shard_map/ppermute | solution.py:267
  322.2 4.8 %copy-start.7 = (f32[200,1024]{1,0:T(8,128)}, f32[200,1024]{1,0:T(8,128)S(1)}, u32[]{:S(2)}) copy-start(f32[200,1024]{1,0:T(8,128)S(1)} %collective-permute-done.3.refs_3_) | copy-start | bytes 2457604
  326.4 0.9 copy-start.8
  327.0 0.9 copy-start.9
  327.9 121.3 %all-to-all-start.4 = ((f32[8,8,20000]{2,1,0:T(8,128)}), f32[8,8,20000]{2,1,0:T(8,128)}, u32[]{:S(2)}, u32[]{:S(2)}) async-start(f32[8,8,20000]{2,1,0:T(8,128)} %shard_map.52), calls=%async_computation.4 | async-start | bytes 10289152 | tf_op jit(solution)/shard_map/all_to_all | solution.py:276
  337.5 9.9 %collective-permute-start.6 = (f32[8,14400]{1,0:T(8,128)}, f32[8,14400]{1,0:T(8,128)S(1)}, u32[]{:S(2)}, u32[]{:S(2)}) collective-permute-start(f32[8,14400]{1,0:T(8,128)} %get-tuple-element.72), channel_id=1, source_target_pairs={{0,1},{1,2},{2,3},{3,0},{4,5},{5,6},{6,7},{7,4},{8,9},{9,10},{10,1... | collective-permute-start | bytes 1382408 | tf_op jit(solution)/shard_map/ppermute | solution.py:267
  337.8 19.7 %collective-permute-start.7 = (f32[8,14400]{1,0:T(8,128)}, f32[8,14400]{1,0:T(8,128)S(1)}, u32[]{:S(2)}, u32[]{:S(2)}) collective-permute-start(f32[8,14400]{1,0:T(8,128)} %get-tuple-element.73), channel_id=1, source_target_pairs={{0,2},{1,3},{2,0},{3,1},{4,6},{5,7},{6,4},{7,5},{8,10},{9,11},{10,... | collective-permute-start | bytes 1382408 | tf_op jit(solution)/shard_map/ppermute | solution.py:267
  338.0 21.4 %collective-permute-start.8 = (f32[8,14400]{1,0:T(8,128)}, f32[8,14400]{1,0:T(8,128)S(1)}, u32[]{:S(2)}, u32[]{:S(2)}) collective-permute-start(f32[8,14400]{1,0:T(8,128)} %get-tuple-element.74), channel_id=1, source_target_pairs={{0,3},{1,0},{2,1},{3,2},{4,7},{5,4},{6,5},{7,6},{8,11},{9,8},{10,9... | collective-permute-start | bytes 1382408 | tf_op jit(solution)/shard_map/ppermute | solution.py:267
  347.5 12.0 %copy-start.10 = (f32[8,14400]{1,0:T(8,128)}, f32[8,14400]{1,0:T(8,128)S(1)}, u32[]{:S(2)}) copy-start(f32[8,14400]{1,0:T(8,128)S(1)} %collective-permute-done.6.refs_7_) | copy-start | bytes 1382404
  357.4 2.0 copy-start.11
  359.4 0.8 copy-start.12
  391.5 30.1 %collective-permute-start.10 = (f32[8,40000]{1,0:T(8,128)}, f32[8,40000]{1,0:T(8,128)S(1)}, u32[]{:S(2)}, u32[]{:S(2)}) collective-permute-start(f32[8,40000]{1,0:T(8,128)} %get-tuple-element.77), channel_id=1, source_target_pairs={{0,2},{1,3},{2,0},{3,1},{4,6},{5,7},{6,4},{7,5},{8,10},{9,11},{10,... | collective-permute-start | bytes 3840008 | tf_op jit(solution)/shard_map/ppermute | solution.py:267
  392.7 56.5 %collective-permute-start.11 = (f32[8,40000]{1,0:T(8,128)}, f32[8,40000]{1,0:T(8,128)S(1)}, u32[]{:S(2)}, u32[]{:S(2)}) collective-permute-start(f32[8,40000]{1,0:T(8,128)} %get-tuple-element.78), channel_id=1, source_target_pairs={{0,3},{1,0},{2,1},{3,2},{4,7},{5,4},{6,5},{7,6},{8,11},{9,8},{10,9... | collective-permute-start | bytes 3840008 | tf_op jit(solution)/shard_map/ppermute | solution.py:267
  392.7 56.5 %collective-permute-start.9 = (f32[8,40000]{1,0:T(8,128)}, f32[8,40000]{1,0:T(8,128)}, u32[]{:S(2)}, u32[]{:S(2)}) collective-permute-start(f32[8,40000]{1,0:T(8,128)} %get-tuple-element.76), channel_id=1, source_target_pairs={{0,1},{1,2},{2,3},{3,0},{4,5},{5,6},{6,7},{7,4},{8,9},{9,10},{10,1... | collective-permute-start | bytes 3840008 | tf_op jit(solution)/shard_map/ppermute | solution.py:267
  421.6 27.6 %copy-start.3 = (f32[8,40000]{1,0:T(8,128)}, f32[8,40000]{1,0:T(8,128)S(1)}, u32[]{:S(2)}) copy-start(f32[8,40000]{1,0:T(8,128)S(1)} %collective-permute-done.10.refs_2_) | copy-start | bytes 3840004
  449.2 1.1 copy-start.4
Sparse Core Ops, SparseCore 0:
  9.5 63.1 all-gather.3
  74.3 84.9 all-gather.5
